TPU v7x, 128 devices: a whole 4x4x4 slice. The times are simulated.
128 devices in a mesh: gx: 32 (over z, y, core), gy: 4 (over x).
Axes of the slice: x: 4, y: 4, z: 4, core: 2. Of those that a mesh axis runs over, the one named last changes fastest.
Arguments:
- snapshot: float32 [512, 256, 512], P('gx', 'gy'), may hold values from -6 to 6
- keep_mask: int32 [512, 256, 4], P('gx', 'gy'), may hold values from 0 to 1, as said below
- exponents: int32 [4], replicated, may hold values from -1 to 2
Outputs:
- coefficients: float32 [512, 256, 512], P('gx', 'gy')
- stream: float32 [524288, 128], P(('gx', 'gy'))
Inputs may be any that keep to these rules, and one draw needn't show every extreme that they name: `keep_mask`: each device block has its own keep rate.
All inputs are finite; a program needn't handle non-finite values.
Results may differ from a plain program's by a relative error of at most 0.0003.
Values sent between devices are 32-bit elements; how exact they have to be, the bound alone decides.
No kernel may reach another device: no remote copies, remote signals or barrier semaphores. Data moves between devices by JAX's collectives and lax.ppermute only.
A program may use at most 64 MiB of HBM per device.

v0:
```python
import math

import jax
import jax.numpy as jnp
from jax import lax
from jax.sharding import PartitionSpec as P

LEVELS = 3


def shifted(value, axis, steps):
    count = lax.axis_size(axis)
    leading, last = (max(0, -steps), min(count, count - steps))
    return lax.ppermute(value, axis, [(source, source + steps) for source in range(leading, last)])


def entering(part, axis, combine, identity):
    place = lax.axis_index(axis)
    gathered = lax.all_gather(part, axis)
    state = jnp.zeros_like(part) + jnp.asarray(identity, part.dtype)

    def one(hop, state):
        return combine(state, lax.dynamic_index_in_dim(gathered, hop, 0, False))

    return lax.fori_loop(0, place, one, state)


def split_pair(values, dim):
    dims_now = values.shape
    paired = values.reshape(dims_now[:dim] + (dims_now[dim] // 2, 2) + dims_now[dim + 1 :])
    return (
        lax.index_in_dim(paired, 0, dim + 1, keepdims=False),
        lax.index_in_dim(paired, 1, dim + 1, keepdims=False),
    )


def alternate(first, second, dim):
    stacked = jnp.stack([first, second], axis=dim + 1)
    dims_now = first.shape
    return stacked.reshape(dims_now[:dim] + (dims_now[dim] * 2,) + dims_now[dim + 1 :])


def first_row(values, dim):
    return lax.slice_in_dim(values, 0, 1, axis=dim)


def last_row(values, dim):
    return lax.slice_in_dim(values, values.shape[dim] - 1, values.shape[dim], axis=dim)


def predict(even_part, odd_part, next_head, dim):
    length = even_part.shape[dim]
    ahead = jnp.concatenate([lax.slice_in_dim(even_part, 1, length, axis=dim), next_head], axis=dim)
    return odd_part - 0.5 * (even_part + ahead)


def update(even_part, detail, prev_tail, dim):
    length = detail.shape[dim]
    behind = jnp.concatenate(
        [prev_tail, lax.slice_in_dim(detail, 0, length - 1, axis=dim)], axis=dim
    )
    return even_part + 0.25 * (behind + detail)


def lift_x(values):
    even_part, odd_part = split_pair(values, 0)
    next_head = shifted(first_row(even_part, 0), "gx", -1)
    detail = predict(even_part, odd_part, next_head, 0)
    prev_tail = shifted(last_row(detail, 0), "gx", 1)
    return (update(even_part, detail, prev_tail, 0), detail)


def lift_y(values):
    even_part, odd_part = split_pair(values, 1)
    next_head = shifted(first_row(even_part, 1), "gy", -1)
    detail = predict(even_part, odd_part, next_head, 1)
    prev_tail = shifted(last_row(detail, 1), "gy", 1)
    return (update(even_part, detail, prev_tail, 1), detail)


def decompose(values, depth):
    smooth_x, detail_x = lift_x(values)
    smooth_xy, detail_y = lift_y(smooth_x)
    coarse = decompose(smooth_xy, depth + 1) if depth + 1 < LEVELS else smooth_xy
    merged = alternate(coarse, detail_y, 1)
    return alternate(merged, detail_x, 0)


def add_counts(earlier, later):
    return earlier + later


def on_device(snapshot, keep_mask, exponents):
    rows_x, rows_y, depth_z = snapshot.shape
    layout = decompose(snapshot, 0)
    x_index = lax.axis_index("gx") * rows_x + jnp.arange(rows_x, dtype=jnp.int32)
    y_index = lax.axis_index("gy") * rows_y + jnp.arange(rows_y, dtype=jnp.int32)
    joined = jnp.bitwise_or(x_index[:, None], y_index[None, :])
    level_code = (
        (joined % 2 == 0).astype(jnp.int32)
        + (joined % 4 == 0).astype(jnp.int32)
        + (joined % 8 == 0).astype(jnp.int32)
    )
    factor = jnp.zeros((rows_x, rows_y), jnp.float32)
    for level_no in range(LEVELS + 1):
        factor = factor + jnp.where(
            level_code == level_no,
            jnp.exp2(exponents[level_no].astype(jnp.float32)),
            jnp.float32(0.0),
        )
    coefficients = layout * factor[:, :, None]
    width = keep_mask.shape[2]
    slots = rows_x * rows_y * width
    tile_rows = coefficients.reshape(slots, depth_z // width)
    keep_flags = keep_mask.reshape(slots)
    kept_total = jnp.sum(keep_flags)
    device = lax.axis_index(("gx", "gy"))
    offset = entering(kept_total, ("gx", "gy"), add_counts, jnp.int32(0))
    lag = (slots - offset % slots) % slots
    ranks = jnp.cumsum(keep_flags) - keep_flags
    target = ranks + slots - lag
    block = math.gcd(512, slots)
    window = jnp.zeros((2 * slots + block, tile_rows.shape[1]), jnp.float32)
    block_ids = jnp.arange(block, dtype=jnp.int32)

    def place(block_no, window_now):
        start = block_no * block
        source = lax.dynamic_slice_in_dim(tile_rows, start, block, 0)
        targets = lax.dynamic_slice_in_dim(target, start, block, 0)
        flags = lax.dynamic_slice_in_dim(keep_flags, start, block, 0)
        base = targets[0]
        onehot = ((targets[None, :] - base == block_ids[:, None]) & (flags[None, :] > 0)).astype(
            jnp.float32
        )
        product_rows = jnp.dot(
            onehot, source, precision=lax.Precision.HIGHEST, preferred_element_type=jnp.float32
        )
        current = lax.dynamic_slice_in_dim(window_now, base, block, 0)
        return lax.dynamic_update_slice_in_dim(window_now, current + product_rows, base, 0)

    window = lax.fori_loop(0, slots // block, place, window)
    positions = jnp.arange(2 * slots, dtype=jnp.int32)
    filled = (positions >= slots - lag) & (positions < slots - lag + kept_total)
    labels_all = jnp.where(filled, offset + positions - (slots - lag) + 1, 0).astype(jnp.float32)
    front_half = (window[:slots], labels_all[:slots])
    arrived = shifted((front_half[0], front_half[1]), ("gx", "gy"), -1)
    packed = window[slots : 2 * slots] + arrived[0]
    labels = labels_all[slots:] + arrived[1]
    devices = lax.axis_size(("gx", "gy"))
    sections = []
    stride = 1
    while stride < devices:
        radix = 2
        sections.append((stride, radix))
        stride = stride * radix
    for stride, radix in sections:
        label_ids = labels.astype(jnp.int32)
        remaining = device - (label_ids - 1) // slots
        digits = jnp.where(label_ids > 0, remaining // stride % radix, 0)
        staying = digits == 0
        packed_next = jnp.where(staying[:, None], packed, 0.0)
        labels_next = jnp.where(staying, labels, 0.0)
        chosen = digits == 1
        moving = (jnp.where(chosen[:, None], packed, 0.0), jnp.where(chosen, labels, 0.0))
        landed = shifted((moving[0], moving[1]), ("gx", "gy"), -(1 * stride))
        packed_next = packed_next + landed[0]
        labels_next = labels_next + landed[1]
        packed = packed_next
        labels = labels_next
    return (coefficients, packed)


def solution(mesh):
    in_specs = (P("gx", "gy", None), P("gx", "gy", None), P())
    out_specs = (P("gx", "gy", None), P(("gx", "gy"), None))
    return jax.shard_map(
        on_device, mesh=mesh, in_specs=in_specs, out_specs=out_specs, check_vma=False
    )
```

profile of v0, /device:TPU:1, one launch (start us, length us, event | category | flops | bytes accessed | tf_op | source)
XLA Modules:
  0.0 783.0 jit_solution(6049301430443813376)
XLA Ops:
  1.5 3.3 collective-permute-start
  7.1 68.0 %all-reduce = s32[128]{0:T(128)S(1)} all-reduce(s32[128]{0:T(128)S(1)} %dynamic-update-slice), channel_id=1, replica_groups=mesh['gx'=32,'gy'=4] {'gx','gy'}, use_global_device_ids=true, to_apply=%add | all-reduce | flops 128 | bytes 1024
  75.1 5.0 while.24
  81.8 2.5 slice_bitcast_fusion.17
  92.7 7.6 collective-permute-start.1
  104.8 2.1 fusion.11
  110.5 2.2 collective-permute-done.2
  113.7 4.1 collective-permute-start.3
  123.3 1.9 collective-permute-start.4
  125.4 7.6 collective-permute-done.4
  133.0 6.2 collective-permute-start.5
  142.3 3.4 collective-permute-done.6
  145.8 3.4 collective-permute-start.7
  150.1 2.1 collective-permute-start.8
  152.3 10.0 %collective-permute-done.8 = f32[1,16,512]{2,1,0:T(8,128)S(1)} collective-permute-done((f32[1,16,512]{2,1,0:T(8,128)S(1)}, f32[1,16,512]{2,1,0:T(8,128)S(1)}, u32[]{:S(2)}, u32[]{:S(2)}) %collective-permute-start.8) | collective-permute-done | bytes 32800 | tf_op jit(solution)/shard_map/ppermute | solution.py:14
  162.3 3.9 collective-permute-start.9
  168.7 3.3 collective-permute-done.10
  172.0 3.4 collective-permute-start.11
  179.8 3.8 mul.216
  183.5 2.2 broadcast_in_dim.180
  185.7 65.8 %while.25 = (s32[]{:T(128)}, f32[8704,128]{1,0:T(8,128)}, s32[4096]{0:T(1024)}, s32[4096]{0:T(1024)S(1)}, f32[4096,128]{1,0:T(8,128)}, /*index=5*/s32[]{:T(128)}, s32[]{:T(128)}, s32[]{:T(128)}, s32[]{:T(128)}, s32[]{:T(128)}) while((s32[]{:T(128)}, f32[8704,128]{1,0:T(8,128)}, s32[4096]{0:T(1024)}, s32[4096]{0:T(1024)S(1)}, ...), condition=%wide.region_6.7_spmd.clone, body=%wide.region_5.6_spmd.clone.sunk | while | flops 403244032 | bytes 1324249 | solution.py:141
  192.1 1.9 dynamic_update_slice.9
  200.4 1.9 dynamic_update_slice.9
  208.6 1.9 dynamic_update_slice.9
  233.3 1.9 dynamic_update_slice.9
  249.7 1.9 dynamic_update_slice.9
  251.6 3.0 slice.221
  254.6 3.0 collective-permute-start.19
  258.3 3.9 collective-permute-start.12
  262.2 41.6 %collective-permute-done.12 = f32[4096]{0:T(1024)S(1)} collective-permute-done((f32[4096]{0:T(1024)S(1)}, f32[4096]{0:T(1024)S(1)}, u32[]{:S(2)}, u32[]{:S(2)}) %collective-permute-start.12) | collective-permute-done | bytes 16416 | tf_op jit(solution)/shard_map/ppermute | solution.py:14
  303.8 4.0 broadcast_select_fusion.6
  307.9 3.8 collective-permute-start.20
  311.7 4.4 collective-permute-start.13
  316.1 39.6 %collective-permute-done.13 = f32[4096]{0:T(1024)S(1)} collective-permute-done((f32[4096]{0:T(1024)S(1)}, f32[4096]{0:T(1024)S(1)}, u32[]{:S(2)}, u32[]{:S(2)}) %collective-permute-start.13) | collective-permute-done | bytes 16416 | tf_op jit(solution)/shard_map/ppermute | solution.py:14
  355.8 5.3 broadcast_select_fusion.5
  361.2 5.3 collective-permute-start.21
  366.5 4.1 collective-permute-start.14
  370.5 44.6 %collective-permute-done.14 = f32[4096]{0:T(1024)S(1)} collective-permute-done((f32[4096]{0:T(1024)S(1)}, f32[4096]{0:T(1024)S(1)}, u32[]{:S(2)}, u32[]{:S(2)}) %collective-permute-start.14) | collective-permute-done | bytes 16416 | tf_op jit(solution)/shard_map/ppermute | solution.py:14
  416.6 2.3 collective-permute-start.22
  418.9 1.9 collective-permute-start.15
  420.8 33.9 %collective-permute-done.15 = f32[4096]{0:T(1024)S(1)} collective-permute-done((f32[4096]{0:T(1024)S(1)}, f32[4096]{0:T(1024)S(1)}, u32[]{:S(2)}, u32[]{:S(2)}) %collective-permute-start.15) | collective-permute-done | bytes 16416 | tf_op jit(solution)/shard_map/ppermute | solution.py:14
  454.8 3.5 broadcast_select_fusion.3
  460.9 45.7 %collective-permute-done.16 = f32[4096]{0:T(1024)S(1)} collective-permute-done((f32[4096]{0:T(1024)S(1)}, f32[4096]{0:T(1024)S(1)}, u32[]{:S(2)}, u32[]{:S(2)}) %collective-permute-start.16) | collective-permute-done | bytes 16416 | tf_op jit(solution)/shard_map/ppermute | solution.py:14
  510.6 57.0 %collective-permute-done.17 = f32[4096]{0:T(1024)S(1)} collective-permute-done((f32[4096]{0:T(1024)S(1)}, f32[4096]{0:T(1024)S(1)}, u32[]{:S(2)}, u32[]{:S(2)}) %collective-permute-start.17) | collective-permute-done | bytes 16416 | tf_op jit(solution)/shard_map/ppermute | solution.py:14
  567.7 3.5 broadcast_select_fusion.1
  573.7 77.5 %collective-permute-done.18 = f32[4096]{0:T(1024)S(1)} collective-permute-done((f32[4096]{0:T(1024)S(1)}, f32[4096]{0:T(1024)S(1)}, u32[]{:S(2)}, u32[]{:S(2)}) %collective-permute-start.18) | collective-permute-done | bytes 16416 | tf_op jit(solution)/shard_map/ppermute | solution.py:14
  655.6 124.8 %collective-permute-done.26 = f32[4096,128]{1,0:T(8,128)S(1)} collective-permute-done((f32[4096,128]{1,0:T(8,128)S(1)}, f32[4096,128]{1,0:T(8,128)S(1)}, u32[]{:S(2)}, u32[]{:S(2)}) %collective-permute-start.26) | collective-permute-done | bytes 2097184 | tf_op jit(solution)/shard_map/ppermute | solution.py:14
  780.4 2.6 select_add_fusion
  (210 shorter events, 94.0 us)
Async XLA Ops:
  1.5 90.1 %collective-permute-start = (f32[1,64,512]{2,1,0:T(8,128)S(1)}, f32[1,64,512]{2,1,0:T(8,128)S(1)}, u32[]{:S(2)}, u32[]{:S(2)}) collective-permute-start(f32[1,64,512]{2,1,0:T(8,128)S(1)} %slice_bitcast_fusion.4), channel_id=1, source_target_pairs={{4,0},{8,4},{12,8},{16,12},{20,16},{24,20},{28,24},{32,28},{36,32}... | collective-permute-start | bytes 393224 | tf_op jit(solution)/shard_map/ppermute | solution.py:14
  80.2 4.1 copy-start.7
  81.7 9.9 %copy-start = (f32[16,64,512]{2,1,0:T(8,128)S(1)}, f32[16,64,512]{2,1,0:T(8,128)}, u32[]{:S(2)}) copy-start(f32[16,64,512]{2,1,0:T(8,128)} %param.7) | copy-start | bytes 6291460
  86.7 4.9 copy-start.3
  92.7 11.9 %collective-permute-start.1 = (f32[1,64,512]{2,1,0:T(8,128)}, f32[1,64,512]{2,1,0:T(8,128)S(1)}, u32[]{:S(2)}, u32[]{:S(2)}) collective-permute-start(f32[1,64,512]{2,1,0:T(8,128)} %slice.227), channel_id=1, source_target_pairs={{0,4},{4,8},{8,12},{12,16},{16,20},{20,24},{24,28},{28,32},{32,36}... | collective-permute-start | bytes 393224 | tf_op jit(solution)/shard_map/ppermute | solution.py:14
  108.1 9.7 %copy-start.8 = (s32[16]{0:T(128)S(1)}, s32[16]{0:T(128)}, u32[]{:S(2)}) copy-start(s32[16]{0:T(128)} %iota_add_fusion.1) | copy-start | bytes 196
  108.1 9.7 %copy-start.9 = (s32[64]{0:T(128)S(1)}, s32[64]{0:T(128)}, u32[]{:S(2)}) copy-start(s32[64]{0:T(128)} %iota_add_fusion) | copy-start | bytes 772
  108.1 4.6 collective-permute-start.2
  110.5 2.2 copy-start.1
  112.9 0.8 copy-start.5
  113.7 9.3 %collective-permute-start.3 = (f32[8,1,512]{2,0,1:T(8,128)S(1)}, f32[8,1,512]{2,0,1:T(8,128)S(1)}, u32[]{:S(2)}, u32[]{:S(2)}) collective-permute-start(f32[8,1,512]{2,0,1:T(8,128)S(1)} %slice.233), channel_id=1, source_target_pairs={{0,1},{1,2},{2,3},{4,5},{5,6},{6,7},{8,9},{9,10},{10,11},{12,13},{... | collective-permute-start | bytes 49160 | tf_op jit(solution)/shard_map/ppermute | solution.py:14
  119.5 2.8 copy-start.4
  119.5 3.1 slice-start
  123.3 9.7 %collective-permute-start.4 = (f32[1,32,512]{2,1,0:T(8,128)S(1)}, f32[1,32,512]{2,1,0:T(8,128)S(1)}, u32[]{:S(2)}, u32[]{:S(2)}) collective-permute-start(f32[1,32,512]{2,1,0:T(8,128)S(1)} %slice_bitcast_fusion.7), channel_id=1, source_target_pairs={{4,0},{8,4},{12,8},{16,12},{20,16},{24,20},{28,24},{32,28},{36,32}... | collective-permute-start | bytes 196616 | tf_op jit(solution)/shard_map/ppermute | solution.py:14
  133.0 7.5 collective-permute-start.5
  139.5 9.7 %copy-start.6 = (f32[8,31,1,512]{3,0,2,1:T(8,128)S(1)}, f32[8,31,1,512]{3,0,2,1:T(8,128)}, u32[]{:S(2)}) copy-start(f32[8,31,1,512]{3,0,2,1:T(8,128)} %get-tuple-element.219) | copy-start | bytes 1523716
  141.0 4.8 collective-permute-start.6
  145.8 4.1 collective-permute-start.7
  150.1 12.2 %collective-permute-start.8 = (f32[1,16,512]{2,1,0:T(8,128)S(1)}, f32[1,16,512]{2,1,0:T(8,128)S(1)}, u32[]{:S(2)}, u32[]{:S(2)}) collective-permute-start(f32[1,16,512]{2,1,0:T(8,128)S(1)} %get-tuple-element.227), channel_id=1, source_target_pairs={{4,0},{8,4},{12,8},{16,12},{20,16},{24,20},{28,24},{32,28},{36,32}... | collective-permute-start | bytes 98312 | tf_op jit(solution)/shard_map/ppermute | solution.py:14
  162.3 4.9 collective-permute-start.9
  167.4 4.6 collective-permute-start.10
  172.0 4.1 collective-permute-start.11
  176.9 1.2 copy-start.2
  254.6 49.2 %collective-permute-start.19 = (f32[4096,128]{1,0:T(8,128)}, f32[4096,128]{1,0:T(8,128)}, u32[]{:S(2)}, u32[]{:S(2)}) collective-permute-start(f32[4096,128]{1,0:T(8,128)} %slice.221), channel_id=1, source_target_pairs={{1,0},{2,1},{3,2},{4,3},{5,4},{6,5},{7,6},{8,7},{9,8},{10,9},{11,1... | collective-permute-start | bytes 6291464 | tf_op jit(solution)/shard_map/ppermute | solution.py:14
  258.3 45.5 %collective-permute-start.12 = (f32[4096]{0:T(1024)S(1)}, f32[4096]{0:T(1024)S(1)}, u32[]{:S(2)}, u32[]{:S(2)}) collective-permute-start(f32[4096]{0:T(1024)S(1)} %slice.260), channel_id=1, source_target_pairs={{1,0},{2,1},{3,2},{4,3},{5,4},{6,5},{7,6},{8,7},{9,8},{10,9},{11,1... | collective-permute-start | bytes 49160 | tf_op jit(solution)/shard_map/ppermute | solution.py:14
  307.9 47.9 %collective-permute-start.20 = (f32[4096,128]{1,0:T(8,128)S(1)}, f32[4096,128]{1,0:T(8,128)S(1)}, u32[]{:S(2)}, u32[]{:S(2)}) collective-permute-start(f32[4096,128]{1,0:T(8,128)S(1)} %broadcast_select_fusion.6), channel_id=1, source_target_pairs={{1,0},{2,1},{3,2},{4,3},{5,4},{6,5},{7,6},{8,7},{9,8},{10,9},{11,1... | collective-permute-start | bytes 6291464 | tf_op jit(solution)/shard_map/ppermute | solution.py:14
  311.7 44.0 %collective-permute-start.13 = (f32[4096]{0:T(1024)S(1)}, f32[4096]{0:T(1024)S(1)}, u32[]{:S(2)}, u32[]{:S(2)}) collective-permute-start(f32[4096]{0:T(1024)S(1)} %get-tuple-element.200), channel_id=1, source_target_pairs={{1,0},{2,1},{3,2},{4,3},{5,4},{6,5},{7,6},{8,7},{9,8},{10,9},{11,1... | collective-permute-start | bytes 49160 | tf_op jit(solution)/shard_map/ppermute | solution.py:14
  361.2 54.0 %collective-permute-start.21 = (f32[4096,128]{1,0:T(8,128)S(1)}, f32[4096,128]{1,0:T(8,128)S(1)}, u32[]{:S(2)}, u32[]{:S(2)}) collective-permute-start(f32[4096,128]{1,0:T(8,128)S(1)} %get-tuple-element.173), channel_id=1, source_target_pairs={{2,0},{3,1},{4,2},{5,3},{6,4},{7,5},{8,6},{9,7},{10,8},{11,9},{12,... | collective-permute-start | bytes 6291464 | tf_op jit(solution)/shard_map/ppermute | solution.py:14
  366.5 48.7 %collective-permute-start.14 = (f32[4096]{0:T(1024)S(1)}, f32[4096]{0:T(1024)S(1)}, u32[]{:S(2)}, u32[]{:S(2)}) collective-permute-start(f32[4096]{0:T(1024)S(1)} %get-tuple-element.195), channel_id=1, source_target_pairs={{2,0},{3,1},{4,2},{5,3},{6,4},{7,5},{8,6},{9,7},{10,8},{11,9},{12,... | collective-permute-start | bytes 49160 | tf_op jit(solution)/shard_map/ppermute | solution.py:14
  416.6 38.2 %collective-permute-start.22 = (f32[4096,128]{1,0:T(8,128)S(1)}, f32[4096,128]{1,0:T(8,128)S(1)}, u32[]{:S(2)}, u32[]{:S(2)}) collective-permute-start(f32[4096,128]{1,0:T(8,128)S(1)} %broadcast_select_fusion.4), channel_id=1, source_target_pairs={{4,0},{5,1},{6,2},{7,3},{8,4},{9,5},{10,6},{11,7},{12,8},{13,9},{1... | collective-permute-start | bytes 6291464 | tf_op jit(solution)/shard_map/ppermute | solution.py:14
  418.9 35.8 %collective-permute-start.15 = (f32[4096]{0:T(1024)S(1)}, f32[4096]{0:T(1024)S(1)}, u32[]{:S(2)}, u32[]{:S(2)}) collective-permute-start(f32[4096]{0:T(1024)S(1)} %get-tuple-element.190), channel_id=1, source_target_pairs={{4,0},{5,1},{6,2},{7,3},{8,4},{9,5},{10,6},{11,7},{12,8},{13,9},{1... | collective-permute-start | bytes 49160 | tf_op jit(solution)/shard_map/ppermute | solution.py:14
  458.3 48.3 %collective-permute-start.23 = (f32[4096,128]{1,0:T(8,128)S(1)}, f32[4096,128]{1,0:T(8,128)S(1)}, u32[]{:S(2)}, u32[]{:S(2)}) collective-permute-start(f32[4096,128]{1,0:T(8,128)S(1)} %get-tuple-element.171), channel_id=1, source_target_pairs={{8,0},{9,1},{10,2},{11,3},{12,4},{13,5},{14,6},{15,7},{16,8},{17,9... | collective-permute-start | bytes 6291464 | tf_op jit(solution)/shard_map/ppermute | solution.py:14
  459.6 47.0 %collective-permute-start.16 = (f32[4096]{0:T(1024)S(1)}, f32[4096]{0:T(1024)S(1)}, u32[]{:S(2)}, u32[]{:S(2)}) collective-permute-start(f32[4096]{0:T(1024)S(1)} %get-tuple-element.185), channel_id=1, source_target_pairs={{8,0},{9,1},{10,2},{11,3},{12,4},{13,5},{14,6},{15,7},{16,8},{17,9... | collective-permute-start | bytes 49160 | tf_op jit(solution)/shard_map/ppermute | solution.py:14
  508.0 59.6 %collective-permute-start.24 = (f32[4096,128]{1,0:T(8,128)S(1)}, f32[4096,128]{1,0:T(8,128)S(1)}, u32[]{:S(2)}, u32[]{:S(2)}) collective-permute-start(f32[4096,128]{1,0:T(8,128)S(1)} %broadcast_select_fusion.2), channel_id=1, source_target_pairs={{16,0},{17,1},{18,2},{19,3},{20,4},{21,5},{22,6},{23,7},{24,8},{25... | collective-permute-start | bytes 6291464 | tf_op jit(solution)/shard_map/ppermute | solution.py:14
  509.3 58.3 %collective-permute-start.17 = (f32[4096]{0:T(1024)S(1)}, f32[4096]{0:T(1024)S(1)}, u32[]{:S(2)}, u32[]{:S(2)}) collective-permute-start(f32[4096]{0:T(1024)S(1)} %get-tuple-element.180), channel_id=1, source_target_pairs={{16,0},{17,1},{18,2},{19,3},{20,4},{21,5},{22,6},{23,7},{24,8},{25... | collective-permute-start | bytes 49160 | tf_op jit(solution)/shard_map/ppermute | solution.py:14
  571.1 80.2 %collective-permute-start.25 = (f32[4096,128]{1,0:T(8,128)S(1)}, f32[4096,128]{1,0:T(8,128)S(1)}, u32[]{:S(2)}, u32[]{:S(2)}) collective-permute-start(f32[4096,128]{1,0:T(8,128)S(1)} %get-tuple-element.169), channel_id=1, source_target_pairs={{32,0},{33,1},{34,2},{35,3},{36,4},{37,5},{38,6},{39,7},{40,8},{41... | collective-permute-start | bytes 6291464 | tf_op jit(solution)/shard_map/ppermute | solution.py:14
  572.4 78.8 %collective-permute-start.18 = (f32[4096]{0:T(1024)S(1)}, f32[4096]{0:T(1024)S(1)}, u32[]{:S(2)}, u32[]{:S(2)}) collective-permute-start(f32[4096]{0:T(1024)S(1)} %get-tuple-element.175), channel_id=1, source_target_pairs={{32,0},{33,1},{34,2},{35,3},{36,4},{37,5},{38,6},{39,7},{40,8},{41... | collective-permute-start | bytes 49160 | tf_op jit(solution)/shard_map/ppermute | solution.py:14
  652.8 127.6 %collective-permute-start.26 = (f32[4096,128]{1,0:T(8,128)S(1)}, f32[4096,128]{1,0:T(8,128)S(1)}, u32[]{:S(2)}, u32[]{:S(2)}) collective-permute-start(f32[4096,128]{1,0:T(8,128)S(1)} %broadcast_select_fusion), channel_id=1, source_target_pairs={{64,0},{65,1},{66,2},{67,3},{68,4},{69,5},{70,6},{71,7},{72,8},{73... | collective-permute-start | bytes 6291464 | tf_op jit(solution)/shard_map/ppermute | solution.py:14
where the time goes:
time: 791 us; the launch traced here: 783 us
  waiting for transfers between devices  494 us (62%)
  starting transfers between devices  77.5 us (10%)
  blocking collectives  68 us (9%)
  local copies, waits for them, and re-layouts  57 us (7%)
  other arithmetic  50 us (6%)
  loops' own time  18.3 us (2%)
  matrix products  13.4 us (2%)
    ppermute x27, waiting for transfers between devices, shifted(): lax.ppermute(value, axis, [(source, source + steps) for source in range(l...  494 us
    ppermute x27, starting transfers between devices, shifted(): lax.ppermute(value, axis, [(source, source + steps) for source in range(l...  77.5 us
    unnamed x1, blocking collectives  68 us
    select_n x7, other arithmetic, on_device(): jnp.where(chosen[:, None], packed, 0.0)  20.5 us
  transfers between devices with their start and end apart: 27, of which 17 were waited for; matrix products, arithmetic and copies ran while one was open for 3% of the time, Pallas kernels for 0%

commit v1 on v0

v1 whole, which is shorter than its diff:
```python
import jax
import jax.numpy as jnp
from jax import lax
from jax.experimental import pallas as pl
from jax.experimental.pallas import tpu as pltpu
from jax.sharding import PartitionSpec as P

ALL = ("gx", "gy")
SUB = 8
LANES = 128
VMEM = pl.BlockSpec(memory_space=pltpu.VMEM)
SMEM = pl.BlockSpec(memory_space=pltpu.SMEM)
PARAMS = pltpu.CompilerParams(vmem_limit_bytes=48 * 2**20)


def shifted(value, axis, steps):
    count = lax.axis_size(axis)
    leading, last = (max(0, -steps), min(count, count - steps))
    return lax.ppermute(value, axis, [(source, source + steps) for source in range(leading, last)])


def sublane():
    return lax.broadcasted_iota(jnp.int32, (SUB, LANES), 0)


def rolled(tile, steps):
    return pltpu.roll(tile, steps % SUB, 0)


def neighbours(tiles, s, sub):
    up = [rolled(t, -s) for t in tiles]
    down = up if 2 * s == SUB else [rolled(t, s) for t in tiles]
    return [
        jnp.where(sub < SUB - s, up[k], up[k + 1]) + jnp.where(sub >= s, down[k], down[k - 1])
        for k in range(1, len(tiles) - 1)
    ]


def weight(value, chosen):
    return jnp.where(chosen, jnp.float32(value), jnp.float32(0.0))


def lift_rows(tiles, s, sub, has_left, has_right):
    odd = weight(0.5, sub % (2 * s) == s)
    even = weight(0.25, sub % (2 * s) == 0)
    left, right = tiles[0], tiles[-1]
    inner = [t - odd * n for t, n in zip(tiles[1:-1], neighbours(tiles, s, sub))]
    ahead = rolled(tiles[1], -s)
    left = left - jnp.where(sub == SUB - s, 0.5 * has_left * ahead, 0.0)
    full = [left] + inner + [right]
    smooth = [t + even * n for t, n in zip(inner, neighbours(full, s, sub))]
    behind = rolled(inner[-1], s)
    if s == 1:
        right = jnp.where(sub == 0, rolled(right, -1) + 0.25 * has_right * behind, right)
        left = left + jnp.where(sub == SUB - 2, 0.25 * rolled(left, -1), 0.0)
    elif s == 2:
        right = jnp.where(
            sub == 0, 0.875 * right + rolled(right, -2) + 0.25 * has_right * behind, right
        )
        left = left + jnp.where(sub == SUB - 4, 0.25 * rolled(left, -2), 0.0)
    return [left] + smooth + [right]


def combine(first, second, scale):
    return [a + scale * b for a, b in zip(first, second)]


def front_parts(c):
    d1, d3, d5 = (combine(c[k], combine(c[k - 1], c[k + 1], 1.0), -0.5) for k in (1, 3, 5))
    c2 = combine(c[2], combine(d1, d3, 1.0), 0.25)
    c4 = combine(c[4], combine(d3, d5, 1.0), 0.25)
    third = [0.25 * (a - 0.5 * b) for a, b in zip(c2, c4)]
    return c[0], combine(c[0], d1, 0.25), third


def back_parts(c):
    d = {k: combine(c[k], combine(c[k - 1], c[k + 1], 1.0), -0.5) for k in (3, 5, 7, 9, 11, 13)}
    e = {k: combine(c[k], combine(d[k - 1], d[k + 1], 1.0), 0.25) for k in (4, 6, 8, 10, 12)}
    d6 = combine(e[6], combine(e[4], e[8], 1.0), -0.5)
    d10 = combine(e[10], combine(e[8], e[12], 1.0), -0.5)
    f8 = combine(e[8], combine(d6, d10, 1.0), 0.25)
    first = combine(c[15], c[14], -0.5)
    second = combine(combine(c[14], d[13], 0.25), e[12], -0.5)
    third = combine(combine(e[12], d10, 0.25), f8, -0.5)
    return first, second, third


def y_edges_kernel(head_ref, tail_ref, to_before_ref, to_after_ref):
    rows = head_ref.shape[0]
    half = rows // 2
    sub = sublane()
    zero = jnp.zeros((SUB, LANES), jnp.float32)

    def before(x, lanes):
        v = head_ref[x, :, lanes]
        d1 = v - weight(0.5, sub % 2 == 1) * (rolled(v, -1) + rolled(v, 1))
        c2 = d1 + 0.25 * (rolled(d1, -1) + rolled(d1, 1))
        second = rolled(v, 1) + 0.25 * d1
        third = 0.25 * (c2 - 0.5 * rolled(c2, -2))
        return jnp.where(
            sub == 0, v, jnp.where(sub == 1, second, jnp.where(sub == 2, third, 0.0))
        )

    def after(x, lanes):
        v = [zero, tail_ref[x, :SUB, lanes], tail_ref[x, SUB:, lanes], zero]
        odd = weight(0.5, sub % 2 == 1)
        d = [zero] + [t - odd * n for t, n in zip(v[1:-1], neighbours(v, 1, sub))] + [zero]
        even = weight(0.25, sub % 2 == 0)
        e = [zero] + [t + even * n for t, n in zip(d[1:-1], neighbours(d, 1, sub))] + [zero]
        odd = weight(0.5, sub % 4 == 2)
        f = [zero] + [t - odd * n for t, n in zip(e[1:-1], neighbours(e, 2, sub))] + [zero]
        even = weight(0.25, sub % 4 == 0)
        g = [t + even * n for t, n in zip(f[1:-1], neighbours(f, 2, sub))]
        first = d[2]
        second = v[2] + 0.25 * rolled(d[2], 1) - 0.5 * rolled(e[2], 2)
        third = e[2] + 0.25 * rolled(f[2], 2) - 0.5 * rolled(g[1], 4)
        return jnp.where(
            sub == 7, first, jnp.where(sub == 6, second, jnp.where(sub == 4, third, 0.0))
        )

    @pl.loop(0, half)
    def _(x):
        for t in range(head_ref.shape[2] // LANES):
            lanes = slice(t * LANES, (t + 1) * LANES)
            to_before_ref[x, :, lanes] = before(x, lanes) + rolled(before(x + half, lanes), 4)
            to_after_ref[x, :, lanes] = after(x, lanes) + rolled(after(x + half, lanes), 4)


def y_edges(snapshot):
    rows, cols, depth = snapshot.shape
    shape = jax.ShapeDtypeStruct((rows // 2, SUB, depth), jnp.float32)
    return pl.pallas_call(
        y_edges_kernel,
        grid=(1,),
        in_specs=[
            pl.BlockSpec((rows, SUB, depth), lambda i: (0, 0, 0)),
            pl.BlockSpec((rows, 2 * SUB, depth), lambda i: (0, cols // (2 * SUB) - 1, 0)),
        ],
        out_specs=[pl.BlockSpec(shape.shape, lambda i: (0, 0, 0))] * 2,
        out_shape=[shape] * 2,
        compiler_params=PARAMS,
        name="y_edges",
    )(snapshot, snapshot)


def row_of(snapshot_ref, left_ref, right_ref, x, lanes, sub):
    rows, cols, _ = snapshot_ref.shape
    half = rows // 2
    left = left_ref[x % half, :, lanes]
    right = right_ref[x % half, :, lanes]
    if x >= half:
        left, right = rolled(left, 4), rolled(right, 4)
    left = jnp.where(sub >= 4, left, 0.0)
    right = jnp.where(sub < 4, right, 0.0)
    inner = [snapshot_ref[x, SUB * k : SUB * (k + 1), lanes] for k in range(cols // SUB)]
    return [left] + inner + [right]


def x_edges_kernel(snapshot_ref, left_ref, right_ref, to_before_ref, to_after_ref):
    rows, cols, depth = snapshot_ref.shape
    sub = sublane()
    half = rows // 2
    count = cols // SUB

    def tile(x, k, lanes):
        if k == 0:
            left = left_ref[x % half, :, lanes]
            return jnp.where(sub >= 4, rolled(left, 4) if x >= half else left, 0.0)
        if k == count + 1:
            right = right_ref[x % half, :, lanes]
            return jnp.where(sub < 4, rolled(right, 4) if x >= half else right, 0.0)
        return snapshot_ref[x, SUB * (k - 1) : SUB * k, lanes]

    @pl.loop(0, depth // LANES)
    def _(t):
        lanes = pl.ds(pl.multiple_of(t * LANES, LANES), LANES)
        for k in range(count + 2):
            c = {x: [tile(x, k, lanes)] for x in range(rows)}
            for level, (a, b) in enumerate(zip(front_parts(c), back_parts(c))):
                to_before_ref[level, SUB * k : SUB * (k + 1), lanes] = a[0]
                to_after_ref[level, SUB * k : SUB * (k + 1), lanes] = b[0]


def x_edges(snapshot, left, right):
    rows, cols, depth = snapshot.shape
    shape = jax.ShapeDtypeStruct((3, cols + 2 * SUB, depth), jnp.float32)
    return pl.pallas_call(
        x_edges_kernel,
        in_specs=[VMEM] * 3,
        out_specs=[VMEM] * 2,
        out_shape=[shape] * 2,
        compiler_params=PARAMS,
        name="x_edges",
    )(snapshot, left, right)


def main_kernel(
    counts_ref,
    row_counts_ref,
    scales_ref,
    snapshot_ref,
    left_ref,
    right_ref,
    before_ref,
    after_ref,
    flags_ref,
    coefficients_ref,
    packed_ref,
    buffer,
    ranks,
):
    rows, cols, depth = snapshot_ref.shape
    slots = packed_ref.shape[0]
    width = depth // LANES
    count = cols // SUB
    per_row = cols * width
    sub = sublane()
    gx, gy = lax.axis_index("gx"), lax.axis_index("gy")
    one, zero = jnp.float32(1.0), jnp.float32(0.0)
    x_left = jnp.where(gx > 0, one, zero)
    x_right = jnp.where(gx < lax.axis_size("gx") - 1, one, zero)
    y_left = jnp.where(gy > 0, one, zero)
    y_right = jnp.where(gy < lax.axis_size("gy") - 1, one, zero)
    device = gx * lax.axis_size("gy") + gy

    scale = [scales_ref[k] for k in range(4)]
    factor = {8: jnp.where(sub % 8 == 0, scale[3], scale[2])}
    factor[4] = jnp.where(sub % 4 == 0, scale[2], scale[1])
    factor[2] = jnp.where(sub % 2 == 0, scale[1], scale[0])
    factor[8] = jnp.where(sub % 4 == 0, factor[8], factor[2])
    factor[4] = jnp.where(sub % 4 == 0, factor[4], factor[2])
    factor[1] = jnp.where(sub % 2 == 0, scale[0], scale[0])
    factor[8] = jnp.where(sub % 2 == 0, factor[8], scale[0])
    factor[4] = jnp.where(sub % 2 == 0, factor[4], scale[0])

    @pl.loop(0, width)
    def _(t):
        lanes = pl.ds(pl.multiple_of(t * LANES, LANES), LANES)

        def load(ref, level):
            return [ref[level, SUB * k : SUB * (k + 1), lanes] for k in range(count + 2)]

        def store(x, row):
            by = 8 if x % 8 == 0 else 4 if x % 4 == 0 else 2 if x % 2 == 0 else 1
            for k in range(count):
                coefficients_ref[x, SUB * k : SUB * (k + 1), lanes] = factor[by] * row[k + 1]

        def step(c, s, beyond, ahead, mine):
            held = sub % s == 0
            half_w, quarter_w = weight(0.5, held), weight(0.25, held)
            end = rows
            c[end] = beyond
            for x in range(s, rows, 2 * s):
                c[x] = [v - half_w * (a + b) for v, a, b in zip(c[x], c[x - s], c[x + s])]
            c[-s] = [v - (half_w * x_left) * a for v, a in zip(ahead, c[0])]
            for x in range(0, rows, 2 * s):
                c[x] = [v + quarter_w * (a + b) for v, a, b in zip(c[x], c[x - s], c[x + s])]
            past = [v + (0.25 * x_right) * a for v, a in zip(mine, c[rows - s])] if mine else None
            return c, past, c[-s]

        def lift(row, s):
            return lift_rows(row, s, sub, y_left, y_right)

        c = {x: row_of(snapshot_ref, left_ref, right_ref, x, lanes, sub) for x in range(rows)}
        c, past, d = step(c, 1, load(after_ref, 0), load(before_ref, 0), load(after_ref, 1))
        for x in range(1, rows, 2):
            store(x, c[x])
        kept = combine(load(before_ref, 1), d, 0.25)
        for x in range(0, rows, 2):
            c[x] = lift(c[x], 1)
        past, kept = lift(past, 1), lift(kept, 1)
        after3, before3 = lift(load(after_ref, 2), 1), lift(load(before_ref, 2), 1)
        mine = [0.875 * v + a for v, a in zip(past, after3)]
        c, past, d = step(c, 2, past, kept, mine)
        for x in range(2, rows, 4):
            store(x, c[x])
        kept = combine(before3, d, 0.25)
        for x in range(0, rows, 4):
            c[x] = lift(c[x], 2)
        past, kept = lift(past, 2), lift(kept, 2)
        c, past, d = step(c, 4, past, kept, None)
        for x in range(4, rows, 8):
            store(x, c[x])
        for x in range(0, rows, 8):
            store(x, lift(c[x], 4))

    buffer[...] = jnp.zeros_like(buffer)
    flags = flags_ref[...]
    source = lax.broadcasted_iota(jnp.int32, (per_row, per_row), 0)
    target = lax.broadcasted_iota(jnp.int32, (per_row, per_row), 1)
    source = source % cols * width + source // cols
    target = target % cols * width + target // cols
    earlier = jnp.where(source < target, one, zero).astype(jnp.bfloat16)
    place = jnp.dot(flags.astype(jnp.bfloat16), earlier, preferred_element_type=jnp.float32)
    ranks[...] = jnp.where(flags > 0, place.astype(jnp.int32), -per_row)

    start = lax.fori_loop(0, device, lambda s, total: total + counts_ref[s], jnp.int32(0))
    span = per_row + SUB

    def pack(x, start):
        at = start % slots
        base = pl.multiple_of(at // SUB * SUB, SUB)
        wanted = ranks[pl.ds(x, 1), :] + (at - base)
        row_id = lax.broadcasted_iota(jnp.int32, (span, per_row), 0)
        onehot = jnp.where(row_id == wanted, one, zero).astype(jnp.bfloat16)
        values = jnp.concatenate(
            [coefficients_ref[x, :, LANES * t : LANES * (t + 1)] for t in range(width)], axis=0
        )
        high = values.astype(jnp.bfloat16)
        low = (values - high.astype(jnp.float32)).astype(jnp.bfloat16)
        both = jnp.dot(
            onehot, jnp.concatenate([high, low], axis=1), preferred_element_type=jnp.float32
        )
        buffer[pl.ds(base, span), :] += both[:, :LANES] + both[:, LANES:]
        return start + row_counts_ref[x]

    lax.fori_loop(0, rows, pack, start)
    packed_ref[span:, :] = buffer[span:slots, :]
    packed_ref[:span, :] = buffer[:span, :] + buffer[slots:, :]


def main(counts, row_counts, scales, snapshot, left, right, before, after, flags):
    rows, cols, depth = snapshot.shape
    per_row = flags.shape[1]
    slots = rows * per_row
    return pl.pallas_call(
        main_kernel,
        in_specs=[SMEM] * 3 + [VMEM] * 6,
        out_specs=[VMEM] * 2,
        out_shape=[
            jax.ShapeDtypeStruct(snapshot.shape, jnp.float32),
            jax.ShapeDtypeStruct((slots, LANES), jnp.float32),
        ],
        scratch_shapes=[
            pltpu.VMEM((slots + per_row + SUB, LANES), jnp.float32),
            pltpu.VMEM((rows, per_row), jnp.int32),
        ],
        compiler_params=PARAMS,
        name="lift_and_pack",
    )(counts, row_counts, scales, snapshot, left, right, before, after, flags)


def merge_kernel(counts_ref, arrived_ref, merged_ref, buffer):
    devices, share, _ = arrived_ref.shape
    slots = devices * share
    device = lax.axis_index("gx") * lax.axis_size("gy") + lax.axis_index("gy")
    buffer[...] = jnp.zeros_like(buffer)
    row_id = lax.broadcasted_iota(jnp.int32, (share, LANES), 0)

    def one(s, start):
        block = start // slots
        first = start % slots - device * share
        rows = arrived_ref[s]
        here = row_id >= first
        buffer[block] += jnp.where(here, rows, 0.0)
        buffer[block + 1] += jnp.where(here, 0.0, rows)
        return start + counts_ref[s]

    lax.fori_loop(0, devices, one, jnp.int32(0))
    merged_ref[...] = buffer[:devices]


def merge(counts, arrived):
    devices, share, _ = arrived.shape
    return pl.pallas_call(
        merge_kernel,
        in_specs=[SMEM, VMEM],
        out_specs=VMEM,
        out_shape=jax.ShapeDtypeStruct(arrived.shape, jnp.float32),
        scratch_shapes=[pltpu.VMEM((devices + 2, share, LANES), jnp.float32)],
        compiler_params=PARAMS,
        name="merge",
    )(counts, arrived)


def on_device(snapshot, keep_mask, exponents):
    rows, cols, depth = snapshot.shape
    width = keep_mask.shape[2]
    devices = lax.axis_size("gx") * lax.axis_size("gy")
    slots = rows * cols * width
    to_before, to_after = y_edges(snapshot)
    right = shifted(to_before, "gy", -1)
    left = shifted(to_after, "gy", 1)
    row_counts = jnp.sum(keep_mask, axis=(1, 2))
    own = jnp.sum(row_counts)
    counts = lax.all_to_all(jnp.full((devices,), own, jnp.int32), ALL, 0, 0, tiled=True)
    flags = keep_mask.transpose(0, 2, 1).reshape(rows, cols * width)
    scales = jnp.exp2(exponents.astype(jnp.float32))
    x_before, x_after = x_edges(snapshot, left, right)
    after = shifted(x_before, "gx", -1)
    before = shifted(x_after, "gx", 1)
    coefficients, packed = main(
        counts, row_counts, scales, snapshot, left, right, before, after, flags
    )
    share = slots // devices
    arrived = lax.all_to_all(packed.reshape(devices, share, LANES), ALL, 0, 0, tiled=True)
    merged = merge(counts, arrived)
    stream = lax.all_to_all(merged, ALL, 0, 0, tiled=True).reshape(slots, LANES)
    return coefficients, stream


def solution(mesh):
    in_specs = (P("gx", "gy", None), P("gx", "gy", None), P())
    out_specs = (P("gx", "gy", None), P(("gx", "gy"), None))
    return jax.shard_map(
        on_device, mesh=mesh, in_specs=in_specs, out_specs=out_specs, check_vma=False
    )
```

time: 791 us -> 127 us (0.16)
  waiting for transfers between devices: 494 us -> 14 us
  starting transfers between devices: 77.5 us -> 22.7 us
  local copies, waits for them, and re-layouts: 57 us -> 4.29 us
  other arithmetic: 50 us -> 3.33 us
  loops' own time: 18.3 us -> 0 us
  matrix products: 13.4 us -> 0 us
  Pallas kernels: 0 us -> 11.8 us
    ppermute x27 -> x4, waiting for transfers between devices: 494 us -> 4.42 us  [shifted(): lax.ppermute(value, axis, [(source, source + steps) for source in range(l...]
    all_to_all x0 -> x2, blocking collectives: none -> 69.3 us  [the longest x1 35.2 us: on_device(): lax.all_to_all(packed.reshape(devices, share, LANES), ALL, 0, 0, tiled=True)]
    unnamed x1 -> x0, blocking collectives: 68 us -> none
    ppermute x27 -> x4, starting transfers between devices: 77.5 us -> 12.5 us  [shifted(): lax.ppermute(value, axis, [(source, source + steps) for source in range(l...]
    select_n x13 -> x0, other arithmetic: 20.8 us -> none  [the longest x7 20.5 us: on_device(): jnp.where(chosen[:, None], packed, 0.0)]
    slice x48 -> x0, local copies, waits for them, and re-layouts: 19.5 us -> none  [the longest x7 4.98 us: predict(): lax.slice_in_dim(even_part, 1, length, axis=dim)]
    another operation x2 -> x0, loops' own time: 18.3 us -> none  [the longest x1 15.6 us: on_device(): window = lax.fori_loop(0, slots // block, place, window)]
    dynamic_update_slice x8 -> x0, local copies, waits for them, and re-layouts: 14.9 us -> none  [place(): lax.dynamic_update_slice_in_dim(window_now, current + product_rows, base, 0)]
  transfers between devices with their start and end apart: 27 -> 5, of which waited for: 17 -> 3; matrix products, arithmetic and copies ran while one was open for 3% -> 4% of each run, Pallas kernels for 0% -> 0%
where the time goes in v1:
time: 127 us; the launch traced here: 126 us
  blocking collectives  69.3 us (55%)
  starting transfers between devices  22.7 us (18%)
  waiting for transfers between devices  14 us (11%)
  Pallas kernels  11.8 us (9%)
  local copies, waits for them, and re-layouts  4.29 us (3%)
  other arithmetic  3.33 us (3%)
    all_to_all x1, blocking collectives, on_device(): lax.all_to_all(packed.reshape(devices, share, LANES), ALL, 0, 0, tiled=True)  35.2 us
    all_to_all x1, blocking collectives, on_device(): stream = lax.all_to_all(merged, ALL, 0, 0, tiled=True).reshape(slots, LANES)  34.2 us
    ppermute x4, starting transfers between devices, shifted(): lax.ppermute(value, axis, [(source, source + steps) for source in range(l...  12.5 us
    all_to_all x1, starting transfers between devices, on_device(): lax.all_to_all(jnp.full((devices,), own, jnp.int32), ALL, 0, 0, tiled=True)  10.2 us
    all_to_all x1, waiting for transfers between devices, on_device(): lax.all_to_all(jnp.full((devices,), own, jnp.int32), ALL, 0, 0, tiled=True)  9.56 us
    pallas_call x1, Pallas kernels, main(): pl.pallas_call(main_kernel, in_specs=[SMEM] * 3 + [VMEM] * 6, out_specs=[...  7.31 us
    ppermute x4, waiting for transfers between devices, shifted(): lax.ppermute(value, axis, [(source, source + steps) for source in range(l...  4.42 us
    unnamed x9, local copies, waits for them, and re-layouts  2.92 us
  transfers between devices with their start and end apart: 5, of which 3 were waited for; matrix products, arithmetic and copies ran while one was open for 4% of the time, Pallas kernels for 0%

profile of v1, /device:TPU:1, one launch (start us, length us, event | category | flops | bytes accessed | tf_op | source)
XLA Modules:
  0.0 126.3 jit_solution(10766838212150858199)
XLA Ops:
  0.6 0.0 copy-start
  0.6 1.6 %copy-done = f32[16,64,512]{2,1,0:T(8,128)S(1)} copy-done((f32[16,64,512]{2,1,0:T(8,128)S(1)}, f32[16,64,512]{2,1,0:T(8,128)}, u32[]{:S(2)}) %copy-start) | copy-done | bytes 2097176
  2.2 0.9 y_edges.1
  3.1 0.0 copy-start.2
  3.1 0.0 copy-start.3
  3.1 0.0 copy-start.1
  3.1 4.1 %collective-permute-start = (f32[8,8,512]{2,1,0:T(8,128)S(1)}, f32[8,8,512]{2,1,0:T(8,128)S(1)}, u32[]{:S(2)}, u32[]{:S(2)}) collective-permute-start(f32[8,8,512]{2,1,0:T(8,128)S(1)} %get-tuple-element.8), channel_id=1, source_target_pairs={{0,1},{1,2},{2,3},{4,5},{5,6},{6,7},{8,9},{9,10},{10,11},{12,13},{... | collective-permute-start | bytes 393224 | tf_op jit(solution)/shard_map/ppermute | solution.py:19
  7.2 1.3 %collective-permute-start.1 = (f32[8,8,512]{2,1,0:T(8,128)S(1)}, f32[8,8,512]{2,1,0:T(8,128)S(1)}, u32[]{:S(2)}, u32[]{:S(2)}) collective-permute-start(f32[8,8,512]{2,1,0:T(8,128)S(1)} %get-tuple-element.9), channel_id=1, source_target_pairs={{1,0},{2,1},{3,2},{5,4},{6,5},{7,6},{9,8},{10,9},{11,10},{13,12},{... | collective-permute-start | bytes 393224 | tf_op jit(solution)/shard_map/ppermute | solution.py:19
  8.5 0.8 collective-permute-done.left_ref
  9.4 3.6 %collective-permute-done.1.right_ref = f32[8,8,512]{2,1,0:T(8,128)S(1)} collective-permute-done((f32[8,8,512]{2,1,0:T(8,128)S(1)}, f32[8,8,512]{2,1,0:T(8,128)S(1)}, u32[]{:S(2)}, u32[]{:S(2)}) %collective-permute-start.1) | collective-permute-done | bytes 131104 | tf_op jit(solution)/shard_map/ppermute | solution.py:19
  12.9 1.4 %x_edges.1 = (f32[3,80,512]{2,1,0:T(8,128)}, f32[3,80,512]{2,1,0:T(8,128)}) custom-call(f32[16,64,512]{2,1,0:T(8,128)S(1)} %copy-done, f32[8,8,512]{2,1,0:T(8,128)S(1)} %collective-permute-done.left_ref, f32[8,8,512]{2,1,0:T(8,128)S(1)} %collective-permute-done.1.right_ref), custom_call_target="tpu_custom_call" | custom-call | tf_op jit(solution)/shard_map/x_edges/pallas_call | solution.py:187
  14.3 5.2 %collective-permute-start.2 = (f32[3,80,512]{2,1,0:T(8,128)}, f32[3,80,512]{2,1,0:T(8,128)S(1)}, u32[]{:S(2)}, u32[]{:S(2)}) collective-permute-start(f32[3,80,512]{2,1,0:T(8,128)} %get-tuple-element.10), channel_id=1, source_target_pairs={{0,4},{4,8},{8,12},{12,16},{16,20},{20,24},{24,28},{28,32},{32,36}... | collective-permute-start | bytes 1474568 | tf_op jit(solution)/shard_map/ppermute | solution.py:19
  19.5 1.9 %collective-permute-start.3 = (f32[3,80,512]{2,1,0:T(8,128)}, f32[3,80,512]{2,1,0:T(8,128)S(1)}, u32[]{:S(2)}, u32[]{:S(2)}) collective-permute-start(f32[3,80,512]{2,1,0:T(8,128)} %get-tuple-element.11), channel_id=1, source_target_pairs={{4,0},{8,4},{12,8},{16,12},{20,16},{24,20},{28,24},{32,28},{36,32}... | collective-permute-start | bytes 1474568 | tf_op jit(solution)/shard_map/ppermute | solution.py:19
  21.4 0.0 copy-done.2
  21.4 1.0 fusion
  22.4 1.3 %broadcast_in_dim.3 = s32[128,1,1]{2,1,0:T(1,128)} broadcast(s32[]{:T(128)} %get-tuple-element.15), dimensions={} | broadcast | bytes 516 | tf_op jit(solution)/shard_map/broadcast_in_dim | solution.py:386
  23.7 10.2 %all-to-all-start = ((s32[128,1,1]{2,1,0:T(1,128)}), s32[128,1,1]{2,1,0:T(1,128)S(1)}, u32[]{:S(2)}, u32[]{:S(2)}) async-start(s32[128,1,1]{2,1,0:T(1,128)} %broadcast_in_dim.3), calls=%async_computation | async-start | bytes 131072 | tf_op jit(solution)/shard_map/all_to_all | solution.py:386
  33.9 0.0 copy-done.3
  34.0 0.1 reshape.15.flags_ref
  34.1 9.6 %all-to-all-done = s32[128,1,1]{2,1,0:T(1,128)S(1)} async-done(((s32[128,1,1]{2,1,0:T(1,128)}), s32[128,1,1]{2,1,0:T(1,128)S(1)}, u32[]{:S(2)}, u32[]{:S(2)}) %all-to-all-start) | async-done | bytes 544 | tf_op jit(solution)/shard_map/all_to_all | solution.py:386
  43.6 2.3 %reduce.1.counts_ref = s32[128]{0:T(128)S(1)} reduce(s32[128,1,1]{2,1,0:T(1,128)S(1)} %all-to-all-done, s32[]{:T(128)} %constant.0.clone.1), dimensions={1,2}, to_apply=%all_to_all.11.reduce_sub_computation | reduce | bytes 1028 | tf_op jit(solution)/shard_map/all_to_all | solution.py:386
  46.0 0.0 collective-permute-done.2.before_ref
  46.0 0.0 collective-permute-done.3.after_ref
  46.0 0.0 copy-done.1
  46.0 7.3 %lift_and_pack.1 = (f32[16,64,512]{2,1,0:T(8,128)}, f32[4096,128]{1,0:T(8,128)S(1)}) custom-call(s32[128]{0:T(128)S(1)} %reduce.1.counts_ref, s32[16]{0:T(128)S(1)} %get-tuple-element.14.row_counts_ref, f32[4]{0:T(128)S(1)} %multiply_exponential_fusion.scales_ref, f32[16,64,512]{2,1,0:T(8,128)S(1)} %copy-done.1, ...), custom_call_target="tpu_custom_call" | custom-call | tf_op jit(solution)/shard_map/lift_and_pack/pallas_call | solution.py:326
  53.3 35.2 %all_to_all.18.arrived_ref = f32[128,32,128]{2,1,0:T(8,128)S(1)} all-to-all(f32[128,32,128]{2,1,0:T(8,128)S(1)} %bitcast.3), channel_id=1, replica_groups=mesh['gx'=32,'gy'=4] {'gx','gy'}, dimensions={0} | all-to-all | bytes 4194304 | tf_op jit(solution)/shard_map/all_to_all | solution.py:396
  88.5 2.3 %merge.1 = f32[128,32,128]{2,1,0:T(8,128)S(1)} custom-call(s32[128]{0:T(128)S(1)} %reduce.1.counts_ref, f32[128,32,128]{2,1,0:T(8,128)S(1)} %all_to_all.18.arrived_ref), custom_call_target="tpu_custom_call" | custom-call | tf_op jit(solution)/shard_map/merge/pallas_call | solution.py:365
  90.8 34.2 %all_to_all.19 = f32[128,32,128]{2,1,0:T(8,128)S(1)} all-to-all(f32[128,32,128]{2,1,0:T(8,128)S(1)} %merge.1), channel_id=1, replica_groups=mesh['gx'=32,'gy'=4] {'gx','gy'}, dimensions={0} | all-to-all | bytes 4194304 | tf_op jit(solution)/shard_map/all_to_all | solution.py:398
  124.9 1.3 %copy.6 = f32[4096,128]{1,0:T(8,128)} copy(f32[4096,128]{1,0:T(8,128)S(1)} %bitcast.4) | data formatting | bytes 4194304
  (1 shorter events, 0.0 us)
Async XLA Ops:
  0.6 1.6 %copy-start = (f32[16,64,512]{2,1,0:T(8,128)S(1)}, f32[16,64,512]{2,1,0:T(8,128)}, u32[]{:S(2)}) copy-start(f32[16,64,512]{2,1,0:T(8,128)} %snapshot_ref.3) | copy-start | bytes 6291460
  3.1 18.3 %copy-start.2 = (s32[16,64,4]{1,2,0:T(4,128)S(1)}, s32[16,64,4]{1,2,0:T(4,128)}, u32[]{:S(2)}) copy-start(s32[16,64,4]{1,2,0:T(4,128)} %param.4) | copy-start | bytes 49156
  3.1 30.8 %copy-start.3 = (s32[4]{0:T(128)S(1)}, s32[4]{0:T(128)}, u32[]{:S(2)}) copy-start(s32[4]{0:T(128)} %param.5) | copy-start | bytes 52
  3.1 42.9 %copy-start.1 = (f32[16,64,512]{2,1,0:T(8,128)S(1)}, f32[16,64,512]{2,1,0:T(8,128)}, u32[]{:S(2)}) copy-start(f32[16,64,512]{2,1,0:T(8,128)} %snapshot_ref.3) | copy-start | bytes 6291460
  3.1 6.2 %collective-permute-start = (f32[8,8,512]{2,1,0:T(8,128)S(1)}, f32[8,8,512]{2,1,0:T(8,128)S(1)}, u32[]{:S(2)}, u32[]{:S(2)}) collective-permute-start(f32[8,8,512]{2,1,0:T(8,128)S(1)} %get-tuple-element.8), channel_id=1, source_target_pairs={{0,1},{1,2},{2,3},{4,5},{5,6},{6,7},{8,9},{9,10},{10,11},{12,13},{... | collective-permute-start | bytes 393224 | tf_op jit(solution)/shard_map/ppermute | solution.py:19
  7.2 5.7 %collective-permute-start.1 = (f32[8,8,512]{2,1,0:T(8,128)S(1)}, f32[8,8,512]{2,1,0:T(8,128)S(1)}, u32[]{:S(2)}, u32[]{:S(2)}) collective-permute-start(f32[8,8,512]{2,1,0:T(8,128)S(1)} %get-tuple-element.9), channel_id=1, source_target_pairs={{1,0},{2,1},{3,2},{5,4},{6,5},{7,6},{9,8},{10,9},{11,10},{13,12},{... | collective-permute-start | bytes 393224 | tf_op jit(solution)/shard_map/ppermute | solution.py:19
  14.3 31.7 %collective-permute-start.2 = (f32[3,80,512]{2,1,0:T(8,128)}, f32[3,80,512]{2,1,0:T(8,128)S(1)}, u32[]{:S(2)}, u32[]{:S(2)}) collective-permute-start(f32[3,80,512]{2,1,0:T(8,128)} %get-tuple-element.10), channel_id=1, source_target_pairs={{0,4},{4,8},{8,12},{12,16},{16,20},{20,24},{24,28},{28,32},{32,36}... | collective-permute-start | bytes 1474568 | tf_op jit(solution)/shard_map/ppermute | solution.py:19
  19.5 26.5 %collective-permute-start.3 = (f32[3,80,512]{2,1,0:T(8,128)}, f32[3,80,512]{2,1,0:T(8,128)S(1)}, u32[]{:S(2)}, u32[]{:S(2)}) collective-permute-start(f32[3,80,512]{2,1,0:T(8,128)} %get-tuple-element.11), channel_id=1, source_target_pairs={{4,0},{8,4},{12,8},{16,12},{20,16},{24,20},{28,24},{32,28},{36,32}... | collective-permute-start | bytes 1474568 | tf_op jit(solution)/shard_map/ppermute | solution.py:19
  23.7 19.9 %all-to-all-start = ((s32[128,1,1]{2,1,0:T(1,128)}), s32[128,1,1]{2,1,0:T(1,128)S(1)}, u32[]{:S(2)}, u32[]{:S(2)}) async-start(s32[128,1,1]{2,1,0:T(1,128)} %broadcast_in_dim.3), calls=%async_computation | async-start | bytes 131072 | tf_op jit(solution)/shard_map/all_to_all | solution.py:386

commit v2 on v1

--- a/solution.py
+++ b/solution.py
@@ -8,9 +8,10 @@
 ALL = ("gx", "gy")
 SUB = 8
 LANES = 128
+TURN = 64
 VMEM = pl.BlockSpec(memory_space=pltpu.VMEM)
 SMEM = pl.BlockSpec(memory_space=pltpu.SMEM)
-PARAMS = pltpu.CompilerParams(vmem_limit_bytes=48 * 2**20)
+PARAMS = pltpu.CompilerParams(vmem_limit_bytes=16 * 2**20)
 
 
 def shifted(value, axis, steps):
@@ -85,11 +86,40 @@
     return first, second, third
 
 
-def y_edges_kernel(head_ref, tail_ref, to_before_ref, to_after_ref):
-    rows = head_ref.shape[0]
+def y_edges_kernel(
+    snapshot_ref,
+    mask_ref,
+    to_before_ref,
+    to_after_ref,
+    counts_ref,
+    starts_ref,
+    head_ref,
+    tail_ref,
+    sems,
+):
+    rows, cols, depth = snapshot_ref.shape
     half = rows // 2
+    copies = [
+        pltpu.make_async_copy(snapshot_ref.at[:, :SUB, :], head_ref, sems.at[0]),
+        pltpu.make_async_copy(snapshot_ref.at[:, cols - 2 * SUB :, :], tail_ref, sems.at[1]),
+    ]
+    for copy in copies:
+        copy.start()
     sub = sublane()
     zero = jnp.zeros((SUB, LANES), jnp.float32)
+
+    kept = mask_ref[:, 0, :]
+    for t in range(1, mask_ref.shape[1]):
+        kept = kept + mask_ref[:, t, :]
+    kept = jnp.sum(kept.astype(jnp.float32), axis=1, keepdims=True)
+    kept = jnp.broadcast_to(kept, (rows, LANES))
+    shape = (rows, rows)
+    later = lax.broadcasted_iota(jnp.int32, shape, 0) > lax.broadcasted_iota(jnp.int32, shape, 1)
+    later = jnp.where(later, jnp.float32(1.0), jnp.float32(0.0)).astype(jnp.bfloat16)
+    starts = jnp.dot(later, kept.astype(jnp.bfloat16), preferred_element_type=jnp.float32)
+    starts_ref[...] = starts.astype(jnp.int32)
+    total = (starts[rows - 1 :, :] + kept[rows - 1 :, :]).astype(jnp.int32)
+    counts_ref[...] = jnp.broadcast_to(total, counts_ref.shape)
 
     def before(x, lanes):
         v = head_ref[x, :, lanes]
@@ -118,29 +148,38 @@
             sub == 7, first, jnp.where(sub == 6, second, jnp.where(sub == 4, third, 0.0))
         )
 
+    for copy in copies:
+        copy.wait()
+
     @pl.loop(0, half)
     def _(x):
-        for t in range(head_ref.shape[2] // LANES):
+        for t in range(depth // LANES):
             lanes = slice(t * LANES, (t + 1) * LANES)
             to_before_ref[x, :, lanes] = before(x, lanes) + rolled(before(x + half, lanes), 4)
             to_after_ref[x, :, lanes] = after(x, lanes) + rolled(after(x + half, lanes), 4)
 
 
-def y_edges(snapshot):
+def y_edges(snapshot, mask, devices):
     rows, cols, depth = snapshot.shape
     shape = jax.ShapeDtypeStruct((rows // 2, SUB, depth), jnp.float32)
     return pl.pallas_call(
         y_edges_kernel,
-        grid=(1,),
-        in_specs=[
-            pl.BlockSpec((rows, SUB, depth), lambda i: (0, 0, 0)),
-            pl.BlockSpec((rows, 2 * SUB, depth), lambda i: (0, cols // (2 * SUB) - 1, 0)),
+        in_specs=[pl.BlockSpec(memory_space=pltpu.HBM), VMEM],
+        out_specs=[VMEM] * 4,
+        out_shape=[
+            shape,
+            shape,
+            jax.ShapeDtypeStruct((devices, LANES), jnp.int32),
+            jax.ShapeDtypeStruct((rows, LANES), jnp.int32),
         ],
-        out_specs=[pl.BlockSpec(shape.shape, lambda i: (0, 0, 0))] * 2,
-        out_shape=[shape] * 2,
+        scratch_shapes=[
+            pltpu.VMEM((rows, SUB, depth), jnp.float32),
+            pltpu.VMEM((rows, 2 * SUB, depth), jnp.float32),
+            pltpu.SemaphoreType.DMA((2,)),
+        ],
         compiler_params=PARAMS,
         name="y_edges",
-    )(snapshot, snapshot)
+    )(snapshot, mask)
 
 
 def row_of(snapshot_ref, left_ref, right_ref, x, lanes, sub):
@@ -156,47 +195,66 @@
     return [left] + inner + [right]
 
 
-def x_edges_kernel(snapshot_ref, left_ref, right_ref, to_before_ref, to_after_ref):
+def x_edges_inner_kernel(snapshot_ref, to_before_ref, to_after_ref):
     rows, cols, depth = snapshot_ref.shape
+
+    @pl.loop(0, cols // SUB)
+    def _(k):
+        inner = pl.ds(pl.multiple_of(SUB * k, SUB), SUB)
+        placed = pl.ds(pl.multiple_of(SUB * k + SUB, SUB), SUB)
+        for t in range(depth // LANES):
+            lanes = slice(t * LANES, (t + 1) * LANES)
+            c = {x: [snapshot_ref[x, inner, lanes]] for x in range(rows)}
+            for level, (a, b) in enumerate(zip(front_parts(c), back_parts(c))):
+                to_before_ref[level, placed, lanes] = a[0]
+                to_after_ref[level, placed, lanes] = b[0]
+
+
+def x_edges_halo_kernel(
+    left_ref, right_ref, before_in_ref, after_in_ref, to_before_ref, to_after_ref
+):
+    half, _, depth = left_ref.shape
+    rows = 2 * half
+    cols = to_before_ref.shape[1] - 2 * SUB
     sub = sublane()
-    half = rows // 2
-    count = cols // SUB
-
-    def tile(x, k, lanes):
-        if k == 0:
-            left = left_ref[x % half, :, lanes]
-            return jnp.where(sub >= 4, rolled(left, 4) if x >= half else left, 0.0)
-        if k == count + 1:
-            right = right_ref[x % half, :, lanes]
-            return jnp.where(sub < 4, rolled(right, 4) if x >= half else right, 0.0)
-        return snapshot_ref[x, SUB * (k - 1) : SUB * k, lanes]
 
     @pl.loop(0, depth // LANES)
     def _(t):
         lanes = pl.ds(pl.multiple_of(t * LANES, LANES), LANES)
-        for k in range(count + 2):
-            c = {x: [tile(x, k, lanes)] for x in range(rows)}
+        for halo_ref, place in ((left_ref, 0), (right_ref, cols + SUB)):
+            held = sub >= 4 if place == 0 else sub < 4
+            packed = [halo_ref[x, :, lanes] for x in range(half)]
+            packed = packed + [rolled(tile, 4) for tile in packed]
+            c = {x: [jnp.where(held, packed[x], 0.0)] for x in range(rows)}
             for level, (a, b) in enumerate(zip(front_parts(c), back_parts(c))):
-                to_before_ref[level, SUB * k : SUB * (k + 1), lanes] = a[0]
-                to_after_ref[level, SUB * k : SUB * (k + 1), lanes] = b[0]
+                to_before_ref[level, place : place + SUB, lanes] = a[0]
+                to_after_ref[level, place : place + SUB, lanes] = b[0]
 
 
 def x_edges(snapshot, left, right):
     rows, cols, depth = snapshot.shape
     shape = jax.ShapeDtypeStruct((3, cols + 2 * SUB, depth), jnp.float32)
-    return pl.pallas_call(
-        x_edges_kernel,
-        in_specs=[VMEM] * 3,
+    before, after = pl.pallas_call(
+        x_edges_inner_kernel,
+        in_specs=[VMEM],
         out_specs=[VMEM] * 2,
         out_shape=[shape] * 2,
         compiler_params=PARAMS,
-        name="x_edges",
-    )(snapshot, left, right)
+        name="x_edges_inner",
+    )(snapshot)
+    return pl.pallas_call(
+        x_edges_halo_kernel,
+        in_specs=[VMEM] * 4,
+        out_specs=[VMEM] * 2,
+        out_shape=[shape] * 2,
+        input_output_aliases={2: 0, 3: 1},
+        compiler_params=PARAMS,
+        name="x_edges_halo",
+    )(left, right, before, after)
 
 
 def main_kernel(
-    counts_ref,
-    row_counts_ref,
+    starts_ref,
     scales_ref,
     snapshot_ref,
     left_ref,
@@ -204,14 +262,15 @@
     before_ref,
     after_ref,
     flags_ref,
+    coefficients_hbm_ref,
+    packed_ref,
     coefficients_ref,
-    packed_ref,
-    buffer,
     ranks,
+    sem,
 ):
     rows, cols, depth = snapshot_ref.shape
-    slots = packed_ref.shape[0]
     width = depth // LANES
+    slots = rows * cols * width
     count = cols // SUB
     per_row = cols * width
     sub = sublane()
@@ -221,7 +280,6 @@
     x_right = jnp.where(gx < lax.axis_size("gx") - 1, one, zero)
     y_left = jnp.where(gy > 0, one, zero)
     y_right = jnp.where(gy < lax.axis_size("gy") - 1, one, zero)
-    device = gx * lax.axis_size("gy") + gy
 
     scale = [scales_ref[k] for k in range(4)]
     factor = {8: jnp.where(sub % 8 == 0, scale[3], scale[2])}
@@ -284,7 +342,9 @@
         for x in range(0, rows, 8):
             store(x, lift(c[x], 4))
 
-    buffer[...] = jnp.zeros_like(buffer)
+    copy = pltpu.make_async_copy(coefficients_ref, coefficients_hbm_ref, sem)
+    copy.start()
+    packed_ref[...] = jnp.zeros_like(packed_ref)
     flags = flags_ref[...]
     source = lax.broadcasted_iota(jnp.int32, (per_row, per_row), 0)
     target = lax.broadcasted_iota(jnp.int32, (per_row, per_row), 1)
@@ -293,13 +353,12 @@
     earlier = jnp.where(source < target, one, zero).astype(jnp.bfloat16)
     place = jnp.dot(flags.astype(jnp.bfloat16), earlier, preferred_element_type=jnp.float32)
     ranks[...] = jnp.where(flags > 0, place.astype(jnp.int32), -per_row)
-
-    start = lax.fori_loop(0, device, lambda s, total: total + counts_ref[s], jnp.int32(0))
     span = per_row + SUB
 
-    def pack(x, start):
-        at = start % slots
-        base = pl.multiple_of(at // SUB * SUB, SUB)
+    @pl.loop(0, rows)
+    def _(x):
+        at = starts_ref[x, 0]
+        base = pl.multiple_of(lax.shift_left(lax.shift_right_logical(at, 3), 3), SUB)
         wanted = ranks[pl.ds(x, 1), :] + (at - base)
         row_id = lax.broadcasted_iota(jnp.int32, (span, per_row), 0)
         onehot = jnp.where(row_id == wanted, one, zero).astype(jnp.bfloat16)
@@ -311,63 +370,98 @@
         both = jnp.dot(
             onehot, jnp.concatenate([high, low], axis=1), preferred_element_type=jnp.float32
         )
-        buffer[pl.ds(base, span), :] += both[:, :LANES] + both[:, LANES:]
-        return start + row_counts_ref[x]
-
-    lax.fori_loop(0, rows, pack, start)
-    packed_ref[span:, :] = buffer[span:slots, :]
-    packed_ref[:span, :] = buffer[:span, :] + buffer[slots:, :]
-
-
-def main(counts, row_counts, scales, snapshot, left, right, before, after, flags):
+        both = both[:, :LANES] + both[:, LANES:]
+        packed_ref[pl.ds(base, SUB), :] += both[:SUB]
+        packed_ref[pl.ds(pl.multiple_of(base + SUB, SUB), per_row), :] = both[SUB:]
+
+    packed_ref[slots : slots + TURN, :] = packed_ref[:TURN, :]
+    copy.wait()
+
+
+def main(starts, scales, snapshot, left, right, before, after, flags):
     rows, cols, depth = snapshot.shape
     per_row = flags.shape[1]
     slots = rows * per_row
     return pl.pallas_call(
         main_kernel,
-        in_specs=[SMEM] * 3 + [VMEM] * 6,
-        out_specs=[VMEM] * 2,
+        in_specs=[SMEM] * 2 + [VMEM] * 6,
+        out_specs=[pl.BlockSpec(memory_space=pltpu.HBM), VMEM],
         out_shape=[
             jax.ShapeDtypeStruct(snapshot.shape, jnp.float32),
-            jax.ShapeDtypeStruct((slots, LANES), jnp.float32),
+            jax.ShapeDtypeStruct((slots + per_row + SUB, LANES), jnp.float32),
         ],
         scratch_shapes=[
-            pltpu.VMEM((slots + per_row + SUB, LANES), jnp.float32),
+            pltpu.VMEM(snapshot.shape, jnp.float32),
             pltpu.VMEM((rows, per_row), jnp.int32),
+            pltpu.SemaphoreType.DMA,
         ],
         compiler_params=PARAMS,
+        cost_estimate=pl.CostEstimate(
+            flops=2 * 10**9, bytes_accessed=16 * 2**20, transcendentals=0
+        ),
         name="lift_and_pack",
-    )(counts, row_counts, scales, snapshot, left, right, before, after, flags)
-
-
-def merge_kernel(counts_ref, arrived_ref, merged_ref, buffer):
+    )(starts, scales, snapshot, left, right, before, after, flags)
+
+
+def turn_kernel(counts_ref, packed_ref, turned_ref):
+    slots = turned_ref.shape[0]
+    device = lax.axis_index("gx") * lax.axis_size("gy") + lax.axis_index("gy")
+    counts = counts_ref[...]
+    row_id = lax.broadcasted_iota(jnp.int32, counts.shape, 0)
+    earlier = jnp.where(row_id < device, counts, 0)
+    offset = jnp.sum(earlier, axis=0, keepdims=True)[0, 0]
+
+    def one(block, carry):
+        start = (block * TURN - offset) & (slots - 1)
+        to = pl.ds(pl.multiple_of(block * TURN, TURN), TURN)
+        turned_ref[to, :] = packed_ref[pl.ds(start, TURN), :]
+        return carry
+
+    lax.fori_loop(0, slots // TURN, one, 0, unroll=4)
+
+
+def turn(counts, packed, slots):
+    return pl.pallas_call(
+        turn_kernel,
+        in_specs=[VMEM] * 2,
+        out_specs=VMEM,
+        out_shape=jax.ShapeDtypeStruct((slots, LANES), jnp.float32),
+        compiler_params=PARAMS,
+        name="turn",
+    )(counts, packed)
+
+
+def merge_kernel(counts_ref, arrived_ref, merged_ref):
     devices, share, _ = arrived_ref.shape
     slots = devices * share
+    shift = slots.bit_length() - 1
     device = lax.axis_index("gx") * lax.axis_size("gy") + lax.axis_index("gy")
-    buffer[...] = jnp.zeros_like(buffer)
-    row_id = lax.broadcasted_iota(jnp.int32, (share, LANES), 0)
-
-    def one(s, start):
-        block = start // slots
-        first = start % slots - device * share
+    merged_ref[...] = jnp.zeros_like(merged_ref)
+    row_id = lax.broadcasted_iota(jnp.int32, (share, LANES), 0) + device * share
+
+    def one(s, carry):
+        start, held = carry
+        end = start + counts_ref[s]
+        block = lax.shift_right_logical(start, shift)
         rows = arrived_ref[s]
-        here = row_id >= first
-        buffer[block] += jnp.where(here, rows, 0.0)
-        buffer[block + 1] += jnp.where(here, 0.0, rows)
-        return start + counts_ref[s]
-
-    lax.fori_loop(0, devices, one, jnp.int32(0))
-    merged_ref[...] = buffer[:devices]
+        here = row_id >= (start & (slots - 1))
+        held = held + jnp.where(here, rows, 0.0)
+        following = jnp.where(here, 0.0, rows)
+        merged_ref[jnp.minimum(block + 1, devices - 1)] = following
+        merged_ref[block] = held
+        crossed = lax.shift_right_logical(end, shift) > block
+        return end, jnp.where(crossed, following, held)
+
+    empty = jnp.zeros((share, LANES), jnp.float32)
+    lax.fori_loop(0, devices, one, (jnp.int32(0), empty), unroll=4)
 
 
 def merge(counts, arrived):
-    devices, share, _ = arrived.shape
     return pl.pallas_call(
         merge_kernel,
         in_specs=[SMEM, VMEM],
         out_specs=VMEM,
         out_shape=jax.ShapeDtypeStruct(arrived.shape, jnp.float32),
-        scratch_shapes=[pltpu.VMEM((devices + 2, share, LANES), jnp.float32)],
         compiler_params=PARAMS,
         name="merge",
     )(counts, arrived)
@@ -378,23 +472,22 @@
     width = keep_mask.shape[2]
     devices = lax.axis_size("gx") * lax.axis_size("gy")
     slots = rows * cols * width
-    to_before, to_after = y_edges(snapshot)
+    mask = keep_mask.transpose(0, 2, 1)
+    to_before, to_after, own_counts, starts = y_edges(snapshot, mask, devices)
     right = shifted(to_before, "gy", -1)
     left = shifted(to_after, "gy", 1)
-    row_counts = jnp.sum(keep_mask, axis=(1, 2))
-    own = jnp.sum(row_counts)
-    counts = lax.all_to_all(jnp.full((devices,), own, jnp.int32), ALL, 0, 0, tiled=True)
-    flags = keep_mask.transpose(0, 2, 1).reshape(rows, cols * width)
+    counts = lax.all_to_all(own_counts.reshape(devices, 1, LANES), ALL, 0, 0, tiled=True)
+    counts = counts.reshape(devices, LANES)
+    flags = mask.reshape(rows, cols * width)
     scales = jnp.exp2(exponents.astype(jnp.float32))
     x_before, x_after = x_edges(snapshot, left, right)
     after = shifted(x_before, "gx", -1)
     before = shifted(x_after, "gx", 1)
-    coefficients, packed = main(
-        counts, row_counts, scales, snapshot, left, right, before, after, flags
-    )
+    coefficients, packed = main(starts, scales, snapshot, left, right, before, after, flags)
+    turned = turn(counts, packed, slots)
     share = slots // devices
-    arrived = lax.all_to_all(packed.reshape(devices, share, LANES), ALL, 0, 0, tiled=True)
-    merged = merge(counts, arrived)
+    arrived = lax.all_to_all(turned.reshape(devices, share, LANES), ALL, 0, 0, tiled=True)
+    merged = merge(counts[:, 0], arrived)
     stream = lax.all_to_all(merged, ALL, 0, 0, tiled=True).reshape(slots, LANES)
     return coefficients, stream
 

time: 127 us -> 122 us (0.961)
  blocking collectives: 69.3 us -> 34.2 us
  waiting for transfers between devices: 14 us -> 36 us
  starting transfers between devices: 22.7 us -> 31.2 us
  other arithmetic: 3.33 us -> 0.01 us
  local copies, waits for them, and re-layouts: 4.29 us -> 6.87 us
    all_to_all x1 -> x0, blocking collectives: 35.2 us -> none  [on_device(): lax.all_to_all(packed.reshape(devices, share, LANES), ALL, 0, 0, tiled=True)]
    all_to_all x1 -> x2, waiting for transfers between devices: 9.56 us -> 32 us  [the longest x1 30.7 us: on_device(): lax.all_to_all(turned.reshape(devices, share, LANES), ALL, 0, 0, tiled=True)]
    all_to_all x1 -> x2, starting transfers between devices: 10.2 us -> 18.7 us  [the longest x1 10.3 us: on_device(): lax.all_to_all(own_counts.reshape(devices, 1, LANES), ALL, 0, 0, tiled=True)]
    unnamed x9 -> x15, local copies, waits for them, and re-layouts: 2.92 us -> 6.68 us
    all_to_all x1 -> x0, other arithmetic: 2.35 us -> none  [on_device(): lax.all_to_all(jnp.full((devices,), own, jnp.int32), ALL, 0, 0, tiled=True)]
    broadcast_in_dim x1 -> x0, local copies, waits for them, and re-layouts: 1.27 us -> none  [on_device(): jnp.full((devices,), own, jnp.int32)]
    pallas_call x3 -> x5, Pallas kernels: 9.55 us -> 10.5 us  [the longest x1 6.82 us: main(): pl.pallas_call(main_kernel, in_specs=[SMEM] * 2 + [VMEM] * 6, out_specs=[...]
  transfers between devices with their start and end apart: 5 -> 6, of which waited for: 3 -> 4; matrix products, arithmetic and copies ran while one was open for 4% -> 0% of each run, Pallas kernels for 0% -> 6%
where the time goes in v2:
time: 122 us; the launch traced here: 121 us
  waiting for transfers between devices  36 us (30%)
  blocking collectives  34.2 us (28%)
  starting transfers between devices  31.2 us (26%)
  Pallas kernels  11.9 us (10%)
  local copies, waits for them, and re-layouts  6.87 us (6%)
    all_to_all x1, blocking collectives, on_device(): stream = lax.all_to_all(merged, ALL, 0, 0, tiled=True).reshape(slots, LANES)  34.2 us
    all_to_all x1, waiting for transfers between devices, on_device(): lax.all_to_all(turned.reshape(devices, share, LANES), ALL, 0, 0, tiled=True)  30.7 us
    ppermute x4, starting transfers between devices, shifted(): lax.ppermute(value, axis, [(source, source + steps) for source in range(l...  12.5 us
    all_to_all x1, starting transfers between devices, on_device(): lax.all_to_all(own_counts.reshape(devices, 1, LANES), ALL, 0, 0, tiled=True)  10.3 us
    all_to_all x1, starting transfers between devices, on_device(): lax.all_to_all(turned.reshape(devices, share, LANES), ALL, 0, 0, tiled=True)  8.49 us
    pallas_call x1, Pallas kernels, main(): pl.pallas_call(main_kernel, in_specs=[SMEM] * 2 + [VMEM] * 6, out_specs=[...  6.82 us
    unnamed x15, local copies, waits for them, and re-layouts  6.68 us
    ppermute x4, waiting for transfers between devices, shifted(): lax.ppermute(value, axis, [(source, source + steps) for source in range(l...  4.05 us
  transfers between devices with their start and end apart: 6, of which 4 were waited for; matrix products, arithmetic and copies ran while one was open for 0% of the time, Pallas kernels for 6%

profile of v2, /device:TPU:1, one launch (start us, length us, event | category | flops | bytes accessed | tf_op | source)
XLA Modules:
  0.0 121.0 jit_solution(12066709484339252947)
XLA Ops:
  0.6 0.0 copy-start
  0.6 1.6 %copy-done = f32[16,64,512]{2,1,0:T(8,128)S(1)} copy-done((f32[16,64,512]{2,1,0:T(8,128)S(1)}, f32[16,64,512]{2,1,0:T(8,128)}, u32[]{:S(2)}) %copy-start) | copy-done | bytes 2097176
  2.2 0.0 copy-start.4
  2.2 0.8 copy-done.4
  3.0 1.6 %y_edges.1 = (f32[8,8,512]{2,1,0:T(8,128)S(1)}, f32[8,8,512]{2,1,0:T(8,128)S(1)}, s32[128,128]{1,0:T(8,128)}, s32[16,128]{1,0:T(8,128)S(1)}) custom-call(f32[16,64,512]{2,1,0:T(8,128)S(1)} %copy-done, s32[16,4,64]{2,1,0:T(4,128)S(1)} %bitcast.9), custom_call_target="tpu_custom_call" | custom-call | tf_op jit(solution)/shard_map/y_edges/pallas_call | solution.py:165
  4.6 0.0 copy-start.5
  4.7 0.0 copy-start.6
  4.7 0.0 copy-start.1
  4.7 4.1 %collective-permute-start = (f32[8,8,512]{2,1,0:T(8,128)S(1)}, f32[8,8,512]{2,1,0:T(8,128)S(1)}, u32[]{:S(2)}, u32[]{:S(2)}) collective-permute-start(f32[8,8,512]{2,1,0:T(8,128)S(1)} %get-tuple-element.13), channel_id=1, source_target_pairs={{0,1},{1,2},{2,3},{4,5},{5,6},{6,7},{8,9},{9,10},{10,11},{12,13},{... | collective-permute-start | bytes 393224 | tf_op jit(solution)/shard_map/ppermute | solution.py:20
  8.8 1.3 %collective-permute-start.1 = (f32[8,8,512]{2,1,0:T(8,128)S(1)}, f32[8,8,512]{2,1,0:T(8,128)S(1)}, u32[]{:S(2)}, u32[]{:S(2)}) collective-permute-start(f32[8,8,512]{2,1,0:T(8,128)S(1)} %get-tuple-element.14), channel_id=1, source_target_pairs={{1,0},{2,1},{3,2},{5,4},{6,5},{7,6},{9,8},{10,9},{11,10},{13,12},{... | collective-permute-start | bytes 393224 | tf_op jit(solution)/shard_map/ppermute | solution.py:20
  10.1 0.4 x_edges_inner.1
  10.4 0.5 collective-permute-done.left_ref
  10.9 3.6 %collective-permute-done.1.right_ref = f32[8,8,512]{2,1,0:T(8,128)S(1)} collective-permute-done((f32[8,8,512]{2,1,0:T(8,128)S(1)}, f32[8,8,512]{2,1,0:T(8,128)S(1)}, u32[]{:S(2)}, u32[]{:S(2)}) %collective-permute-start.1) | collective-permute-done | bytes 131104 | tf_op jit(solution)/shard_map/ppermute | solution.py:20
  14.5 0.1 x_edges_halo.1
  14.6 5.2 %collective-permute-start.2 = (f32[3,80,512]{2,1,0:T(8,128)S(1)}, f32[3,80,512]{2,1,0:T(8,128)}, u32[]{:S(2)}, u32[]{:S(2)}) collective-permute-start(f32[3,80,512]{2,1,0:T(8,128)S(1)} %get-tuple-element.17), channel_id=1, source_target_pairs={{0,4},{4,8},{8,12},{12,16},{16,20},{20,24},{24,28},{28,32},{32,36}... | collective-permute-start | bytes 1474568 | tf_op jit(solution)/shard_map/ppermute | solution.py:20
  19.8 1.9 %collective-permute-start.3 = (f32[3,80,512]{2,1,0:T(8,128)S(1)}, f32[3,80,512]{2,1,0:T(8,128)}, u32[]{:S(2)}, u32[]{:S(2)}) collective-permute-start(f32[3,80,512]{2,1,0:T(8,128)S(1)} %get-tuple-element.18), channel_id=1, source_target_pairs={{4,0},{8,4},{12,8},{16,12},{20,16},{24,20},{28,24},{32,28},{36,32}... | collective-permute-start | bytes 1474568 | tf_op jit(solution)/shard_map/ppermute | solution.py:20
  21.8 10.3 %all-to-all-start = ((s32[128,1,128]{2,1,0:T(1,128)}), s32[128,1,128]{2,1,0:T(1,128)S(1)}, u32[]{:S(2)}, u32[]{:S(2)}) async-start(s32[128,1,128]{2,1,0:T(1,128)} %bitcast.2), calls=%async_computation | async-start | bytes 131072 | tf_op jit(solution)/shard_map/all_to_all | solution.py:479
  32.0 0.0 copy-done.5
  32.0 0.1 reshape.19.flags_ref
  32.1 0.0 copy-done.6
  32.1 0.0 collective-permute-done.2.before_ref
  32.1 0.0 collective-permute-done.3.after_ref
  32.1 0.0 copy-done.1
  32.1 6.8 %lift_and_pack.1 = (f32[16,64,512]{2,1,0:T(8,128)}, f32[4360,128]{1,0:T(8,128)S(1)}) custom-call(s32[16,128]{1,0:T(8,128)S(1)} %get-tuple-element.12.starts_ref, f32[4]{0:T(128)S(1)} %multiply_exponential_fusion.scales_ref, f32[16,64,512]{2,1,0:T(8,128)S(1)} %copy-done.1, f32[8,8,512]{2,1,0:T(8,128)S(1)} %collective-permute-done.left_ref, ...), custom_call_target="tpu_custom_call" | custom-call | flops 2000000000 | bytes 16777216 | tf_op jit(solution)/shard_map/lift_and_pack/pallas_call | solution.py:385
  39.0 0.0 copy-start.2
  39.0 1.4 %copy-done.2 = f32[4360,128]{1,0:T(8,128)} copy-done((f32[4360,128]{1,0:T(8,128)}, f32[4360,128]{1,0:T(8,128)S(1)}, u32[]{:S(2)}) %copy-start.2) | copy-done | bytes 2232344
  40.4 1.3 %all-to-all-done = s32[128,1,128]{2,1,0:T(1,128)S(1)} async-done(((s32[128,1,128]{2,1,0:T(1,128)}), s32[128,1,128]{2,1,0:T(1,128)S(1)}, u32[]{:S(2)}, u32[]{:S(2)}) %all-to-all-start) | async-done | bytes 65568 | tf_op jit(solution)/shard_map/all_to_all | solution.py:479
  41.6 0.0 copy-start.3
  41.6 1.6 %copy-done.3 = f32[4360,128]{1,0:T(8,128)S(1)} copy-done((f32[4360,128]{1,0:T(8,128)S(1)}, f32[4360,128]{1,0:T(8,128)}, u32[]{:S(2)}) %copy-start.3) | copy-done | bytes 2232344
  43.3 1.6 %turn.1 = f32[4096,128]{1,0:T(8,128)} custom-call(s32[128,128]{1,0:T(8,128)S(1)} %bitcast.7, f32[4360,128]{1,0:T(8,128)S(1)} %copy-done.3), custom_call_target="tpu_custom_call" | custom-call | tf_op jit(solution)/shard_map/turn/pallas_call | solution.py:424
  44.8 8.5 %all-to-all-start.1 = ((f32[128,32,128]{2,1,0:T(8,128)}), f32[128,32,128]{2,1,0:T(8,128)S(1)}, u32[]{:S(2)}, u32[]{:S(2)}) async-start(f32[128,32,128]{2,1,0:T(8,128)} %bitcast.4), calls=%async_computation.1 | async-start | bytes 4194304 | tf_op jit(solution)/shard_map/all_to_all | solution.py:489
  53.3 0.1 slice_reduce_fusion.counts_ref
  53.4 30.7 %all-to-all-done.1.arrived_ref = f32[128,32,128]{2,1,0:T(8,128)S(1)} async-done(((f32[128,32,128]{2,1,0:T(8,128)}), f32[128,32,128]{2,1,0:T(8,128)S(1)}, u32[]{:S(2)}, u32[]{:S(2)}) %all-to-all-start.1) | async-done | bytes 2097184 | tf_op jit(solution)/shard_map/all_to_all | solution.py:489
  84.1 1.4 %merge.1 = f32[128,32,128]{2,1,0:T(8,128)S(1)} custom-call(s32[128]{0:T(128)S(1)} %slice_reduce_fusion.counts_ref, f32[128,32,128]{2,1,0:T(8,128)S(1)} %all-to-all-done.1.arrived_ref), custom_call_target="tpu_custom_call" | custom-call | tf_op jit(solution)/shard_map/merge/pallas_call | solution.py:460
  85.5 34.2 %all_to_all.15 = f32[128,32,128]{2,1,0:T(8,128)S(1)} all-to-all(f32[128,32,128]{2,1,0:T(8,128)S(1)} %merge.1), channel_id=1, replica_groups=mesh['gx'=32,'gy'=4] {'gx','gy'}, dimensions={0} | all-to-all | bytes 4194304 | tf_op jit(solution)/shard_map/all_to_all | solution.py:491
  119.7 1.3 %copy.11 = f32[4096,128]{1,0:T(8,128)} copy(f32[4096,128]{1,0:T(8,128)S(1)} %bitcast.11) | data formatting | bytes 4194304
  (1 shorter events, 0.0 us)
Async XLA Ops:
  0.6 1.6 %copy-start = (f32[16,64,512]{2,1,0:T(8,128)S(1)}, f32[16,64,512]{2,1,0:T(8,128)}, u32[]{:S(2)}) copy-start(f32[16,64,512]{2,1,0:T(8,128)} %snapshot_ref.5) | copy-start | bytes 6291460
  2.2 0.8 copy-start.4
  4.6 27.4 %copy-start.5 = (s32[16,64,4]{1,2,0:T(4,128)S(1)}, s32[16,64,4]{1,2,0:T(4,128)}, u32[]{:S(2)}) copy-start(s32[16,64,4]{1,2,0:T(4,128)} %param.4) | copy-start | bytes 49156
  4.7 27.5 %copy-start.6 = (s32[4]{0:T(128)S(1)}, s32[4]{0:T(128)}, u32[]{:S(2)}) copy-start(s32[4]{0:T(128)} %param.5) | copy-start | bytes 52
  4.7 27.5 %copy-start.1 = (f32[16,64,512]{2,1,0:T(8,128)S(1)}, f32[16,64,512]{2,1,0:T(8,128)}, u32[]{:S(2)}) copy-start(f32[16,64,512]{2,1,0:T(8,128)} %snapshot_ref.5) | copy-start | bytes 6291460
  4.7 6.2 %collective-permute-start = (f32[8,8,512]{2,1,0:T(8,128)S(1)}, f32[8,8,512]{2,1,0:T(8,128)S(1)}, u32[]{:S(2)}, u32[]{:S(2)}) collective-permute-start(f32[8,8,512]{2,1,0:T(8,128)S(1)} %get-tuple-element.13), channel_id=1, source_target_pairs={{0,1},{1,2},{2,3},{4,5},{5,6},{6,7},{8,9},{9,10},{10,11},{12,13},{... | collective-permute-start | bytes 393224 | tf_op jit(solution)/shard_map/ppermute | solution.py:20
  8.8 5.7 %collective-permute-start.1 = (f32[8,8,512]{2,1,0:T(8,128)S(1)}, f32[8,8,512]{2,1,0:T(8,128)S(1)}, u32[]{:S(2)}, u32[]{:S(2)}) collective-permute-start(f32[8,8,512]{2,1,0:T(8,128)S(1)} %get-tuple-element.14), channel_id=1, source_target_pairs={{1,0},{2,1},{3,2},{5,4},{6,5},{7,6},{9,8},{10,9},{11,10},{13,12},{... | collective-permute-start | bytes 393224 | tf_op jit(solution)/shard_map/ppermute | solution.py:20
  14.6 17.5 %collective-permute-start.2 = (f32[3,80,512]{2,1,0:T(8,128)S(1)}, f32[3,80,512]{2,1,0:T(8,128)}, u32[]{:S(2)}, u32[]{:S(2)}) collective-permute-start(f32[3,80,512]{2,1,0:T(8,128)S(1)} %get-tuple-element.17), channel_id=1, source_target_pairs={{0,4},{4,8},{8,12},{12,16},{16,20},{20,24},{24,28},{28,32},{32,36}... | collective-permute-start | bytes 1474568 | tf_op jit(solution)/shard_map/ppermute | solution.py:20
  19.8 12.3 %collective-permute-start.3 = (f32[3,80,512]{2,1,0:T(8,128)S(1)}, f32[3,80,512]{2,1,0:T(8,128)}, u32[]{:S(2)}, u32[]{:S(2)}) collective-permute-start(f32[3,80,512]{2,1,0:T(8,128)S(1)} %get-tuple-element.18), channel_id=1, source_target_pairs={{4,0},{8,4},{12,8},{16,12},{20,16},{24,20},{28,24},{32,28},{36,32}... | collective-permute-start | bytes 1474568 | tf_op jit(solution)/shard_map/ppermute | solution.py:20
  21.8 19.9 %all-to-all-start = ((s32[128,1,128]{2,1,0:T(1,128)}), s32[128,1,128]{2,1,0:T(1,128)S(1)}, u32[]{:S(2)}, u32[]{:S(2)}) async-start(s32[128,1,128]{2,1,0:T(1,128)} %bitcast.2), calls=%async_computation | async-start | bytes 131072 | tf_op jit(solution)/shard_map/all_to_all | solution.py:479
  39.0 1.4 %copy-start.2 = (f32[4360,128]{1,0:T(8,128)}, f32[4360,128]{1,0:T(8,128)S(1)}, u32[]{:S(2)}) copy-start(f32[4360,128]{1,0:T(8,128)S(1)} %get-tuple-element.21.packed_ref) | copy-start | bytes 6696964
  41.6 1.6 %copy-start.3 = (f32[4360,128]{1,0:T(8,128)S(1)}, f32[4360,128]{1,0:T(8,128)}, u32[]{:S(2)}) copy-start(f32[4360,128]{1,0:T(8,128)} %copy-done.2) | copy-start | bytes 6696964
  44.8 39.3 %all-to-all-start.1 = ((f32[128,32,128]{2,1,0:T(8,128)}), f32[128,32,128]{2,1,0:T(8,128)S(1)}, u32[]{:S(2)}, u32[]{:S(2)}) async-start(f32[128,32,128]{2,1,0:T(8,128)} %bitcast.4), calls=%async_computation.1 | async-start | bytes 4194304 | tf_op jit(solution)/shard_map/all_to_all | solution.py:489

commit v3 on v2

--- a/solution.py
+++ b/solution.py
@@ -8,7 +8,7 @@
 ALL = ("gx", "gy")
 SUB = 8
 LANES = 128
-TURN = 64
+PACK_LIMIT = 50 * 2**20
 VMEM = pl.BlockSpec(memory_space=pltpu.VMEM)
 SMEM = pl.BlockSpec(memory_space=pltpu.SMEM)
 PARAMS = pltpu.CompilerParams(vmem_limit_bytes=16 * 2**20)
@@ -86,28 +86,8 @@
     return first, second, third
 
 
-def y_edges_kernel(
-    snapshot_ref,
-    mask_ref,
-    to_before_ref,
-    to_after_ref,
-    counts_ref,
-    starts_ref,
-    head_ref,
-    tail_ref,
-    sems,
-):
-    rows, cols, depth = snapshot_ref.shape
-    half = rows // 2
-    copies = [
-        pltpu.make_async_copy(snapshot_ref.at[:, :SUB, :], head_ref, sems.at[0]),
-        pltpu.make_async_copy(snapshot_ref.at[:, cols - 2 * SUB :, :], tail_ref, sems.at[1]),
-    ]
-    for copy in copies:
-        copy.start()
-    sub = sublane()
-    zero = jnp.zeros((SUB, LANES), jnp.float32)
-
+def count_kept(mask_ref, counts_ref, starts_ref):
+    rows = mask_ref.shape[0]
     kept = mask_ref[:, 0, :]
     for t in range(1, mask_ref.shape[1]):
         kept = kept + mask_ref[:, t, :]
@@ -121,8 +101,15 @@
     total = (starts[rows - 1 :, :] + kept[rows - 1 :, :]).astype(jnp.int32)
     counts_ref[...] = jnp.broadcast_to(total, counts_ref.shape)
 
+
+def y_edges_kernel(snapshot_ref, to_before_ref, to_after_ref):
+    rows, cols, depth = snapshot_ref.shape
+    half = rows // 2
+    sub = sublane()
+    zero = jnp.zeros((SUB, LANES), jnp.float32)
+
     def before(x, lanes):
-        v = head_ref[x, :, lanes]
+        v = snapshot_ref[x, :SUB, lanes]
         d1 = v - weight(0.5, sub % 2 == 1) * (rolled(v, -1) + rolled(v, 1))
         c2 = d1 + 0.25 * (rolled(d1, -1) + rolled(d1, 1))
         second = rolled(v, 1) + 0.25 * d1
@@ -132,7 +119,8 @@
         )
 
     def after(x, lanes):
-        v = [zero, tail_ref[x, :SUB, lanes], tail_ref[x, SUB:, lanes], zero]
+        last = [snapshot_ref[x, cols - n * SUB : cols - (n - 1) * SUB, lanes] for n in (2, 1)]
+        v = [zero] + last + [zero]
         odd = weight(0.5, sub % 2 == 1)
         d = [zero] + [t - odd * n for t, n in zip(v[1:-1], neighbours(v, 1, sub))] + [zero]
         even = weight(0.25, sub % 2 == 0)
@@ -148,9 +136,6 @@
             sub == 7, first, jnp.where(sub == 6, second, jnp.where(sub == 4, third, 0.0))
         )
 
-    for copy in copies:
-        copy.wait()
-
     @pl.loop(0, half)
     def _(x):
         for t in range(depth // LANES):
@@ -159,27 +144,17 @@
             to_after_ref[x, :, lanes] = after(x, lanes) + rolled(after(x + half, lanes), 4)
 
 
-def y_edges(snapshot, mask, devices):
+def y_edges(snapshot):
     rows, cols, depth = snapshot.shape
     shape = jax.ShapeDtypeStruct((rows // 2, SUB, depth), jnp.float32)
     return pl.pallas_call(
         y_edges_kernel,
-        in_specs=[pl.BlockSpec(memory_space=pltpu.HBM), VMEM],
-        out_specs=[VMEM] * 4,
-        out_shape=[
-            shape,
-            shape,
-            jax.ShapeDtypeStruct((devices, LANES), jnp.int32),
-            jax.ShapeDtypeStruct((rows, LANES), jnp.int32),
-        ],
-        scratch_shapes=[
-            pltpu.VMEM((rows, SUB, depth), jnp.float32),
-            pltpu.VMEM((rows, 2 * SUB, depth), jnp.float32),
-            pltpu.SemaphoreType.DMA((2,)),
-        ],
+        in_specs=[VMEM],
+        out_specs=[VMEM] * 2,
+        out_shape=[shape] * 2,
         compiler_params=PARAMS,
         name="y_edges",
-    )(snapshot, mask)
+    )(snapshot)
 
 
 def row_of(snapshot_ref, left_ref, right_ref, x, lanes, sub):
@@ -195,8 +170,11 @@
     return [left] + inner + [right]
 
 
-def x_edges_inner_kernel(snapshot_ref, to_before_ref, to_after_ref):
+def x_edges_inner_kernel(
+    snapshot_ref, mask_ref, to_before_ref, to_after_ref, counts_ref, starts_ref
+):
     rows, cols, depth = snapshot_ref.shape
+    count_kept(mask_ref, counts_ref, starts_ref)
 
     @pl.loop(0, cols // SUB)
     def _(k):
@@ -231,17 +209,26 @@
                 to_after_ref[level, place : place + SUB, lanes] = b[0]
 
 
-def x_edges(snapshot, left, right):
+def x_edges_inner(snapshot, mask, devices):
     rows, cols, depth = snapshot.shape
     shape = jax.ShapeDtypeStruct((3, cols + 2 * SUB, depth), jnp.float32)
-    before, after = pl.pallas_call(
+    return pl.pallas_call(
         x_edges_inner_kernel,
-        in_specs=[VMEM],
-        out_specs=[VMEM] * 2,
-        out_shape=[shape] * 2,
+        in_specs=[VMEM] * 2,
+        out_specs=[VMEM] * 4,
+        out_shape=[
+            shape,
+            shape,
+            jax.ShapeDtypeStruct((devices, LANES), jnp.int32),
+            jax.ShapeDtypeStruct((rows, LANES), jnp.int32),
+        ],
         compiler_params=PARAMS,
         name="x_edges_inner",
-    )(snapshot)
+    )(snapshot, mask)
+
+
+def x_edges_halo(left, right, before, after):
+    shape = jax.ShapeDtypeStruct(before.shape, jnp.float32)
     return pl.pallas_call(
         x_edges_halo_kernel,
         in_specs=[VMEM] * 4,
@@ -253,26 +240,20 @@
     )(left, right, before, after)
 
 
-def main_kernel(
-    starts_ref,
+def lift_kernel(
     scales_ref,
     snapshot_ref,
     left_ref,
     right_ref,
     before_ref,
     after_ref,
-    flags_ref,
     coefficients_hbm_ref,
-    packed_ref,
     coefficients_ref,
-    ranks,
-    sem,
+    sems,
 ):
     rows, cols, depth = snapshot_ref.shape
     width = depth // LANES
-    slots = rows * cols * width
     count = cols // SUB
-    per_row = cols * width
     sub = sublane()
     gx, gy = lax.axis_index("gx"), lax.axis_index("gy")
     one, zero = jnp.float32(1.0), jnp.float32(0.0)
@@ -290,6 +271,12 @@
     factor[1] = jnp.where(sub % 2 == 0, scale[0], scale[0])
     factor[8] = jnp.where(sub % 2 == 0, factor[8], scale[0])
     factor[4] = jnp.where(sub % 2 == 0, factor[4], scale[0])
+
+    def write(t):
+        lanes = pl.ds(pl.multiple_of(t * LANES, LANES), LANES)
+        return pltpu.make_async_copy(
+            coefficients_ref.at[:, :, lanes], coefficients_hbm_ref.at[:, :, lanes], sems.at[t]
+        )
 
     @pl.loop(0, width)
     def _(t):
@@ -341,10 +328,66 @@
             store(x, c[x])
         for x in range(0, rows, 8):
             store(x, lift(c[x], 4))
-
-    copy = pltpu.make_async_copy(coefficients_ref, coefficients_hbm_ref, sem)
-    copy.start()
-    packed_ref[...] = jnp.zeros_like(packed_ref)
+        write(t).start()
+
+    @pl.loop(0, width)
+    def _(t):
+        write(t).wait()
+
+
+def lift(scales, snapshot, left, right, before, after):
+    return pl.pallas_call(
+        lift_kernel,
+        in_specs=[SMEM] + [VMEM] * 5,
+        out_specs=pl.BlockSpec(memory_space=pltpu.HBM),
+        out_shape=jax.ShapeDtypeStruct(snapshot.shape, jnp.float32),
+        scratch_shapes=[
+            pltpu.VMEM(snapshot.shape, jnp.float32),
+            pltpu.SemaphoreType.DMA((snapshot.shape[2] // LANES,)),
+        ],
+        compiler_params=PARAMS,
+        cost_estimate=pl.CostEstimate(
+            flops=2 * 10**9, bytes_accessed=16 * 2**20, transcendentals=0
+        ),
+        name="lift",
+    )(scales, snapshot, left, right, before, after)
+
+
+def pack_kernel(
+    table_ref,
+    starts_ref,
+    coefficients_hbm_ref,
+    flags_ref,
+    packed_ref,
+    counts_ref,
+    coefficients_ref,
+    buffer,
+    ranks,
+    sems,
+):
+    rows, cols, depth = coefficients_ref.shape
+    width = depth // LANES
+    slots = rows * cols * width
+    per_row = cols * width
+    one, zero = jnp.float32(1.0), jnp.float32(0.0)
+    group = rows // sems.shape[0]
+
+    def read(part):
+        part = pl.ds(part * group, group)
+        return pltpu.make_async_copy(
+            coefficients_hbm_ref.at[part], coefficients_ref.at[part], sems.at[part.start // group]
+        )
+
+    for part in range(rows // group):
+        read(part).start()
+
+    device = lax.axis_index("gx") * lax.axis_size("gy") + lax.axis_index("gy")
+    table = table_ref[...]
+    row_id = lax.broadcasted_iota(jnp.int32, table.shape, 0)
+    lane_id = lax.broadcasted_iota(jnp.int32, table.shape, 1)
+    offset = jnp.sum(jnp.where(row_id < device, table, 0), axis=0, keepdims=True)[0, 0]
+    counts_ref[...] = jnp.sum(jnp.where(row_id == lane_id, table, 0), axis=0, keepdims=True)
+    buffer[...] = jnp.zeros_like(buffer)
     flags = flags_ref[...]
     source = lax.broadcasted_iota(jnp.int32, (per_row, per_row), 0)
     target = lax.broadcasted_iota(jnp.int32, (per_row, per_row), 1)
@@ -355,11 +398,10 @@
     ranks[...] = jnp.where(flags > 0, place.astype(jnp.int32), -per_row)
     span = per_row + SUB
 
-    @pl.loop(0, rows)
-    def _(x):
-        at = starts_ref[x, 0]
+    def place_row(x):
+        at = (offset + starts_ref[x, 0]) & (slots - 1)
         base = pl.multiple_of(lax.shift_left(lax.shift_right_logical(at, 3), 3), SUB)
-        wanted = ranks[pl.ds(x, 1), :] + (at - base)
+        wanted = ranks[x : x + 1, :] + (at - base)
         row_id = lax.broadcasted_iota(jnp.int32, (span, per_row), 0)
         onehot = jnp.where(row_id == wanted, one, zero).astype(jnp.bfloat16)
         values = jnp.concatenate(
@@ -370,65 +412,38 @@
         both = jnp.dot(
             onehot, jnp.concatenate([high, low], axis=1), preferred_element_type=jnp.float32
         )
-        both = both[:, :LANES] + both[:, LANES:]
-        packed_ref[pl.ds(base, SUB), :] += both[:SUB]
-        packed_ref[pl.ds(pl.multiple_of(base + SUB, SUB), per_row), :] = both[SUB:]
-
-    packed_ref[slots : slots + TURN, :] = packed_ref[:TURN, :]
-    copy.wait()
-
-
-def main(starts, scales, snapshot, left, right, before, after, flags):
-    rows, cols, depth = snapshot.shape
+        buffer[pl.ds(base, span), :] += both[:, :LANES] + both[:, LANES:]
+
+    for part in range(rows // group):
+        read(part).wait()
+        for x in range(part * group, part * group + group):
+            place_row(x)
+
+    packed_ref[span:, :] = buffer[span:slots, :]
+    packed_ref[:span, :] = buffer[:span, :] + buffer[slots:, :]
+
+
+def pack(table, starts, coefficients, flags):
+    rows, cols, depth = coefficients.shape
     per_row = flags.shape[1]
     slots = rows * per_row
     return pl.pallas_call(
-        main_kernel,
-        in_specs=[SMEM] * 2 + [VMEM] * 6,
-        out_specs=[pl.BlockSpec(memory_space=pltpu.HBM), VMEM],
+        pack_kernel,
+        in_specs=[VMEM, SMEM, pl.BlockSpec(memory_space=pltpu.HBM), VMEM],
+        out_specs=[VMEM] * 2,
         out_shape=[
-            jax.ShapeDtypeStruct(snapshot.shape, jnp.float32),
-            jax.ShapeDtypeStruct((slots + per_row + SUB, LANES), jnp.float32),
+            jax.ShapeDtypeStruct((slots, LANES), jnp.float32),
+            jax.ShapeDtypeStruct((1, table.shape[0]), jnp.int32),
         ],
         scratch_shapes=[
-            pltpu.VMEM(snapshot.shape, jnp.float32),
+            pltpu.VMEM(coefficients.shape, jnp.float32),
+            pltpu.VMEM((slots + per_row + SUB, LANES), jnp.float32),
             pltpu.VMEM((rows, per_row), jnp.int32),
-            pltpu.SemaphoreType.DMA,
+            pltpu.SemaphoreType.DMA((4,)),
         ],
-        compiler_params=PARAMS,
-        cost_estimate=pl.CostEstimate(
-            flops=2 * 10**9, bytes_accessed=16 * 2**20, transcendentals=0
-        ),
-        name="lift_and_pack",
-    )(starts, scales, snapshot, left, right, before, after, flags)
-
-
-def turn_kernel(counts_ref, packed_ref, turned_ref):
-    slots = turned_ref.shape[0]
-    device = lax.axis_index("gx") * lax.axis_size("gy") + lax.axis_index("gy")
-    counts = counts_ref[...]
-    row_id = lax.broadcasted_iota(jnp.int32, counts.shape, 0)
-    earlier = jnp.where(row_id < device, counts, 0)
-    offset = jnp.sum(earlier, axis=0, keepdims=True)[0, 0]
-
-    def one(block, carry):
-        start = (block * TURN - offset) & (slots - 1)
-        to = pl.ds(pl.multiple_of(block * TURN, TURN), TURN)
-        turned_ref[to, :] = packed_ref[pl.ds(start, TURN), :]
-        return carry
-
-    lax.fori_loop(0, slots // TURN, one, 0, unroll=4)
-
-
-def turn(counts, packed, slots):
-    return pl.pallas_call(
-        turn_kernel,
-        in_specs=[VMEM] * 2,
-        out_specs=VMEM,
-        out_shape=jax.ShapeDtypeStruct((slots, LANES), jnp.float32),
-        compiler_params=PARAMS,
-        name="turn",
-    )(counts, packed)
+        compiler_params=pltpu.CompilerParams(vmem_limit_bytes=PACK_LIMIT),
+        name="pack",
+    )(table, starts, coefficients, flags)
 
 
 def merge_kernel(counts_ref, arrived_ref, merged_ref):
@@ -441,7 +456,7 @@
 
     def one(s, carry):
         start, held = carry
-        end = start + counts_ref[s]
+        end = start + counts_ref[0, s]
         block = lax.shift_right_logical(start, shift)
         rows = arrived_ref[s]
         here = row_id >= (start & (slots - 1))
@@ -473,21 +488,22 @@
     devices = lax.axis_size("gx") * lax.axis_size("gy")
     slots = rows * cols * width
     mask = keep_mask.transpose(0, 2, 1)
-    to_before, to_after, own_counts, starts = y_edges(snapshot, mask, devices)
+    to_before, to_after = y_edges(snapshot)
     right = shifted(to_before, "gy", -1)
     left = shifted(to_after, "gy", 1)
-    counts = lax.all_to_all(own_counts.reshape(devices, 1, LANES), ALL, 0, 0, tiled=True)
-    counts = counts.reshape(devices, LANES)
+    x_before, x_after, own_counts, starts = x_edges_inner(snapshot, mask, devices)
+    table = lax.all_to_all(own_counts.reshape(devices, 1, LANES), ALL, 0, 0, tiled=True)
+    table = table.reshape(devices, LANES)
     flags = mask.reshape(rows, cols * width)
     scales = jnp.exp2(exponents.astype(jnp.float32))
-    x_before, x_after = x_edges(snapshot, left, right)
+    x_before, x_after = x_edges_halo(left, right, x_before, x_after)
     after = shifted(x_before, "gx", -1)
     before = shifted(x_after, "gx", 1)
-    coefficients, packed = main(starts, scales, snapshot, left, right, before, after, flags)
-    turned = turn(counts, packed, slots)
+    coefficients = lift(scales, snapshot, left, right, before, after)
+    packed, counts = pack(table, starts, coefficients, flags)
     share = slots // devices
-    arrived = lax.all_to_all(turned.reshape(devices, share, LANES), ALL, 0, 0, tiled=True)
-    merged = merge(counts[:, 0], arrived)
+    arrived = lax.all_to_all(packed.reshape(devices, share, LANES), ALL, 0, 0, tiled=True)
+    merged = merge(counts, arrived)
     stream = lax.all_to_all(merged, ALL, 0, 0, tiled=True).reshape(slots, LANES)
     return coefficients, stream
 

time: 122 us -> 116 us (0.951)
  blocking collectives: 34.2 us -> 69.2 us
  waiting for transfers between devices: 36 us -> 8.59 us
  starting transfers between devices: 31.2 us -> 22.7 us
  local copies, waits for them, and re-layouts: 6.87 us -> 3.01 us
    all_to_all x0 -> x1, blocking collectives: none -> 35 us  [on_device(): lax.all_to_all(packed.reshape(devices, share, LANES), ALL, 0, 0, tiled=True)]
    all_to_all x1 -> x0, waiting for transfers between devices: 30.7 us -> none  [on_device(): lax.all_to_all(turned.reshape(devices, share, LANES), ALL, 0, 0, tiled=True)]
    all_to_all x1 -> x0, starting transfers between devices: 8.49 us -> none  [on_device(): lax.all_to_all(turned.reshape(devices, share, LANES), ALL, 0, 0, tiled=True)]
    all_to_all x1, waiting for transfers between devices: 1.27 us -> 5.36 us  [on_device(): lax.all_to_all(own_counts.reshape(devices, 1, LANES), ALL, 0, 0, tiled=True)]
    unnamed x15 -> x9, local copies, waits for them, and re-layouts: 6.68 us -> 2.92 us
  transfers between devices with their start and end apart: 6 -> 5, of which waited for: 4 -> 2; matrix products, arithmetic and copies ran while one was open for 0% -> 0% of each run, Pallas kernels for 6% -> 5%
where the time goes in v3:
time: 116 us; the launch traced here: 115 us
  blocking collectives  69.2 us (60%)
  starting transfers between devices  22.7 us (20%)
  Pallas kernels  10.9 us (9%)
  waiting for transfers between devices  8.59 us (7%)
  local copies, waits for them, and re-layouts  3.01 us (3%)
    all_to_all x1, blocking collectives, on_device(): lax.all_to_all(packed.reshape(devices, share, LANES), ALL, 0, 0, tiled=True)  35 us
    all_to_all x1, blocking collectives, on_device(): stream = lax.all_to_all(merged, ALL, 0, 0, tiled=True).reshape(slots, LANES)  34.2 us
    ppermute x4, starting transfers between devices, shifted(): lax.ppermute(value, axis, [(source, source + steps) for source in range(l...  12.5 us
    all_to_all x1, starting transfers between devices, on_device(): lax.all_to_all(own_counts.reshape(devices, 1, LANES), ALL, 0, 0, tiled=True)  10.3 us
    all_to_all x1, waiting for transfers between devices, on_device(): lax.all_to_all(own_counts.reshape(devices, 1, LANES), ALL, 0, 0, tiled=True)  5.36 us
    pallas_call x1, Pallas kernels, lift(): pl.pallas_call(lift_kernel, in_specs=[SMEM] + [VMEM] * 5, out_specs=pl.Bl...  4.12 us
    pallas_call x1, Pallas kernels, pack(): pl.pallas_call(pack_kernel, in_specs=[VMEM, SMEM, pl.BlockSpec(memory_spa...  3.26 us
    ppermute x4, waiting for transfers between devices, shifted(): lax.ppermute(value, axis, [(source, source + steps) for source in range(l...  3.23 us
  transfers between devices with their start and end apart: 5, of which 2 were waited for; matrix products, arithmetic and copies ran while one was open for 0% of the time, Pallas kernels for 5%

profile of v3, /device:TPU:1, one launch (start us, length us, event | category | flops | bytes accessed | tf_op | source)
XLA Modules:
  0.0 115.2 jit_solution(7044315884891349631)
XLA Ops:
  0.6 0.0 copy-start
  0.6 1.6 %copy-done = f32[16,64,512]{2,1,0:T(8,128)S(1)} copy-done((f32[16,64,512]{2,1,0:T(8,128)S(1)}, f32[16,64,512]{2,1,0:T(8,128)}, u32[]{:S(2)}) %copy-start) | copy-done | bytes 2097176
  2.2 0.0 copy-start.2
  2.2 0.8 y_edges.1
  3.1 0.0 copy-start.3
  3.1 0.0 copy-start.1
  3.1 4.1 %collective-permute-start = (f32[8,8,512]{2,1,0:T(8,128)S(1)}, f32[8,8,512]{2,1,0:T(8,128)S(1)}, u32[]{:S(2)}, u32[]{:S(2)}) collective-permute-start(f32[8,8,512]{2,1,0:T(8,128)S(1)} %get-tuple-element.12), channel_id=1, source_target_pairs={{0,1},{1,2},{2,3},{4,5},{5,6},{6,7},{8,9},{9,10},{10,11},{12,13},{... | collective-permute-start | bytes 393224 | tf_op jit(solution)/shard_map/ppermute | solution.py:20
  7.2 1.3 %collective-permute-start.1 = (f32[8,8,512]{2,1,0:T(8,128)S(1)}, f32[8,8,512]{2,1,0:T(8,128)S(1)}, u32[]{:S(2)}, u32[]{:S(2)}) collective-permute-start(f32[8,8,512]{2,1,0:T(8,128)S(1)} %get-tuple-element.13), channel_id=1, source_target_pairs={{1,0},{2,1},{3,2},{5,4},{6,5},{7,6},{9,8},{10,9},{11,10},{13,12},{... | collective-permute-start | bytes 393224 | tf_op jit(solution)/shard_map/ppermute | solution.py:20
  8.5 0.0 copy-done.2
  8.5 1.2 %x_edges_inner.1 = (f32[3,80,512]{2,1,0:T(8,128)S(1)}, f32[3,80,512]{2,1,0:T(8,128)S(1)}, s32[128,128]{1,0:T(8,128)}, s32[16,128]{1,0:T(8,128)S(1)}) custom-call(f32[16,64,512]{2,1,0:T(8,128)S(1)} %copy-done, s32[16,4,64]{2,1,0:T(4,128)S(1)} %bitcast.9), custom_call_target="tpu_custom_call" | custom-call | tf_op jit(solution)/shard_map/x_edges_inner/pallas_call | solution.py:215
  9.7 0.0 collective-permute-done.left_ref
  9.7 3.2 %collective-permute-done.1.right_ref = f32[8,8,512]{2,1,0:T(8,128)S(1)} collective-permute-done((f32[8,8,512]{2,1,0:T(8,128)S(1)}, f32[8,8,512]{2,1,0:T(8,128)S(1)}, u32[]{:S(2)}, u32[]{:S(2)}) %collective-permute-start.1) | collective-permute-done | bytes 131104 | tf_op jit(solution)/shard_map/ppermute | solution.py:20
  12.9 0.1 x_edges_halo.1
  13.0 5.2 %collective-permute-start.2 = (f32[3,80,512]{2,1,0:T(8,128)S(1)}, f32[3,80,512]{2,1,0:T(8,128)}, u32[]{:S(2)}, u32[]{:S(2)}) collective-permute-start(f32[3,80,512]{2,1,0:T(8,128)S(1)} %get-tuple-element.16), channel_id=1, source_target_pairs={{0,4},{4,8},{8,12},{12,16},{16,20},{20,24},{24,28},{28,32},{32,36}... | collective-permute-start | bytes 1474568 | tf_op jit(solution)/shard_map/ppermute | solution.py:20
  18.2 1.9 %collective-permute-start.3 = (f32[3,80,512]{2,1,0:T(8,128)S(1)}, f32[3,80,512]{2,1,0:T(8,128)}, u32[]{:S(2)}, u32[]{:S(2)}) collective-permute-start(f32[3,80,512]{2,1,0:T(8,128)S(1)} %get-tuple-element.17), channel_id=1, source_target_pairs={{4,0},{8,4},{12,8},{16,12},{20,16},{24,20},{28,24},{32,28},{36,32}... | collective-permute-start | bytes 1474568 | tf_op jit(solution)/shard_map/ppermute | solution.py:20
  20.2 10.3 %all-to-all-start = ((s32[128,1,128]{2,1,0:T(1,128)}), s32[128,1,128]{2,1,0:T(1,128)S(1)}, u32[]{:S(2)}, u32[]{:S(2)}) async-start(s32[128,1,128]{2,1,0:T(1,128)} %bitcast.2), calls=%async_computation | async-start | bytes 131072 | tf_op jit(solution)/shard_map/all_to_all | solution.py:495
  30.4 0.1 reshape.21.flags_ref
  30.5 0.0 copy-done.3
  30.5 0.0 collective-permute-done.2.before_ref
  30.5 0.0 collective-permute-done.3.after_ref
  30.5 0.0 copy-done.1
  30.5 4.1 %lift.1.coefficients_hbm_ref = f32[16,64,512]{2,1,0:T(8,128)} custom-call(f32[4]{0:T(128)S(1)} %multiply_exponential_fusion.scales_ref, f32[16,64,512]{2,1,0:T(8,128)S(1)} %copy-done.1, f32[8,8,512]{2,1,0:T(8,128)S(1)} %collective-permute-done.left_ref, f32[8,8,512]{2,1,0:T(8,128)S(1)} %collective-permute-done.1.right_ref, ...), custom_call_target="tpu_custom_call" | custom-call | flops 2000000000 | bytes 16777216 | tf_op jit(solution)/shard_map/lift/pallas_call | solution.py:339
  34.7 5.4 %all-to-all-done = s32[128,1,128]{2,1,0:T(1,128)S(1)} async-done(((s32[128,1,128]{2,1,0:T(1,128)}), s32[128,1,128]{2,1,0:T(1,128)S(1)}, u32[]{:S(2)}, u32[]{:S(2)}) %all-to-all-start) | async-done | bytes 65568 | tf_op jit(solution)/shard_map/all_to_all | solution.py:495
  40.0 3.3 %pack.1 = (f32[4096,128]{1,0:T(8,128)S(1)}, s32[1,128]{1,0:T(1,128)S(1)}) custom-call(s32[128,128]{1,0:T(8,128)S(1)} %bitcast.8, s32[16,128]{1,0:T(8,128)S(1)} %get-tuple-element.19.starts_ref, f32[16,64,512]{2,1,0:T(8,128)} %lift.1.coefficients_hbm_ref, s32[16,256]{1,0:T(8,128)S(1)} %reshape.21.flags_ref), custom_call_target="tpu_custom_call" | custom-call | tf_op jit(solution)/shard_map/pack/pallas_call | solution.py:430
  43.3 35.0 %all_to_all.15.arrived_ref = f32[128,32,128]{2,1,0:T(8,128)S(1)} all-to-all(f32[128,32,128]{2,1,0:T(8,128)S(1)} %bitcast.7), channel_id=1, replica_groups=mesh['gx'=32,'gy'=4] {'gx','gy'}, dimensions={0} | all-to-all | bytes 4194304 | tf_op jit(solution)/shard_map/all_to_all | solution.py:505
  78.3 1.4 %merge.1 = f32[128,32,128]{2,1,0:T(8,128)S(1)} custom-call(s32[1,128]{1,0:T(1,128)S(1)} %get-tuple-element.20.counts_ref, f32[128,32,128]{2,1,0:T(8,128)S(1)} %all_to_all.15.arrived_ref), custom_call_target="tpu_custom_call" | custom-call | tf_op jit(solution)/shard_map/merge/pallas_call | solution.py:475
  79.7 34.2 %all_to_all.16 = f32[128,32,128]{2,1,0:T(8,128)S(1)} all-to-all(f32[128,32,128]{2,1,0:T(8,128)S(1)} %merge.1), channel_id=1, replica_groups=mesh['gx'=32,'gy'=4] {'gx','gy'}, dimensions={0} | all-to-all | bytes 4194304 | tf_op jit(solution)/shard_map/all_to_all | solution.py:507
  113.9 1.3 %copy.11 = f32[4096,128]{1,0:T(8,128)} copy(f32[4096,128]{1,0:T(8,128)S(1)} %bitcast.11) | data formatting | bytes 4194304
  (1 shorter events, 0.0 us)
Async XLA Ops:
  0.6 1.6 %copy-start = (f32[16,64,512]{2,1,0:T(8,128)S(1)}, f32[16,64,512]{2,1,0:T(8,128)}, u32[]{:S(2)}) copy-start(f32[16,64,512]{2,1,0:T(8,128)} %snapshot_ref.5) | copy-start | bytes 6291460
  2.2 6.3 %copy-start.2 = (s32[16,64,4]{1,2,0:T(4,128)S(1)}, s32[16,64,4]{1,2,0:T(4,128)}, u32[]{:S(2)}) copy-start(s32[16,64,4]{1,2,0:T(4,128)} %param.4) | copy-start | bytes 49156
  3.1 27.5 %copy-start.3 = (s32[4]{0:T(128)S(1)}, s32[4]{0:T(128)}, u32[]{:S(2)}) copy-start(s32[4]{0:T(128)} %param.5) | copy-start | bytes 52
  3.1 27.5 %copy-start.1 = (f32[16,64,512]{2,1,0:T(8,128)S(1)}, f32[16,64,512]{2,1,0:T(8,128)}, u32[]{:S(2)}) copy-start(f32[16,64,512]{2,1,0:T(8,128)} %snapshot_ref.5) | copy-start | bytes 6291460
  3.1 6.6 %collective-permute-start = (f32[8,8,512]{2,1,0:T(8,128)S(1)}, f32[8,8,512]{2,1,0:T(8,128)S(1)}, u32[]{:S(2)}, u32[]{:S(2)}) collective-permute-start(f32[8,8,512]{2,1,0:T(8,128)S(1)} %get-tuple-element.12), channel_id=1, source_target_pairs={{0,1},{1,2},{2,3},{4,5},{5,6},{6,7},{8,9},{9,10},{10,11},{12,13},{... | collective-permute-start | bytes 393224 | tf_op jit(solution)/shard_map/ppermute | solution.py:20
  7.2 5.7 %collective-permute-start.1 = (f32[8,8,512]{2,1,0:T(8,128)S(1)}, f32[8,8,512]{2,1,0:T(8,128)S(1)}, u32[]{:S(2)}, u32[]{:S(2)}) collective-permute-start(f32[8,8,512]{2,1,0:T(8,128)S(1)} %get-tuple-element.13), channel_id=1, source_target_pairs={{1,0},{2,1},{3,2},{5,4},{6,5},{7,6},{9,8},{10,9},{11,10},{13,12},{... | collective-permute-start | bytes 393224 | tf_op jit(solution)/shard_map/ppermute | solution.py:20
  13.0 17.5 %collective-permute-start.2 = (f32[3,80,512]{2,1,0:T(8,128)S(1)}, f32[3,80,512]{2,1,0:T(8,128)}, u32[]{:S(2)}, u32[]{:S(2)}) collective-permute-start(f32[3,80,512]{2,1,0:T(8,128)S(1)} %get-tuple-element.16), channel_id=1, source_target_pairs={{0,4},{4,8},{8,12},{12,16},{16,20},{20,24},{24,28},{28,32},{32,36}... | collective-permute-start | bytes 1474568 | tf_op jit(solution)/shard_map/ppermute | solution.py:20
  18.2 12.3 %collective-permute-start.3 = (f32[3,80,512]{2,1,0:T(8,128)S(1)}, f32[3,80,512]{2,1,0:T(8,128)}, u32[]{:S(2)}, u32[]{:S(2)}) collective-permute-start(f32[3,80,512]{2,1,0:T(8,128)S(1)} %get-tuple-element.17), channel_id=1, source_target_pairs={{4,0},{8,4},{12,8},{16,12},{20,16},{24,20},{28,24},{32,28},{36,32}... | collective-permute-start | bytes 1474568 | tf_op jit(solution)/shard_map/ppermute | solution.py:20
  20.2 19.9 %all-to-all-start = ((s32[128,1,128]{2,1,0:T(1,128)}), s32[128,1,128]{2,1,0:T(1,128)S(1)}, u32[]{:S(2)}, u32[]{:S(2)}) async-start(s32[128,1,128]{2,1,0:T(1,128)} %bitcast.2), calls=%async_computation | async-start | bytes 131072 | tf_op jit(solution)/shard_map/all_to_all | solution.py:495

commit v4 on v3

--- a/solution.py
+++ b/solution.py
@@ -37,6 +37,26 @@
     ]
 
 
+def around_odd(tiles, s, sub):
+    up = [rolled(t, -s) for t in tiles]
+    if 2 * s == SUB:
+        return [a + b for a, b in zip(up[:-1], up[1:])]
+    return [
+        jnp.where(sub == SUB - s, up[k + 1], up[k]) + rolled(tiles[k], s)
+        for k in range(len(tiles) - 1)
+    ]
+
+
+def around_even(tiles, s, sub):
+    down = [rolled(t, s) for t in tiles]
+    if 2 * s == SUB:
+        return [a + b for a, b in zip(down[1:], down[:-1])]
+    return [
+        jnp.where(sub == 0, down[k - 1], down[k]) + rolled(tiles[k], -s)
+        for k in range(1, len(tiles))
+    ]
+
+
 def weight(value, chosen):
     return jnp.where(chosen, jnp.float32(value), jnp.float32(0.0))
 
@@ -45,11 +65,10 @@
     odd = weight(0.5, sub % (2 * s) == s)
     even = weight(0.25, sub % (2 * s) == 0)
     left, right = tiles[0], tiles[-1]
-    inner = [t - odd * n for t, n in zip(tiles[1:-1], neighbours(tiles, s, sub))]
+    inner = [t - odd * n for t, n in zip(tiles[1:-1], around_odd(tiles[1:], s, sub))]
     ahead = rolled(tiles[1], -s)
     left = left - jnp.where(sub == SUB - s, 0.5 * has_left * ahead, 0.0)
-    full = [left] + inner + [right]
-    smooth = [t + even * n for t, n in zip(inner, neighbours(full, s, sub))]
+    smooth = [t + even * n for t, n in zip(inner, around_even([left] + inner, s, sub))]
     behind = rolled(inner[-1], s)
     if s == 1:
         right = jnp.where(sub == 0, rolled(right, -1) + 0.25 * has_right * behind, right)
@@ -157,19 +176,6 @@
     )(snapshot)
 
 
-def row_of(snapshot_ref, left_ref, right_ref, x, lanes, sub):
-    rows, cols, _ = snapshot_ref.shape
-    half = rows // 2
-    left = left_ref[x % half, :, lanes]
-    right = right_ref[x % half, :, lanes]
-    if x >= half:
-        left, right = rolled(left, 4), rolled(right, 4)
-    left = jnp.where(sub >= 4, left, 0.0)
-    right = jnp.where(sub < 4, right, 0.0)
-    inner = [snapshot_ref[x, SUB * k : SUB * (k + 1), lanes] for k in range(cols // SUB)]
-    return [left] + inner + [right]
-
-
 def x_edges_inner_kernel(
     snapshot_ref, mask_ref, to_before_ref, to_after_ref, counts_ref, starts_ref
 ):
@@ -248,7 +254,9 @@
     before_ref,
     after_ref,
     coefficients_hbm_ref,
-    coefficients_ref,
+    front_ref,
+    back_ref,
+    work,
     sems,
 ):
     rows, cols, depth = snapshot_ref.shape
@@ -272,78 +280,121 @@
     factor[8] = jnp.where(sub % 2 == 0, factor[8], scale[0])
     factor[4] = jnp.where(sub % 2 == 0, factor[4], scale[0])
 
+    half = rows // 2
+    past_at, kept_at, after_at, before_at = range(half, half + 4)
+
     def write(t):
         lanes = pl.ds(pl.multiple_of(t * LANES, LANES), LANES)
-        return pltpu.make_async_copy(
-            coefficients_ref.at[:, :, lanes], coefficients_hbm_ref.at[:, :, lanes], sems.at[t]
-        )
+        return [
+            pltpu.make_async_copy(
+                ref.at[:, :, lanes], coefficients_hbm_ref.at[at : at + half, :, lanes], sems.at[t, i]
+            )
+            for i, (ref, at) in enumerate(((front_ref, 0), (back_ref, half)))
+        ]
 
     @pl.loop(0, width)
     def _(t):
         lanes = pl.ds(pl.multiple_of(t * LANES, LANES), LANES)
 
-        def load(ref, level):
-            return [ref[level, SUB * k : SUB * (k + 1), lanes] for k in range(count + 2)]
-
-        def store(x, row):
-            by = 8 if x % 8 == 0 else 4 if x % 4 == 0 else 2 if x % 2 == 0 else 1
-            for k in range(count):
-                coefficients_ref[x, SUB * k : SUB * (k + 1), lanes] = factor[by] * row[k + 1]
-
-        def step(c, s, beyond, ahead, mine):
+        def span(k):
+            return slice(SUB * k, SUB * (k + 1))
+
+        def store(x, k, tile):
+            if 1 <= k <= count:
+                by = 8 if x % 8 == 0 else 4 if x % 4 == 0 else 2 if x % 2 == 0 else 1
+                ref = front_ref if x < half else back_ref
+                ref[x % half, span(k - 1), lanes] = factor[by] * tile
+
+        def entry(x, k):
+            if 1 <= k <= count:
+                return snapshot_ref[x, span(k - 1), lanes]
+            tile = (left_ref if k == 0 else right_ref)[x % half, :, lanes]
+            tile = rolled(tile, 4) if x >= half else tile
+            return jnp.where(sub >= 4 if k == 0 else sub < 4, tile, 0.0)
+
+        def step(c, s, beyond, ahead):
             held = sub % s == 0
-            half_w, quarter_w = weight(0.5, held), weight(0.25, held)
-            end = rows
-            c[end] = beyond
+            half_w, quarter_w = (weight(0.5, held), weight(0.25, held)) if s > 1 else (0.5, 0.25)
+            c[rows] = beyond
             for x in range(s, rows, 2 * s):
-                c[x] = [v - half_w * (a + b) for v, a, b in zip(c[x], c[x - s], c[x + s])]
-            c[-s] = [v - (half_w * x_left) * a for v, a in zip(ahead, c[0])]
+                c[x] = c[x] - half_w * (c[x - s] + c[x + s])
+            c[-s] = ahead - (half_w * x_left) * c[0]
             for x in range(0, rows, 2 * s):
-                c[x] = [v + quarter_w * (a + b) for v, a, b in zip(c[x], c[x - s], c[x + s])]
-            past = [v + (0.25 * x_right) * a for v, a in zip(mine, c[rows - s])] if mine else None
-            return c, past, c[-s]
-
-        def lift(row, s):
-            return lift_rows(row, s, sub, y_left, y_right)
-
-        c = {x: row_of(snapshot_ref, left_ref, right_ref, x, lanes, sub) for x in range(rows)}
-        c, past, d = step(c, 1, load(after_ref, 0), load(before_ref, 0), load(after_ref, 1))
-        for x in range(1, rows, 2):
-            store(x, c[x])
-        kept = combine(load(before_ref, 1), d, 0.25)
-        for x in range(0, rows, 2):
-            c[x] = lift(c[x], 1)
-        past, kept = lift(past, 1), lift(kept, 1)
-        after3, before3 = lift(load(after_ref, 2), 1), lift(load(before_ref, 2), 1)
-        mine = [0.875 * v + a for v, a in zip(past, after3)]
-        c, past, d = step(c, 2, past, kept, mine)
-        for x in range(2, rows, 4):
-            store(x, c[x])
-        kept = combine(before3, d, 0.25)
-        for x in range(0, rows, 4):
-            c[x] = lift(c[x], 2)
-        past, kept = lift(past, 2), lift(kept, 2)
-        c, past, d = step(c, 4, past, kept, None)
-        for x in range(4, rows, 8):
-            store(x, c[x])
+                c[x] = c[x] + quarter_w * (c[x - s] + c[x + s])
+            return c
+
+        def lift_row(source, target, s):
+            row = [source(k) for k in range(count + 2)]
+            for k, tile in enumerate(lift_rows(row, s, sub, y_left, y_right)):
+                target(k, tile)
+
+        def held_at(at):
+            return lambda k: work[at, span(k)]
+
+        def put_at(at):
+            def put(k, tile):
+                work[at, span(k)] = tile
+
+            return put
+
+        for k in range(count + 2):
+            c = {x: entry(x, k) for x in range(rows)}
+            c = step(c, 1, after_ref[0, span(k), lanes], before_ref[0, span(k), lanes])
+            for x in range(1, rows, 2):
+                store(x, k, c[x])
+            for x in range(0, rows, 2):
+                work[x // 2, span(k)] = c[x]
+            work[past_at, span(k)] = after_ref[1, span(k), lanes] + (0.25 * x_right) * c[rows - 1]
+            work[kept_at, span(k)] = before_ref[1, span(k), lanes] + 0.25 * c[-1]
+        for at in range(half + 2):
+            lift_row(held_at(at), put_at(at), 1)
+        lift_row(lambda k: after_ref[2, span(k), lanes], put_at(after_at), 1)
+        lift_row(lambda k: before_ref[2, span(k), lanes], put_at(before_at), 1)
+        for k in range(count + 2):
+            c = {x: work[x // 2, span(k)] for x in range(0, rows, 2)}
+            past = work[past_at, span(k)]
+            c = step(c, 2, past, work[kept_at, span(k)])
+            for x in range(2, rows, 4):
+                store(x, k, c[x])
+            for x in range(0, rows, 4):
+                work[x // 2, span(k)] = c[x]
+            mine = 0.875 * past + work[after_at, span(k)]
+            work[past_at, span(k)] = mine + (0.25 * x_right) * c[rows - 2]
+            work[kept_at, span(k)] = work[before_at, span(k)] + 0.25 * c[-2]
+        for at in [x // 2 for x in range(0, rows, 4)] + [past_at, kept_at]:
+            lift_row(held_at(at), put_at(at), 2)
+        for k in range(count + 2):
+            c = {x: work[x // 2, span(k)] for x in range(0, rows, 4)}
+            c = step(c, 4, work[past_at, span(k)], work[kept_at, span(k)])
+            for x in range(4, rows, 8):
+                store(x, k, c[x])
+            for x in range(0, rows, 8):
+                work[x // 2, span(k)] = c[x]
         for x in range(0, rows, 8):
-            store(x, lift(c[x], 4))
-        write(t).start()
+            lift_row(held_at(x // 2), lambda k, tile, x=x: store(x, k, tile), 4)
+        for copy in write(t):
+            copy.start()
 
     @pl.loop(0, width)
     def _(t):
-        write(t).wait()
+        for copy in write(t):
+            copy.wait()
 
 
 def lift(scales, snapshot, left, right, before, after):
+    rows, cols, depth = snapshot.shape
     return pl.pallas_call(
         lift_kernel,
         in_specs=[SMEM] + [VMEM] * 5,
-        out_specs=pl.BlockSpec(memory_space=pltpu.HBM),
-        out_shape=jax.ShapeDtypeStruct(snapshot.shape, jnp.float32),
+        out_specs=[pl.BlockSpec(memory_space=pltpu.HBM), VMEM],
+        out_shape=[
+            jax.ShapeDtypeStruct(snapshot.shape, jnp.float32),
+            jax.ShapeDtypeStruct((rows // 2, cols, depth), jnp.float32),
+        ],
         scratch_shapes=[
-            pltpu.VMEM(snapshot.shape, jnp.float32),
-            pltpu.SemaphoreType.DMA((snapshot.shape[2] // LANES,)),
+            pltpu.VMEM((rows // 2, cols, depth), jnp.float32),
+            pltpu.VMEM((rows // 2 + 4, cols + 2 * SUB, LANES), jnp.float32),
+            pltpu.SemaphoreType.DMA((depth // LANES, 2)),
         ],
         compiler_params=PARAMS,
         cost_estimate=pl.CostEstimate(
@@ -357,29 +408,33 @@
     table_ref,
     starts_ref,
     coefficients_hbm_ref,
+    front_ref,
     flags_ref,
     packed_ref,
     counts_ref,
-    coefficients_ref,
+    back_ref,
     buffer,
     ranks,
     sems,
 ):
-    rows, cols, depth = coefficients_ref.shape
+    half, cols, depth = front_ref.shape
+    rows = 2 * half
     width = depth // LANES
     slots = rows * cols * width
     per_row = cols * width
     one, zero = jnp.float32(1.0), jnp.float32(0.0)
-    group = rows // sems.shape[0]
-
-    def read(part):
-        part = pl.ds(part * group, group)
-        return pltpu.make_async_copy(
-            coefficients_hbm_ref.at[part], coefficients_ref.at[part], sems.at[part.start // group]
+    parts = sems.shape[0]
+    group = half // parts
+    copies = [
+        pltpu.make_async_copy(
+            coefficients_hbm_ref.at[half + group * part : half + group * (part + 1)],
+            back_ref.at[group * part : group * (part + 1)],
+            sems.at[part],
         )
-
-    for part in range(rows // group):
-        read(part).start()
+        for part in range(parts)
+    ]
+    for copy in copies:
+        copy.start()
 
     device = lax.axis_index("gx") * lax.axis_size("gy") + lax.axis_index("gy")
     table = table_ref[...]
@@ -399,13 +454,14 @@
     span = per_row + SUB
 
     def place_row(x):
+        ref = front_ref if x < half else back_ref
         at = (offset + starts_ref[x, 0]) & (slots - 1)
         base = pl.multiple_of(lax.shift_left(lax.shift_right_logical(at, 3), 3), SUB)
         wanted = ranks[x : x + 1, :] + (at - base)
         row_id = lax.broadcasted_iota(jnp.int32, (span, per_row), 0)
         onehot = jnp.where(row_id == wanted, one, zero).astype(jnp.bfloat16)
         values = jnp.concatenate(
-            [coefficients_ref[x, :, LANES * t : LANES * (t + 1)] for t in range(width)], axis=0
+            [ref[x % half, :, LANES * t : LANES * (t + 1)] for t in range(width)], axis=0
         )
         high = values.astype(jnp.bfloat16)
         low = (values - high.astype(jnp.float32)).astype(jnp.bfloat16)
@@ -414,36 +470,36 @@
         )
         buffer[pl.ds(base, span), :] += both[:, :LANES] + both[:, LANES:]
 
-    for part in range(rows // group):
-        read(part).wait()
-        for x in range(part * group, part * group + group):
-            place_row(x)
+    for x in range(rows):
+        if x >= half and x % group == 0:
+            copies[(x - half) // group].wait()
+        place_row(x)
 
     packed_ref[span:, :] = buffer[span:slots, :]
     packed_ref[:span, :] = buffer[:span, :] + buffer[slots:, :]
 
 
-def pack(table, starts, coefficients, flags):
+def pack(table, starts, coefficients, front, flags):
     rows, cols, depth = coefficients.shape
     per_row = flags.shape[1]
     slots = rows * per_row
     return pl.pallas_call(
         pack_kernel,
-        in_specs=[VMEM, SMEM, pl.BlockSpec(memory_space=pltpu.HBM), VMEM],
+        in_specs=[VMEM, SMEM, pl.BlockSpec(memory_space=pltpu.HBM), VMEM, VMEM],
         out_specs=[VMEM] * 2,
         out_shape=[
             jax.ShapeDtypeStruct((slots, LANES), jnp.float32),
             jax.ShapeDtypeStruct((1, table.shape[0]), jnp.int32),
         ],
         scratch_shapes=[
-            pltpu.VMEM(coefficients.shape, jnp.float32),
+            pltpu.VMEM((rows // 2, cols, depth), jnp.float32),
             pltpu.VMEM((slots + per_row + SUB, LANES), jnp.float32),
             pltpu.VMEM((rows, per_row), jnp.int32),
-            pltpu.SemaphoreType.DMA((4,)),
+            pltpu.SemaphoreType.DMA((2,)),
         ],
         compiler_params=pltpu.CompilerParams(vmem_limit_bytes=PACK_LIMIT),
         name="pack",
-    )(table, starts, coefficients, flags)
+    )(table, starts, coefficients, front, flags)
 
 
 def merge_kernel(counts_ref, arrived_ref, merged_ref):
@@ -499,8 +555,8 @@
     x_before, x_after = x_edges_halo(left, right, x_before, x_after)
     after = shifted(x_before, "gx", -1)
     before = shifted(x_after, "gx", 1)
-    coefficients = lift(scales, snapshot, left, right, before, after)
-    packed, counts = pack(table, starts, coefficients, flags)
+    coefficients, front = lift(scales, snapshot, left, right, before, after)
+    packed, counts = pack(table, starts, coefficients, front, flags)
     share = slots // devices
     arrived = lax.all_to_all(packed.reshape(devices, share, LANES), ALL, 0, 0, tiled=True)
     merged = merge(counts, arrived)

time: 116 us -> 115 us (level)
  transfers between devices with their start and end apart: 5 -> 5, of which waited for: 2 -> 2; matrix products, arithmetic and copies ran while one was open for 0% -> 0% of each run, Pallas kernels for 5% -> 4%
where the time goes in v4:
time: 115 us; the launch traced here: 114 us
  blocking collectives  69.1 us (60%)
  starting transfers between devices  22.7 us (20%)
  Pallas kernels  10.1 us (9%)
  waiting for transfers between devices  8.74 us (8%)
  local copies, waits for them, and re-layouts  3.01 us (3%)
    all_to_all x1, blocking collectives, on_device(): lax.all_to_all(packed.reshape(devices, share, LANES), ALL, 0, 0, tiled=True)  34.9 us
    all_to_all x1, blocking collectives, on_device(): stream = lax.all_to_all(merged, ALL, 0, 0, tiled=True).reshape(slots, LANES)  34.2 us
    ppermute x4, starting transfers between devices, shifted(): lax.ppermute(value, axis, [(source, source + steps) for source in range(l...  12.5 us
    all_to_all x1, starting transfers between devices, on_device(): lax.all_to_all(own_counts.reshape(devices, 1, LANES), ALL, 0, 0, tiled=True)  10.3 us
    all_to_all x1, waiting for transfers between devices, on_device(): lax.all_to_all(own_counts.reshape(devices, 1, LANES), ALL, 0, 0, tiled=True)  5.51 us
    pallas_call x1, Pallas kernels, lift(): pl.pallas_call(lift_kernel, in_specs=[SMEM] + [VMEM] * 5, out_specs=[pl.B...  3.97 us
    ppermute x4, waiting for transfers between devices, shifted(): lax.ppermute(value, axis, [(source, source + steps) for source in range(l...  3.23 us
    unnamed x9, local copies, waits for them, and re-layouts  2.92 us
  transfers between devices with their start and end apart: 5, of which 2 were waited for; matrix products, arithmetic and copies ran while one was open for 0% of the time, Pallas kernels for 4%

profile of v4, /device:TPU:1, one launch (start us, length us, event | category | flops | bytes accessed | tf_op | source)
XLA Modules:
  0.0 114.5 jit_solution(6107573353941814389)
XLA Ops:
  0.6 0.0 copy-start
  0.6 1.6 %copy-done = f32[16,64,512]{2,1,0:T(8,128)S(1)} copy-done((f32[16,64,512]{2,1,0:T(8,128)S(1)}, f32[16,64,512]{2,1,0:T(8,128)}, u32[]{:S(2)}) %copy-start) | copy-done | bytes 2097176
  2.2 0.0 copy-start.2
  2.2 0.8 y_edges.1
  3.1 0.0 copy-start.3
  3.1 0.0 copy-start.1
  3.1 4.1 %collective-permute-start = (f32[8,8,512]{2,1,0:T(8,128)S(1)}, f32[8,8,512]{2,1,0:T(8,128)S(1)}, u32[]{:S(2)}, u32[]{:S(2)}) collective-permute-start(f32[8,8,512]{2,1,0:T(8,128)S(1)} %get-tuple-element.14), channel_id=1, source_target_pairs={{0,1},{1,2},{2,3},{4,5},{5,6},{6,7},{8,9},{9,10},{10,11},{12,13},{... | collective-permute-start | bytes 393224 | tf_op jit(solution)/shard_map/ppermute | solution.py:20
  7.2 1.3 %collective-permute-start.1 = (f32[8,8,512]{2,1,0:T(8,128)S(1)}, f32[8,8,512]{2,1,0:T(8,128)S(1)}, u32[]{:S(2)}, u32[]{:S(2)}) collective-permute-start(f32[8,8,512]{2,1,0:T(8,128)S(1)} %get-tuple-element.15), channel_id=1, source_target_pairs={{1,0},{2,1},{3,2},{5,4},{6,5},{7,6},{9,8},{10,9},{11,10},{13,12},{... | collective-permute-start | bytes 393224 | tf_op jit(solution)/shard_map/ppermute | solution.py:20
  8.5 0.0 copy-done.2
  8.5 1.2 %x_edges_inner.1 = (f32[3,80,512]{2,1,0:T(8,128)S(1)}, f32[3,80,512]{2,1,0:T(8,128)S(1)}, s32[128,128]{1,0:T(8,128)}, s32[16,128]{1,0:T(8,128)S(1)}) custom-call(f32[16,64,512]{2,1,0:T(8,128)S(1)} %copy-done, s32[16,4,64]{2,1,0:T(4,128)S(1)} %bitcast.9), custom_call_target="tpu_custom_call" | custom-call | tf_op jit(solution)/shard_map/x_edges_inner/pallas_call | solution.py:221
  9.7 0.0 collective-permute-done.left_ref
  9.7 3.2 %collective-permute-done.1.right_ref = f32[8,8,512]{2,1,0:T(8,128)S(1)} collective-permute-done((f32[8,8,512]{2,1,0:T(8,128)S(1)}, f32[8,8,512]{2,1,0:T(8,128)S(1)}, u32[]{:S(2)}, u32[]{:S(2)}) %collective-permute-start.1) | collective-permute-done | bytes 131104 | tf_op jit(solution)/shard_map/ppermute | solution.py:20
  12.9 0.1 x_edges_halo.1
  13.0 5.2 %collective-permute-start.2 = (f32[3,80,512]{2,1,0:T(8,128)S(1)}, f32[3,80,512]{2,1,0:T(8,128)}, u32[]{:S(2)}, u32[]{:S(2)}) collective-permute-start(f32[3,80,512]{2,1,0:T(8,128)S(1)} %get-tuple-element.18), channel_id=1, source_target_pairs={{0,4},{4,8},{8,12},{12,16},{16,20},{20,24},{24,28},{28,32},{32,36}... | collective-permute-start | bytes 1474568 | tf_op jit(solution)/shard_map/ppermute | solution.py:20
  18.2 1.9 %collective-permute-start.3 = (f32[3,80,512]{2,1,0:T(8,128)S(1)}, f32[3,80,512]{2,1,0:T(8,128)}, u32[]{:S(2)}, u32[]{:S(2)}) collective-permute-start(f32[3,80,512]{2,1,0:T(8,128)S(1)} %get-tuple-element.19), channel_id=1, source_target_pairs={{4,0},{8,4},{12,8},{16,12},{20,16},{24,20},{28,24},{32,28},{36,32}... | collective-permute-start | bytes 1474568 | tf_op jit(solution)/shard_map/ppermute | solution.py:20
  20.2 10.3 %all-to-all-start = ((s32[128,1,128]{2,1,0:T(1,128)}), s32[128,1,128]{2,1,0:T(1,128)S(1)}, u32[]{:S(2)}, u32[]{:S(2)}) async-start(s32[128,1,128]{2,1,0:T(1,128)} %bitcast.2), calls=%async_computation | async-start | bytes 131072 | tf_op jit(solution)/shard_map/all_to_all | solution.py:551
  30.4 0.1 reshape.21.flags_ref
  30.5 0.0 copy-done.3
  30.5 0.0 collective-permute-done.2.before_ref
  30.5 0.0 collective-permute-done.3.after_ref
  30.5 0.0 copy-done.1
  30.5 4.0 %lift.1 = (f32[16,64,512]{2,1,0:T(8,128)}, f32[8,64,512]{2,1,0:T(8,128)S(1)}) custom-call(f32[4]{0:T(128)S(1)} %multiply_exponential_fusion.scales_ref, f32[16,64,512]{2,1,0:T(8,128)S(1)} %copy-done.1, f32[8,8,512]{2,1,0:T(8,128)S(1)} %collective-permute-done.left_ref, f32[8,8,512]{2,1,0:T(8,128)S(1)} %collective-permute-done.1.right_ref, ...), custom_call_target="tpu_custom_call" | custom-call | flops 2000000000 | bytes 16777216 | tf_op jit(solution)/shard_map/lift/pallas_call | solution.py:386
  34.5 5.5 %all-to-all-done = s32[128,1,128]{2,1,0:T(1,128)S(1)} async-done(((s32[128,1,128]{2,1,0:T(1,128)}), s32[128,1,128]{2,1,0:T(1,128)S(1)}, u32[]{:S(2)}, u32[]{:S(2)}) %all-to-all-start) | async-done | bytes 65568 | tf_op jit(solution)/shard_map/all_to_all | solution.py:551
  40.0 2.6 %pack.1 = (f32[4096,128]{1,0:T(8,128)S(1)}, s32[1,128]{1,0:T(1,128)S(1)}) custom-call(s32[128,128]{1,0:T(8,128)S(1)} %bitcast.8, s32[16,128]{1,0:T(8,128)S(1)} %get-tuple-element.22.starts_ref, f32[16,64,512]{2,1,0:T(8,128)} %get-tuple-element.28.coefficients_hbm_ref, f32[8,64,512]{2,1,0:T(8,128)S(1)} %get-tuple-element.23.front_ref, ...), custom_call_target="tpu_custom_call" | custom-call | tf_op jit(solution)/shard_map/pack/pallas_call | solution.py:486
  42.7 34.9 %all_to_all.15.arrived_ref = f32[128,32,128]{2,1,0:T(8,128)S(1)} all-to-all(f32[128,32,128]{2,1,0:T(8,128)S(1)} %bitcast.7), channel_id=1, replica_groups=mesh['gx'=32,'gy'=4] {'gx','gy'}, dimensions={0} | all-to-all | bytes 4194304 | tf_op jit(solution)/shard_map/all_to_all | solution.py:561
  77.6 1.4 %merge.1 = f32[128,32,128]{2,1,0:T(8,128)S(1)} custom-call(s32[1,128]{1,0:T(1,128)S(1)} %get-tuple-element.24.counts_ref, f32[128,32,128]{2,1,0:T(8,128)S(1)} %all_to_all.15.arrived_ref), custom_call_target="tpu_custom_call" | custom-call | tf_op jit(solution)/shard_map/merge/pallas_call | solution.py:531
  79.0 34.2 %all_to_all.16 = f32[128,32,128]{2,1,0:T(8,128)S(1)} all-to-all(f32[128,32,128]{2,1,0:T(8,128)S(1)} %merge.1), channel_id=1, replica_groups=mesh['gx'=32,'gy'=4] {'gx','gy'}, dimensions={0} | all-to-all | bytes 4194304 | tf_op jit(solution)/shard_map/all_to_all | solution.py:563
  113.2 1.3 %copy.11 = f32[4096,128]{1,0:T(8,128)} copy(f32[4096,128]{1,0:T(8,128)S(1)} %bitcast.11) | data formatting | bytes 4194304
  (1 shorter events, 0.0 us)
Async XLA Ops:
  0.6 1.6 %copy-start = (f32[16,64,512]{2,1,0:T(8,128)S(1)}, f32[16,64,512]{2,1,0:T(8,128)}, u32[]{:S(2)}) copy-start(f32[16,64,512]{2,1,0:T(8,128)} %snapshot_ref.5) | copy-start | bytes 6291460
  2.2 6.3 %copy-start.2 = (s32[16,64,4]{1,2,0:T(4,128)S(1)}, s32[16,64,4]{1,2,0:T(4,128)}, u32[]{:S(2)}) copy-start(s32[16,64,4]{1,2,0:T(4,128)} %param.4) | copy-start | bytes 49156
  3.1 27.5 %copy-start.3 = (s32[4]{0:T(128)S(1)}, s32[4]{0:T(128)}, u32[]{:S(2)}) copy-start(s32[4]{0:T(128)} %param.5) | copy-start | bytes 52
  3.1 27.5 %copy-start.1 = (f32[16,64,512]{2,1,0:T(8,128)S(1)}, f32[16,64,512]{2,1,0:T(8,128)}, u32[]{:S(2)}) copy-start(f32[16,64,512]{2,1,0:T(8,128)} %snapshot_ref.5) | copy-start | bytes 6291460
  3.1 6.6 %collective-permute-start = (f32[8,8,512]{2,1,0:T(8,128)S(1)}, f32[8,8,512]{2,1,0:T(8,128)S(1)}, u32[]{:S(2)}, u32[]{:S(2)}) collective-permute-start(f32[8,8,512]{2,1,0:T(8,128)S(1)} %get-tuple-element.14), channel_id=1, source_target_pairs={{0,1},{1,2},{2,3},{4,5},{5,6},{6,7},{8,9},{9,10},{10,11},{12,13},{... | collective-permute-start | bytes 393224 | tf_op jit(solution)/shard_map/ppermute | solution.py:20
  7.2 5.7 %collective-permute-start.1 = (f32[8,8,512]{2,1,0:T(8,128)S(1)}, f32[8,8,512]{2,1,0:T(8,128)S(1)}, u32[]{:S(2)}, u32[]{:S(2)}) collective-permute-start(f32[8,8,512]{2,1,0:T(8,128)S(1)} %get-tuple-element.15), channel_id=1, source_target_pairs={{1,0},{2,1},{3,2},{5,4},{6,5},{7,6},{9,8},{10,9},{11,10},{13,12},{... | collective-permute-start | bytes 393224 | tf_op jit(solution)/shard_map/ppermute | solution.py:20
  13.0 17.5 %collective-permute-start.2 = (f32[3,80,512]{2,1,0:T(8,128)S(1)}, f32[3,80,512]{2,1,0:T(8,128)}, u32[]{:S(2)}, u32[]{:S(2)}) collective-permute-start(f32[3,80,512]{2,1,0:T(8,128)S(1)} %get-tuple-element.18), channel_id=1, source_target_pairs={{0,4},{4,8},{8,12},{12,16},{16,20},{20,24},{24,28},{28,32},{32,36}... | collective-permute-start | bytes 1474568 | tf_op jit(solution)/shard_map/ppermute | solution.py:20
  18.2 12.3 %collective-permute-start.3 = (f32[3,80,512]{2,1,0:T(8,128)S(1)}, f32[3,80,512]{2,1,0:T(8,128)}, u32[]{:S(2)}, u32[]{:S(2)}) collective-permute-start(f32[3,80,512]{2,1,0:T(8,128)S(1)} %get-tuple-element.19), channel_id=1, source_target_pairs={{4,0},{8,4},{12,8},{16,12},{20,16},{24,20},{28,24},{32,28},{36,32}... | collective-permute-start | bytes 1474568 | tf_op jit(solution)/shard_map/ppermute | solution.py:20
  20.2 19.9 %all-to-all-start = ((s32[128,1,128]{2,1,0:T(1,128)}), s32[128,1,128]{2,1,0:T(1,128)S(1)}, u32[]{:S(2)}, u32[]{:S(2)}) async-start(s32[128,1,128]{2,1,0:T(1,128)} %bitcast.2), calls=%async_computation | async-start | bytes 131072 | tf_op jit(solution)/shard_map/all_to_all | solution.py:551

commit v5 on v4

--- a/solution.py
+++ b/solution.py
@@ -14,10 +14,16 @@
 PARAMS = pltpu.CompilerParams(vmem_limit_bytes=16 * 2**20)
 
 
-def shifted(value, axis, steps):
+def pairs_exchange(first, second, axis, ring):
     count = lax.axis_size(axis)
-    leading, last = (max(0, -steps), min(count, count - steps))
-    return lax.ppermute(value, axis, [(source, source + steps) for source in range(leading, last)])
+    inner = [(k, k ^ 1) for k in range(count)]
+    outer = [(k, k + 1 if k % 2 else k - 1) for k in range(0 if ring else 1, count - (not ring))]
+    outer = [(a % count, b % count) for a, b in outer]
+    return lax.ppermute(first, axis, inner), lax.ppermute(second, axis, outer)
+
+
+def is_even(axis):
+    return lax.axis_index(axis) % 2 == 0
 
 
 def sublane():
@@ -121,9 +127,10 @@
     counts_ref[...] = jnp.broadcast_to(total, counts_ref.shape)
 
 
-def y_edges_kernel(snapshot_ref, to_before_ref, to_after_ref):
+def y_edges_kernel(snapshot_ref, inner_ref, outer_ref):
     rows, cols, depth = snapshot_ref.shape
     half = rows // 2
+    even_gy = is_even("gy")
     sub = sublane()
     zero = jnp.zeros((SUB, LANES), jnp.float32)
 
@@ -159,8 +166,10 @@
     def _(x):
         for t in range(depth // LANES):
             lanes = slice(t * LANES, (t + 1) * LANES)
-            to_before_ref[x, :, lanes] = before(x, lanes) + rolled(before(x + half, lanes), 4)
-            to_after_ref[x, :, lanes] = after(x, lanes) + rolled(after(x + half, lanes), 4)
+            to_before = before(x, lanes) + rolled(before(x + half, lanes), 4)
+            to_after = after(x, lanes) + rolled(after(x + half, lanes), 4)
+            inner_ref[x, :, lanes] = jnp.where(even_gy, to_after, to_before)
+            outer_ref[x, :, lanes] = jnp.where(even_gy, to_before, to_after)
 
 
 def y_edges(snapshot):
@@ -177,42 +186,49 @@
 
 
 def x_edges_inner_kernel(
-    snapshot_ref, mask_ref, to_before_ref, to_after_ref, counts_ref, starts_ref
+    snapshot_ref, mask_ref, inner_ref, outer_ref, counts_ref, starts_ref
 ):
     rows, cols, depth = snapshot_ref.shape
+    even_gx = is_even("gx")
     count_kept(mask_ref, counts_ref, starts_ref)
 
     @pl.loop(0, cols // SUB)
     def _(k):
-        inner = pl.ds(pl.multiple_of(SUB * k, SUB), SUB)
+        here = pl.ds(pl.multiple_of(SUB * k, SUB), SUB)
         placed = pl.ds(pl.multiple_of(SUB * k + SUB, SUB), SUB)
         for t in range(depth // LANES):
             lanes = slice(t * LANES, (t + 1) * LANES)
-            c = {x: [snapshot_ref[x, inner, lanes]] for x in range(rows)}
+            c = {x: [snapshot_ref[x, here, lanes]] for x in range(rows)}
             for level, (a, b) in enumerate(zip(front_parts(c), back_parts(c))):
-                to_before_ref[level, placed, lanes] = a[0]
-                to_after_ref[level, placed, lanes] = b[0]
-
-
-def x_edges_halo_kernel(
-    left_ref, right_ref, before_in_ref, after_in_ref, to_before_ref, to_after_ref
-):
-    half, _, depth = left_ref.shape
+                inner_ref[level, placed, lanes] = jnp.where(even_gx, b[0], a[0])
+                outer_ref[level, placed, lanes] = jnp.where(even_gx, a[0], b[0])
+
+
+def x_edges_halo_kernel(y_inner_ref, y_outer_ref, _, __, inner_ref, outer_ref):
+    half, _, depth = y_inner_ref.shape
     rows = 2 * half
-    cols = to_before_ref.shape[1] - 2 * SUB
+    cols = inner_ref.shape[1] - 2 * SUB
     sub = sublane()
+    gy = lax.axis_index("gy")
+    even_gy, even_gx = is_even("gy"), is_even("gx")
 
     @pl.loop(0, depth // LANES)
     def _(t):
         lanes = pl.ds(pl.multiple_of(t * LANES, LANES), LANES)
-        for halo_ref, place in ((left_ref, 0), (right_ref, cols + SUB)):
-            held = sub >= 4 if place == 0 else sub < 4
-            packed = [halo_ref[x, :, lanes] for x in range(half)]
+        for place in (0, cols + SUB):
+            if place == 0:
+                held, swap = (sub >= 4) & (gy > 0), even_gy
+            else:
+                held, swap = (sub < 4) & (gy < lax.axis_size("gy") - 1), ~even_gy
+            packed = [
+                jnp.where(swap, y_outer_ref[x, :, lanes], y_inner_ref[x, :, lanes])
+                for x in range(half)
+            ]
             packed = packed + [rolled(tile, 4) for tile in packed]
             c = {x: [jnp.where(held, packed[x], 0.0)] for x in range(rows)}
             for level, (a, b) in enumerate(zip(front_parts(c), back_parts(c))):
-                to_before_ref[level, place : place + SUB, lanes] = a[0]
-                to_after_ref[level, place : place + SUB, lanes] = b[0]
+                inner_ref[level, place : place + SUB, lanes] = jnp.where(even_gx, b[0], a[0])
+                outer_ref[level, place : place + SUB, lanes] = jnp.where(even_gx, a[0], b[0])
 
 
 def x_edges_inner(snapshot, mask, devices):
@@ -233,8 +249,8 @@
     )(snapshot, mask)
 
 
-def x_edges_halo(left, right, before, after):
-    shape = jax.ShapeDtypeStruct(before.shape, jnp.float32)
+def x_edges_halo(y_inner, y_outer, x_inner, x_outer):
+    shape = jax.ShapeDtypeStruct(x_inner.shape, jnp.float32)
     return pl.pallas_call(
         x_edges_halo_kernel,
         in_specs=[VMEM] * 4,
@@ -243,16 +259,16 @@
         input_output_aliases={2: 0, 3: 1},
         compiler_params=PARAMS,
         name="x_edges_halo",
-    )(left, right, before, after)
+    )(y_inner, y_outer, x_inner, x_outer)
 
 
 def lift_kernel(
     scales_ref,
     snapshot_ref,
-    left_ref,
-    right_ref,
-    before_ref,
-    after_ref,
+    y_inner_ref,
+    y_outer_ref,
+    x_inner_ref,
+    x_outer_ref,
     coefficients_hbm_ref,
     front_ref,
     back_ref,
@@ -280,6 +296,9 @@
     factor[8] = jnp.where(sub % 2 == 0, factor[8], scale[0])
     factor[4] = jnp.where(sub % 2 == 0, factor[4], scale[0])
 
+    even_gx, even_gy = is_even("gx"), is_even("gy")
+    left_held = (sub >= 4) & (gy > 0)
+    right_held = (sub < 4) & (gy < lax.axis_size("gy") - 1)
     half = rows // 2
     past_at, kept_at, after_at, before_at = range(half, half + 4)
 
@@ -308,9 +327,18 @@
         def entry(x, k):
             if 1 <= k <= count:
                 return snapshot_ref[x, span(k - 1), lanes]
-            tile = (left_ref if k == 0 else right_ref)[x % half, :, lanes]
+            inner, outer = y_inner_ref[x % half, :, lanes], y_outer_ref[x % half, :, lanes]
+            tile = jnp.where(even_gy if k == 0 else ~even_gy, outer, inner)
             tile = rolled(tile, 4) if x >= half else tile
-            return jnp.where(sub >= 4 if k == 0 else sub < 4, tile, 0.0)
+            return jnp.where(left_held if k == 0 else right_held, tile, 0.0)
+
+        def before(level, k):
+            inner, outer = x_inner_ref[level, span(k), lanes], x_outer_ref[level, span(k), lanes]
+            return jnp.where(even_gx, outer, inner)
+
+        def after(level, k):
+            inner, outer = x_inner_ref[level, span(k), lanes], x_outer_ref[level, span(k), lanes]
+            return jnp.where(even_gx, inner, outer)
 
         def step(c, s, beyond, ahead):
             held = sub % s == 0
@@ -339,17 +367,17 @@
 
         for k in range(count + 2):
             c = {x: entry(x, k) for x in range(rows)}
-            c = step(c, 1, after_ref[0, span(k), lanes], before_ref[0, span(k), lanes])
+            c = step(c, 1, after(0, k), before(0, k))
             for x in range(1, rows, 2):
                 store(x, k, c[x])
             for x in range(0, rows, 2):
                 work[x // 2, span(k)] = c[x]
-            work[past_at, span(k)] = after_ref[1, span(k), lanes] + (0.25 * x_right) * c[rows - 1]
-            work[kept_at, span(k)] = before_ref[1, span(k), lanes] + 0.25 * c[-1]
+            work[past_at, span(k)] = after(1, k) + (0.25 * x_right) * c[rows - 1]
+            work[kept_at, span(k)] = before(1, k) + 0.25 * c[-1]
         for at in range(half + 2):
             lift_row(held_at(at), put_at(at), 1)
-        lift_row(lambda k: after_ref[2, span(k), lanes], put_at(after_at), 1)
-        lift_row(lambda k: before_ref[2, span(k), lanes], put_at(before_at), 1)
+        lift_row(lambda k: after(2, k), put_at(after_at), 1)
+        lift_row(lambda k: before(2, k), put_at(before_at), 1)
         for k in range(count + 2):
             c = {x: work[x // 2, span(k)] for x in range(0, rows, 2)}
             past = work[past_at, span(k)]
@@ -381,7 +409,7 @@
             copy.wait()
 
 
-def lift(scales, snapshot, left, right, before, after):
+def lift(scales, snapshot, y_inner, y_outer, x_inner, x_outer):
     rows, cols, depth = snapshot.shape
     return pl.pallas_call(
         lift_kernel,
@@ -401,7 +429,7 @@
             flops=2 * 10**9, bytes_accessed=16 * 2**20, transcendentals=0
         ),
         name="lift",
-    )(scales, snapshot, left, right, before, after)
+    )(scales, snapshot, y_inner, y_outer, x_inner, x_outer)
 
 
 def pack_kernel(
@@ -544,18 +572,14 @@
     devices = lax.axis_size("gx") * lax.axis_size("gy")
     slots = rows * cols * width
     mask = keep_mask.transpose(0, 2, 1)
-    to_before, to_after = y_edges(snapshot)
-    right = shifted(to_before, "gy", -1)
-    left = shifted(to_after, "gy", 1)
-    x_before, x_after, own_counts, starts = x_edges_inner(snapshot, mask, devices)
+    y_halo = pairs_exchange(*y_edges(snapshot), "gy", ring=True)
+    x_inner, x_outer, own_counts, starts = x_edges_inner(snapshot, mask, devices)
     table = lax.all_to_all(own_counts.reshape(devices, 1, LANES), ALL, 0, 0, tiled=True)
     table = table.reshape(devices, LANES)
     flags = mask.reshape(rows, cols * width)
     scales = jnp.exp2(exponents.astype(jnp.float32))
-    x_before, x_after = x_edges_halo(left, right, x_before, x_after)
-    after = shifted(x_before, "gx", -1)
-    before = shifted(x_after, "gx", 1)
-    coefficients, front = lift(scales, snapshot, left, right, before, after)
+    x_halo = pairs_exchange(*x_edges_halo(*y_halo, x_inner, x_outer), "gx", ring=False)
+    coefficients, front = lift(scales, snapshot, *y_halo, *x_halo)
     packed, counts = pack(table, starts, coefficients, front, flags)
     share = slots // devices
     arrived = lax.all_to_all(packed.reshape(devices, share, LANES), ALL, 0, 0, tiled=True)

time: 115 us -> 109 us (0.948)
  starting transfers between devices: 22.7 us -> 18.1 us
  waiting for transfers between devices: 8.74 us -> 7.4 us
    ppermute x4, starting transfers between devices: 12.5 us -> 9.23 us  [pairs_exchange(): return (lax.ppermute(first, axis, inner), lax.ppermute(second, axis, outer))]
    all_to_all x1, starting transfers between devices: 10.3 us -> 8.89 us  [on_device(): lax.all_to_all(own_counts.reshape(devices, 1, LANES), ALL, 0, 0, tiled=True)]
    ppermute x4, waiting for transfers between devices: 3.23 us -> 2.02 us  [pairs_exchange(): return (lax.ppermute(first, axis, inner), lax.ppermute(second, axis, outer))]
  transfers between devices with their start and end apart: 5 -> 5, of which waited for: 2 -> 2; matrix products, arithmetic and copies ran while one was open for 0% -> 0% of each run, Pallas kernels for 4% -> 5%
where the time goes in v5:
time: 109 us
  blocking collectives  69.2 us (63%)
  starting transfers between devices  18.1 us (17%)
  Pallas kernels  10.3 us (9%)
  waiting for transfers between devices  7.4 us (7%)
  local copies, waits for them, and re-layouts  3.01 us (3%)
    all_to_all x1, blocking collectives, on_device(): lax.all_to_all(packed.reshape(devices, share, LANES), ALL, 0, 0, tiled=True)  35 us
    all_to_all x1, blocking collectives, on_device(): stream = lax.all_to_all(merged, ALL, 0, 0, tiled=True).reshape(slots, LANES)  34.2 us
    ppermute x4, starting transfers between devices, pairs_exchange(): return (lax.ppermute(first, axis, inner), lax.ppermute(second, axis, outer))  9.23 us
    all_to_all x1, starting transfers between devices, on_device(): lax.all_to_all(own_counts.reshape(devices, 1, LANES), ALL, 0, 0, tiled=True)  8.89 us
    all_to_all x1, waiting for transfers between devices, on_device(): lax.all_to_all(own_counts.reshape(devices, 1, LANES), ALL, 0, 0, tiled=True)  5.38 us
    pallas_call x1, Pallas kernels, lift(): pl.pallas_call(lift_kernel, in_specs=[SMEM] + [VMEM] * 5, out_specs=[pl.B...  4.1 us
    unnamed x9, local copies, waits for them, and re-layouts  2.92 us
    pallas_call x1, Pallas kernels, pack(): pl.pallas_call(pack_kernel, in_specs=[VMEM, SMEM, pl.BlockSpec(memory_spa...  2.64 us
  transfers between devices with their start and end apart: 5, of which 2 were waited for; matrix products, arithmetic and copies ran while one was open for 0% of the time, Pallas kernels for 5%

profile of v5, /device:TPU:1, one launch (start us, length us, event | category | flops | bytes accessed | tf_op | source)
XLA Modules:
  0.0 108.8 jit_solution(99171918181115934)
XLA Ops:
  0.6 0.0 copy-start
  0.6 1.6 %copy-done = f32[16,64,512]{2,1,0:T(8,128)S(1)} copy-done((f32[16,64,512]{2,1,0:T(8,128)S(1)}, f32[16,64,512]{2,1,0:T(8,128)}, u32[]{:S(2)}) %copy-start) | copy-done | bytes 2097176
  2.2 0.0 copy-start.2
  2.2 0.8 y_edges.1
  3.0 0.0 copy-start.3
  3.1 0.0 copy-start.1
  3.1 2.1 %collective-permute-start = (f32[8,8,512]{2,1,0:T(8,128)S(1)}, f32[8,8,512]{2,1,0:T(8,128)S(1)}, u32[]{:S(2)}, u32[]{:S(2)}) collective-permute-start(f32[8,8,512]{2,1,0:T(8,128)S(1)} %get-tuple-element.14), channel_id=1, source_target_pairs={{0,1},{1,0},{2,3},{3,2},{4,5},{5,4},{6,7},{7,6},{8,9},{9,8},{10,11... | collective-permute-start | bytes 393224 | tf_op jit(solution)/shard_map/ppermute | solution.py:22
  5.2 1.8 %collective-permute-start.1 = (f32[8,8,512]{2,1,0:T(8,128)S(1)}, f32[8,8,512]{2,1,0:T(8,128)S(1)}, u32[]{:S(2)}, u32[]{:S(2)}) collective-permute-start(f32[8,8,512]{2,1,0:T(8,128)S(1)} %get-tuple-element.15), channel_id=1, source_target_pairs={{0,3},{1,2},{2,1},{3,0},{4,7},{5,6},{6,5},{7,4},{8,11},{9,10},{10,... | collective-permute-start | bytes 393224 | tf_op jit(solution)/shard_map/ppermute | solution.py:22
  7.0 0.0 copy-done.2
  7.0 1.2 %x_edges_inner.1 = (f32[3,80,512]{2,1,0:T(8,128)S(1)}, f32[3,80,512]{2,1,0:T(8,128)S(1)}, s32[128,128]{1,0:T(8,128)}, s32[16,128]{1,0:T(8,128)S(1)}) custom-call(f32[16,64,512]{2,1,0:T(8,128)S(1)} %copy-done, s32[16,4,64]{2,1,0:T(4,128)S(1)} %bitcast.9), custom_call_target="tpu_custom_call" | custom-call | tf_op jit(solution)/shard_map/x_edges_inner/pallas_call | solution.py:237
  8.2 0.0 collective-permute-done.y_inner_ref
  8.2 2.0 %collective-permute-done.1.y_outer_ref = f32[8,8,512]{2,1,0:T(8,128)S(1)} collective-permute-done((f32[8,8,512]{2,1,0:T(8,128)S(1)}, f32[8,8,512]{2,1,0:T(8,128)S(1)}, u32[]{:S(2)}, u32[]{:S(2)}) %collective-permute-start.1) | collective-permute-done | bytes 131104 | tf_op jit(solution)/shard_map/ppermute | solution.py:22
  10.2 0.2 x_edges_halo.1
  10.4 2.2 %collective-permute-start.2 = (f32[3,80,512]{2,1,0:T(8,128)S(1)}, f32[3,80,512]{2,1,0:T(8,128)}, u32[]{:S(2)}, u32[]{:S(2)}) collective-permute-start(f32[3,80,512]{2,1,0:T(8,128)S(1)} %get-tuple-element.18), channel_id=1, source_target_pairs={{0,4},{4,0},{8,12},{12,8},{16,20},{20,16},{24,28},{28,24},{32,36},... | collective-permute-start | bytes 1474568 | tf_op jit(solution)/shard_map/ppermute | solution.py:22
  12.6 3.1 %collective-permute-start.3 = (f32[3,80,512]{2,1,0:T(8,128)S(1)}, f32[3,80,512]{2,1,0:T(8,128)}, u32[]{:S(2)}, u32[]{:S(2)}) collective-permute-start(f32[3,80,512]{2,1,0:T(8,128)S(1)} %get-tuple-element.19), channel_id=1, source_target_pairs={{4,8},{8,4},{12,16},{16,12},{20,24},{24,20},{28,32},{32,28},{36,40... | collective-permute-start | bytes 1474568 | tf_op jit(solution)/shard_map/ppermute | solution.py:22
  15.7 8.9 %all-to-all-start = ((s32[128,1,128]{2,1,0:T(1,128)}), s32[128,1,128]{2,1,0:T(1,128)S(1)}, u32[]{:S(2)}, u32[]{:S(2)}) async-start(s32[128,1,128]{2,1,0:T(1,128)} %bitcast.2), calls=%async_computation | async-start | bytes 131072 | tf_op jit(solution)/shard_map/all_to_all | solution.py:577
  24.6 0.1 reshape.21.flags_ref
  24.7 0.0 copy-done.3
  24.7 0.0 collective-permute-done.2.x_inner_ref
  24.7 0.0 collective-permute-done.3.x_outer_ref
  24.7 0.0 copy-done.1
  24.7 4.1 %lift.1 = (f32[16,64,512]{2,1,0:T(8,128)}, f32[8,64,512]{2,1,0:T(8,128)S(1)}) custom-call(f32[4]{0:T(128)S(1)} %multiply_exponential_fusion.scales_ref, f32[16,64,512]{2,1,0:T(8,128)S(1)} %copy-done.1, f32[8,8,512]{2,1,0:T(8,128)S(1)} %collective-permute-done.y_inner_ref, f32[8,8,512]{2,1,0:T(8,128)S(1)} %collective-permute-done.1.y_outer_ref, ...), custom_call_target="tpu_custom_call" | custom-call | flops 2000000000 | bytes 16777216 | tf_op jit(solution)/shard_map/lift/pallas_call | solution.py:414
  28.8 5.4 %all-to-all-done = s32[128,1,128]{2,1,0:T(1,128)S(1)} async-done(((s32[128,1,128]{2,1,0:T(1,128)}), s32[128,1,128]{2,1,0:T(1,128)S(1)}, u32[]{:S(2)}, u32[]{:S(2)}) %all-to-all-start) | async-done | bytes 65568 | tf_op jit(solution)/shard_map/all_to_all | solution.py:577
  34.2 2.6 %pack.1 = (f32[4096,128]{1,0:T(8,128)S(1)}, s32[1,128]{1,0:T(1,128)S(1)}) custom-call(s32[128,128]{1,0:T(8,128)S(1)} %bitcast.8, s32[16,128]{1,0:T(8,128)S(1)} %get-tuple-element.22.starts_ref, f32[16,64,512]{2,1,0:T(8,128)} %get-tuple-element.28.coefficients_hbm_ref, f32[8,64,512]{2,1,0:T(8,128)S(1)} %get-tuple-element.23.front_ref, ...), custom_call_target="tpu_custom_call" | custom-call | tf_op jit(solution)/shard_map/pack/pallas_call | solution.py:514
  36.8 35.0 %all_to_all.15.arrived_ref = f32[128,32,128]{2,1,0:T(8,128)S(1)} all-to-all(f32[128,32,128]{2,1,0:T(8,128)S(1)} %bitcast.7), channel_id=1, replica_groups=mesh['gx'=32,'gy'=4] {'gx','gy'}, dimensions={0} | all-to-all | bytes 4194304 | tf_op jit(solution)/shard_map/all_to_all | solution.py:585
  71.9 1.4 %merge.1 = f32[128,32,128]{2,1,0:T(8,128)S(1)} custom-call(s32[1,128]{1,0:T(1,128)S(1)} %get-tuple-element.24.counts_ref, f32[128,32,128]{2,1,0:T(8,128)S(1)} %all_to_all.15.arrived_ref), custom_call_target="tpu_custom_call" | custom-call | tf_op jit(solution)/shard_map/merge/pallas_call | solution.py:559
  73.3 34.2 %all_to_all.16 = f32[128,32,128]{2,1,0:T(8,128)S(1)} all-to-all(f32[128,32,128]{2,1,0:T(8,128)S(1)} %merge.1), channel_id=1, replica_groups=mesh['gx'=32,'gy'=4] {'gx','gy'}, dimensions={0} | all-to-all | bytes 4194304 | tf_op jit(solution)/shard_map/all_to_all | solution.py:587
  107.5 1.3 %copy.11 = f32[4096,128]{1,0:T(8,128)} copy(f32[4096,128]{1,0:T(8,128)S(1)} %bitcast.11) | data formatting | bytes 4194304
  (1 shorter events, 0.0 us)
Async XLA Ops:
  0.6 1.6 %copy-start = (f32[16,64,512]{2,1,0:T(8,128)S(1)}, f32[16,64,512]{2,1,0:T(8,128)}, u32[]{:S(2)}) copy-start(f32[16,64,512]{2,1,0:T(8,128)} %snapshot_ref.5) | copy-start | bytes 6291460
  2.2 4.8 %copy-start.2 = (s32[16,64,4]{1,2,0:T(4,128)S(1)}, s32[16,64,4]{1,2,0:T(4,128)}, u32[]{:S(2)}) copy-start(s32[16,64,4]{1,2,0:T(4,128)} %param.4) | copy-start | bytes 49156
  3.0 21.6 %copy-start.3 = (s32[4]{0:T(128)S(1)}, s32[4]{0:T(128)}, u32[]{:S(2)}) copy-start(s32[4]{0:T(128)} %param.5) | copy-start | bytes 52
  3.1 21.6 %copy-start.1 = (f32[16,64,512]{2,1,0:T(8,128)S(1)}, f32[16,64,512]{2,1,0:T(8,128)}, u32[]{:S(2)}) copy-start(f32[16,64,512]{2,1,0:T(8,128)} %snapshot_ref.5) | copy-start | bytes 6291460
  3.1 5.1 %collective-permute-start = (f32[8,8,512]{2,1,0:T(8,128)S(1)}, f32[8,8,512]{2,1,0:T(8,128)S(1)}, u32[]{:S(2)}, u32[]{:S(2)}) collective-permute-start(f32[8,8,512]{2,1,0:T(8,128)S(1)} %get-tuple-element.14), channel_id=1, source_target_pairs={{0,1},{1,0},{2,3},{3,2},{4,5},{5,4},{6,7},{7,6},{8,9},{9,8},{10,11... | collective-permute-start | bytes 393224 | tf_op jit(solution)/shard_map/ppermute | solution.py:22
  5.2 5.0 %collective-permute-start.1 = (f32[8,8,512]{2,1,0:T(8,128)S(1)}, f32[8,8,512]{2,1,0:T(8,128)S(1)}, u32[]{:S(2)}, u32[]{:S(2)}) collective-permute-start(f32[8,8,512]{2,1,0:T(8,128)S(1)} %get-tuple-element.15), channel_id=1, source_target_pairs={{0,3},{1,2},{2,1},{3,0},{4,7},{5,6},{6,5},{7,4},{8,11},{9,10},{10,... | collective-permute-start | bytes 393224 | tf_op jit(solution)/shard_map/ppermute | solution.py:22
  10.4 14.3 %collective-permute-start.2 = (f32[3,80,512]{2,1,0:T(8,128)S(1)}, f32[3,80,512]{2,1,0:T(8,128)}, u32[]{:S(2)}, u32[]{:S(2)}) collective-permute-start(f32[3,80,512]{2,1,0:T(8,128)S(1)} %get-tuple-element.18), channel_id=1, source_target_pairs={{0,4},{4,0},{8,12},{12,8},{16,20},{20,16},{24,28},{28,24},{32,36},... | collective-permute-start | bytes 1474568 | tf_op jit(solution)/shard_map/ppermute | solution.py:22
  12.6 12.1 %collective-permute-start.3 = (f32[3,80,512]{2,1,0:T(8,128)S(1)}, f32[3,80,512]{2,1,0:T(8,128)}, u32[]{:S(2)}, u32[]{:S(2)}) collective-permute-start(f32[3,80,512]{2,1,0:T(8,128)S(1)} %get-tuple-element.19), channel_id=1, source_target_pairs={{4,8},{8,4},{12,16},{16,12},{20,24},{24,20},{28,32},{32,28},{36,40... | collective-permute-start | bytes 1474568 | tf_op jit(solution)/shard_map/ppermute | solution.py:22
  15.7 18.5 %all-to-all-start = ((s32[128,1,128]{2,1,0:T(1,128)}), s32[128,1,128]{2,1,0:T(1,128)S(1)}, u32[]{:S(2)}, u32[]{:S(2)}) async-start(s32[128,1,128]{2,1,0:T(1,128)} %bitcast.2), calls=%async_computation | async-start | bytes 131072 | tf_op jit(solution)/shard_map/all_to_all | solution.py:577

commit v6 on v5

--- a/solution.py
+++ b/solution.py
@@ -8,6 +8,7 @@
 ALL = ("gx", "gy")
 SUB = 8
 LANES = 128
+EDGE_LIMIT = 50 * 2**20
 PACK_LIMIT = 50 * 2**20
 VMEM = pl.BlockSpec(memory_space=pltpu.VMEM)
 SMEM = pl.BlockSpec(memory_space=pltpu.SMEM)
@@ -127,9 +128,16 @@
     counts_ref[...] = jnp.broadcast_to(total, counts_ref.shape)
 
 
-def y_edges_kernel(snapshot_ref, inner_ref, outer_ref):
+def y_edges_kernel(source_ref, inner_ref, outer_ref, snapshot_ref, sems):
     rows, cols, depth = snapshot_ref.shape
     half = rows // 2
+    cuts = [(0, SUB), (cols - 2 * SUB, cols), (SUB, cols - 2 * SUB)]
+    copies = [
+        pltpu.make_async_copy(source_ref.at[:, a:b, :], snapshot_ref.at[:, a:b, :], sems.at[k])
+        for k, (a, b) in enumerate(cuts)
+    ]
+    for copy in copies:
+        copy.start()
     even_gy = is_even("gy")
     sub = sublane()
     zero = jnp.zeros((SUB, LANES), jnp.float32)
@@ -162,6 +170,9 @@
             sub == 7, first, jnp.where(sub == 6, second, jnp.where(sub == 4, third, 0.0))
         )
 
+    for copy in copies[:2]:
+        copy.wait()
+
     @pl.loop(0, half)
     def _(x):
         for t in range(depth // LANES):
@@ -171,16 +182,19 @@
             inner_ref[x, :, lanes] = jnp.where(even_gy, to_after, to_before)
             outer_ref[x, :, lanes] = jnp.where(even_gy, to_before, to_after)
 
+    copies[2].wait()
+
 
 def y_edges(snapshot):
     rows, cols, depth = snapshot.shape
     shape = jax.ShapeDtypeStruct((rows // 2, SUB, depth), jnp.float32)
     return pl.pallas_call(
         y_edges_kernel,
-        in_specs=[VMEM],
-        out_specs=[VMEM] * 2,
-        out_shape=[shape] * 2,
-        compiler_params=PARAMS,
+        in_specs=[pl.BlockSpec(memory_space=pltpu.HBM)],
+        out_specs=[VMEM] * 3,
+        out_shape=[shape, shape, jax.ShapeDtypeStruct(snapshot.shape, jnp.float32)],
+        scratch_shapes=[pltpu.SemaphoreType.DMA((3,))],
+        compiler_params=pltpu.CompilerParams(vmem_limit_bytes=EDGE_LIMIT),
         name="y_edges",
     )(snapshot)
 
@@ -572,8 +586,9 @@
     devices = lax.axis_size("gx") * lax.axis_size("gy")
     slots = rows * cols * width
     mask = keep_mask.transpose(0, 2, 1)
-    y_halo = pairs_exchange(*y_edges(snapshot), "gy", ring=True)
-    x_inner, x_outer, own_counts, starts = x_edges_inner(snapshot, mask, devices)
+    y_inner, y_outer, held = y_edges(snapshot)
+    y_halo = pairs_exchange(y_inner, y_outer, "gy", ring=True)
+    x_inner, x_outer, own_counts, starts = x_edges_inner(held, mask, devices)
     table = lax.all_to_all(own_counts.reshape(devices, 1, LANES), ALL, 0, 0, tiled=True)
     table = table.reshape(devices, LANES)
     flags = mask.reshape(rows, cols * width)

time: 109 us -> 109 us (level)
  local copies, waits for them, and re-layouts: 3.01 us -> 1.42 us
  Pallas kernels: 10.3 us -> 11.4 us
    unnamed x9 -> x7, local copies, waits for them, and re-layouts: 2.92 us -> 1.34 us
    pallas_call x1, Pallas kernels: 0.81 us -> 1.97 us  [y_edges(): pl.pallas_call(y_edges_kernel, in_specs=[pl.BlockSpec(memory_space=pltpu....]
where the time goes in v6:
time: 109 us; the launch traced here: 108 us
  blocking collectives  69.2 us (63%)
  starting transfers between devices  18.1 us (17%)
  Pallas kernels  11.4 us (10%)
  waiting for transfers between devices  7.4 us (7%)
  local copies, waits for them, and re-layouts  1.42 us (1%)
    all_to_all x1, blocking collectives, on_device(): lax.all_to_all(packed.reshape(devices, share, LANES), ALL, 0, 0, tiled=True)  35 us
    all_to_all x1, blocking collectives, on_device(): stream = lax.all_to_all(merged, ALL, 0, 0, tiled=True).reshape(slots, LANES)  34.2 us
    ppermute x4, starting transfers between devices, pairs_exchange(): return (lax.ppermute(first, axis, inner), lax.ppermute(second, axis, outer))  9.23 us
    all_to_all x1, starting transfers between devices, on_device(): lax.all_to_all(own_counts.reshape(devices, 1, LANES), ALL, 0, 0, tiled=True)  8.89 us
    all_to_all x1, waiting for transfers between devices, on_device(): lax.all_to_all(own_counts.reshape(devices, 1, LANES), ALL, 0, 0, tiled=True)  5.38 us
    pallas_call x1, Pallas kernels, lift(): pl.pallas_call(lift_kernel, in_specs=[SMEM] + [VMEM] * 5, out_specs=[pl.B...  4.1 us
    pallas_call x1, Pallas kernels, pack(): pl.pallas_call(pack_kernel, in_specs=[VMEM, SMEM, pl.BlockSpec(memory_spa...  2.64 us
  transfers between devices with their start and end apart: 5, of which 2 were waited for; matrix products, arithmetic and copies ran while one was open for 0% of the time, Pallas kernels for 5%

profile of v6, /device:TPU:1, one launch (start us, length us, event | category | flops | bytes accessed | tf_op | source)
XLA Modules:
  0.0 108.3 jit_solution(12065533939101518683)
XLA Ops:
  0.6 0.0 copy-start.1
  0.6 2.0 %y_edges.1 = (f32[8,8,512]{2,1,0:T(8,128)S(1)}, f32[8,8,512]{2,1,0:T(8,128)S(1)}, f32[16,64,512]{2,1,0:T(8,128)S(1)}) custom-call(f32[16,64,512]{2,1,0:T(8,128)} %snapshot_ref.1), custom_call_target="tpu_custom_call" | custom-call | tf_op jit(solution)/shard_map/y_edges/pallas_call | solution.py:191
  2.6 0.0 copy-start.2
  2.6 0.0 copy-start
  2.6 2.1 %collective-permute-start = (f32[8,8,512]{2,1,0:T(8,128)S(1)}, f32[8,8,512]{2,1,0:T(8,128)S(1)}, u32[]{:S(2)}, u32[]{:S(2)}) collective-permute-start(f32[8,8,512]{2,1,0:T(8,128)S(1)} %get-tuple-element.15), channel_id=1, source_target_pairs={{0,1},{1,0},{2,3},{3,2},{4,5},{5,4},{6,7},{7,6},{8,9},{9,8},{10,11... | collective-permute-start | bytes 393224 | tf_op jit(solution)/shard_map/ppermute | solution.py:23
  4.8 1.8 %collective-permute-start.1 = (f32[8,8,512]{2,1,0:T(8,128)S(1)}, f32[8,8,512]{2,1,0:T(8,128)S(1)}, u32[]{:S(2)}, u32[]{:S(2)}) collective-permute-start(f32[8,8,512]{2,1,0:T(8,128)S(1)} %get-tuple-element.16), channel_id=1, source_target_pairs={{0,3},{1,2},{2,1},{3,0},{4,7},{5,6},{6,5},{7,4},{8,11},{9,10},{10,... | collective-permute-start | bytes 393224 | tf_op jit(solution)/shard_map/ppermute | solution.py:23
  6.6 0.0 copy-done.1
  6.6 1.2 %x_edges_inner.1 = (f32[3,80,512]{2,1,0:T(8,128)S(1)}, f32[3,80,512]{2,1,0:T(8,128)S(1)}, s32[128,128]{1,0:T(8,128)}, s32[16,128]{1,0:T(8,128)S(1)}) custom-call(f32[16,64,512]{2,1,0:T(8,128)S(1)} %get-tuple-element.17.snapshot_ref, s32[16,4,64]{2,1,0:T(4,128)S(1)} %bitcast.9), custom_call_target="tpu_custom_call" | custom-call | tf_op jit(solution)/shard_map/x_edges_inner/pallas_call | solution.py:251
  7.8 0.0 collective-permute-done.y_inner_ref
  7.8 2.0 %collective-permute-done.1.y_outer_ref = f32[8,8,512]{2,1,0:T(8,128)S(1)} collective-permute-done((f32[8,8,512]{2,1,0:T(8,128)S(1)}, f32[8,8,512]{2,1,0:T(8,128)S(1)}, u32[]{:S(2)}, u32[]{:S(2)}) %collective-permute-start.1) | collective-permute-done | bytes 131104 | tf_op jit(solution)/shard_map/ppermute | solution.py:23
  9.8 0.2 x_edges_halo.1
  10.0 2.2 %collective-permute-start.2 = (f32[3,80,512]{2,1,0:T(8,128)S(1)}, f32[3,80,512]{2,1,0:T(8,128)}, u32[]{:S(2)}, u32[]{:S(2)}) collective-permute-start(f32[3,80,512]{2,1,0:T(8,128)S(1)} %get-tuple-element.20), channel_id=1, source_target_pairs={{0,4},{4,0},{8,12},{12,8},{16,20},{20,16},{24,28},{28,24},{32,36},... | collective-permute-start | bytes 1474568 | tf_op jit(solution)/shard_map/ppermute | solution.py:23
  12.1 3.1 %collective-permute-start.3 = (f32[3,80,512]{2,1,0:T(8,128)S(1)}, f32[3,80,512]{2,1,0:T(8,128)}, u32[]{:S(2)}, u32[]{:S(2)}) collective-permute-start(f32[3,80,512]{2,1,0:T(8,128)S(1)} %get-tuple-element.21), channel_id=1, source_target_pairs={{4,8},{8,4},{12,16},{16,12},{20,24},{24,20},{28,32},{32,28},{36,40... | collective-permute-start | bytes 1474568 | tf_op jit(solution)/shard_map/ppermute | solution.py:23
  15.2 8.9 %all-to-all-start = ((s32[128,1,128]{2,1,0:T(1,128)}), s32[128,1,128]{2,1,0:T(1,128)S(1)}, u32[]{:S(2)}, u32[]{:S(2)}) async-start(s32[128,1,128]{2,1,0:T(1,128)} %bitcast.2), calls=%async_computation | async-start | bytes 131072 | tf_op jit(solution)/shard_map/all_to_all | solution.py:592
  24.1 0.1 reshape.21.flags_ref
  24.2 0.0 copy-done.2
  24.2 0.0 collective-permute-done.2.x_inner_ref
  24.3 0.0 collective-permute-done.3.x_outer_ref
  24.3 0.0 copy-done
  24.3 4.1 %lift.1 = (f32[16,64,512]{2,1,0:T(8,128)}, f32[8,64,512]{2,1,0:T(8,128)S(1)}) custom-call(f32[4]{0:T(128)S(1)} %multiply_exponential_fusion.scales_ref, f32[16,64,512]{2,1,0:T(8,128)S(1)} %copy-done, f32[8,8,512]{2,1,0:T(8,128)S(1)} %collective-permute-done.y_inner_ref, f32[8,8,512]{2,1,0:T(8,128)S(1)} %collective-permute-done.1.y_outer_ref, ...), custom_call_target="tpu_custom_call" | custom-call | flops 2000000000 | bytes 16777216 | tf_op jit(solution)/shard_map/lift/pallas_call | solution.py:428
  28.4 5.4 %all-to-all-done = s32[128,1,128]{2,1,0:T(1,128)S(1)} async-done(((s32[128,1,128]{2,1,0:T(1,128)}), s32[128,1,128]{2,1,0:T(1,128)S(1)}, u32[]{:S(2)}, u32[]{:S(2)}) %all-to-all-start) | async-done | bytes 65568 | tf_op jit(solution)/shard_map/all_to_all | solution.py:592
  33.8 2.6 %pack.1 = (f32[4096,128]{1,0:T(8,128)S(1)}, s32[1,128]{1,0:T(1,128)S(1)}) custom-call(s32[128,128]{1,0:T(8,128)S(1)} %bitcast.8, s32[16,128]{1,0:T(8,128)S(1)} %get-tuple-element.24.starts_ref, f32[16,64,512]{2,1,0:T(8,128)} %get-tuple-element.30.coefficients_hbm_ref, f32[8,64,512]{2,1,0:T(8,128)S(1)} %get-tuple-element.25.front_ref, ...), custom_call_target="tpu_custom_call" | custom-call | tf_op jit(solution)/shard_map/pack/pallas_call | solution.py:528
  36.4 35.0 %all_to_all.15.arrived_ref = f32[128,32,128]{2,1,0:T(8,128)S(1)} all-to-all(f32[128,32,128]{2,1,0:T(8,128)S(1)} %bitcast.7), channel_id=1, replica_groups=mesh['gx'=32,'gy'=4] {'gx','gy'}, dimensions={0} | all-to-all | bytes 4194304 | tf_op jit(solution)/shard_map/all_to_all | solution.py:600
  71.4 1.4 %merge.1 = f32[128,32,128]{2,1,0:T(8,128)S(1)} custom-call(s32[1,128]{1,0:T(1,128)S(1)} %get-tuple-element.26.counts_ref, f32[128,32,128]{2,1,0:T(8,128)S(1)} %all_to_all.15.arrived_ref), custom_call_target="tpu_custom_call" | custom-call | tf_op jit(solution)/shard_map/merge/pallas_call | solution.py:573
  72.8 34.2 %all_to_all.16 = f32[128,32,128]{2,1,0:T(8,128)S(1)} all-to-all(f32[128,32,128]{2,1,0:T(8,128)S(1)} %merge.1), channel_id=1, replica_groups=mesh['gx'=32,'gy'=4] {'gx','gy'}, dimensions={0} | all-to-all | bytes 4194304 | tf_op jit(solution)/shard_map/all_to_all | solution.py:602
  107.0 1.3 %copy.11 = f32[4096,128]{1,0:T(8,128)} copy(f32[4096,128]{1,0:T(8,128)S(1)} %bitcast.11) | data formatting | bytes 4194304
  (1 shorter events, 0.0 us)
Async XLA Ops:
  0.6 5.9 %copy-start.1 = (s32[16,64,4]{1,2,0:T(4,128)S(1)}, s32[16,64,4]{1,2,0:T(4,128)}, u32[]{:S(2)}) copy-start(s32[16,64,4]{1,2,0:T(4,128)} %param.4) | copy-start | bytes 49156
  2.6 21.6 %copy-start.2 = (s32[4]{0:T(128)S(1)}, s32[4]{0:T(128)}, u32[]{:S(2)}) copy-start(s32[4]{0:T(128)} %param.5) | copy-start | bytes 52
  2.6 21.6 %copy-start = (f32[16,64,512]{2,1,0:T(8,128)S(1)}, f32[16,64,512]{2,1,0:T(8,128)}, u32[]{:S(2)}) copy-start(f32[16,64,512]{2,1,0:T(8,128)} %snapshot_ref.1) | copy-start | bytes 6291460
  2.6 5.1 %collective-permute-start = (f32[8,8,512]{2,1,0:T(8,128)S(1)}, f32[8,8,512]{2,1,0:T(8,128)S(1)}, u32[]{:S(2)}, u32[]{:S(2)}) collective-permute-start(f32[8,8,512]{2,1,0:T(8,128)S(1)} %get-tuple-element.15), channel_id=1, source_target_pairs={{0,1},{1,0},{2,3},{3,2},{4,5},{5,4},{6,7},{7,6},{8,9},{9,8},{10,11... | collective-permute-start | bytes 393224 | tf_op jit(solution)/shard_map/ppermute | solution.py:23
  4.8 5.0 %collective-permute-start.1 = (f32[8,8,512]{2,1,0:T(8,128)S(1)}, f32[8,8,512]{2,1,0:T(8,128)S(1)}, u32[]{:S(2)}, u32[]{:S(2)}) collective-permute-start(f32[8,8,512]{2,1,0:T(8,128)S(1)} %get-tuple-element.16), channel_id=1, source_target_pairs={{0,3},{1,2},{2,1},{3,0},{4,7},{5,6},{6,5},{7,4},{8,11},{9,10},{10,... | collective-permute-start | bytes 393224 | tf_op jit(solution)/shard_map/ppermute | solution.py:23
  10.0 14.3 %collective-permute-start.2 = (f32[3,80,512]{2,1,0:T(8,128)S(1)}, f32[3,80,512]{2,1,0:T(8,128)}, u32[]{:S(2)}, u32[]{:S(2)}) collective-permute-start(f32[3,80,512]{2,1,0:T(8,128)S(1)} %get-tuple-element.20), channel_id=1, source_target_pairs={{0,4},{4,0},{8,12},{12,8},{16,20},{20,16},{24,28},{28,24},{32,36},... | collective-permute-start | bytes 1474568 | tf_op jit(solution)/shard_map/ppermute | solution.py:23
  12.1 12.1 %collective-permute-start.3 = (f32[3,80,512]{2,1,0:T(8,128)S(1)}, f32[3,80,512]{2,1,0:T(8,128)}, u32[]{:S(2)}, u32[]{:S(2)}) collective-permute-start(f32[3,80,512]{2,1,0:T(8,128)S(1)} %get-tuple-element.21), channel_id=1, source_target_pairs={{4,8},{8,4},{12,16},{16,12},{20,24},{24,20},{28,32},{32,28},{36,40... | collective-permute-start | bytes 1474568 | tf_op jit(solution)/shard_map/ppermute | solution.py:23
  15.2 18.5 %all-to-all-start = ((s32[128,1,128]{2,1,0:T(1,128)}), s32[128,1,128]{2,1,0:T(1,128)S(1)}, u32[]{:S(2)}, u32[]{:S(2)}) async-start(s32[128,1,128]{2,1,0:T(1,128)} %bitcast.2), calls=%async_computation | async-start | bytes 131072 | tf_op jit(solution)/shard_map/all_to_all | solution.py:592

commit v7 on v6

--- a/solution.py
+++ b/solution.py
@@ -348,11 +348,11 @@
 
         def before(level, k):
             inner, outer = x_inner_ref[level, span(k), lanes], x_outer_ref[level, span(k), lanes]
-            return jnp.where(even_gx, outer, inner)
+            return jnp.where(gx > 0, jnp.where(even_gx, outer, inner), 0.0)
 
         def after(level, k):
             inner, outer = x_inner_ref[level, span(k), lanes], x_outer_ref[level, span(k), lanes]
-            return jnp.where(even_gx, inner, outer)
+            return jnp.where(gx < lax.axis_size("gx") - 1, jnp.where(even_gx, inner, outer), 0.0)
 
         def step(c, s, beyond, ahead):
             held = sub % s == 0
@@ -593,7 +593,7 @@
     table = table.reshape(devices, LANES)
     flags = mask.reshape(rows, cols * width)
     scales = jnp.exp2(exponents.astype(jnp.float32))
-    x_halo = pairs_exchange(*x_edges_halo(*y_halo, x_inner, x_outer), "gx", ring=False)
+    x_halo = pairs_exchange(*x_edges_halo(*y_halo, x_inner, x_outer), "gx", ring=True)
     coefficients, front = lift(scales, snapshot, *y_halo, *x_halo)
     packed, counts = pack(table, starts, coefficients, front, flags)
     share = slots // devices

time: 109 us -> 108 us (level)
  starting transfers between devices: 18.1 us -> 16.3 us
  blocking collectives: 69.2 us -> 70.7 us
    ppermute x4, starting transfers between devices: 9.23 us -> 7.4 us  [pairs_exchange(): return (lax.ppermute(first, axis, inner), lax.ppermute(second, axis, outer))]
    all_to_all x1, blocking collectives: 35 us -> 36.5 us  [on_device(): lax.all_to_all(packed.reshape(devices, share, LANES), ALL, 0, 0, tiled=True)]
where the time goes in v7:
time: 108 us
  blocking collectives  70.7 us (65%)
  starting transfers between devices  16.3 us (15%)
  Pallas kernels  11.5 us (11%)
  waiting for transfers between devices  7.39 us (7%)
  local copies, waits for them, and re-layouts  1.42 us (1%)
    all_to_all x1, blocking collectives, on_device(): lax.all_to_all(packed.reshape(devices, share, LANES), ALL, 0, 0, tiled=True)  36.5 us
    all_to_all x1, blocking collectives, on_device(): stream = lax.all_to_all(merged, ALL, 0, 0, tiled=True).reshape(slots, LANES)  34.2 us
    all_to_all x1, starting transfers between devices, on_device(): lax.all_to_all(own_counts.reshape(devices, 1, LANES), ALL, 0, 0, tiled=True)  8.88 us
    ppermute x4, starting transfers between devices, pairs_exchange(): return (lax.ppermute(first, axis, inner), lax.ppermute(second, axis, outer))  7.4 us
    all_to_all x1, waiting for transfers between devices, on_device(): lax.all_to_all(own_counts.reshape(devices, 1, LANES), ALL, 0, 0, tiled=True)  5.36 us
    pallas_call x1, Pallas kernels, lift(): pl.pallas_call(lift_kernel, in_specs=[SMEM] + [VMEM] * 5, out_specs=[pl.B...  4.12 us
    pallas_call x1, Pallas kernels, pack(): pl.pallas_call(pack_kernel, in_specs=[VMEM, SMEM, pl.BlockSpec(memory_spa...  2.63 us
  transfers between devices with their start and end apart: 5, of which 2 were waited for; matrix products, arithmetic and copies ran while one was open for 0% of the time, Pallas kernels for 5%

profile of v7, /device:TPU:1, one launch (start us, length us, event | category | flops | bytes accessed | tf_op | source)
XLA Modules:
  0.0 107.9 jit_solution(15812213686780237190)
XLA Ops:
  0.6 0.0 copy-start.1
  0.6 2.0 %y_edges.1 = (f32[8,8,512]{2,1,0:T(8,128)S(1)}, f32[8,8,512]{2,1,0:T(8,128)S(1)}, f32[16,64,512]{2,1,0:T(8,128)S(1)}) custom-call(f32[16,64,512]{2,1,0:T(8,128)} %snapshot_ref.1), custom_call_target="tpu_custom_call" | custom-call | tf_op jit(solution)/shard_map/y_edges/pallas_call | solution.py:191
  2.6 0.0 copy-start.2
  2.6 0.0 copy-start
  2.6 2.1 %collective-permute-start = (f32[8,8,512]{2,1,0:T(8,128)S(1)}, f32[8,8,512]{2,1,0:T(8,128)S(1)}, u32[]{:S(2)}, u32[]{:S(2)}) collective-permute-start(f32[8,8,512]{2,1,0:T(8,128)S(1)} %get-tuple-element.15), channel_id=1, source_target_pairs={{0,1},{1,0},{2,3},{3,2},{4,5},{5,4},{6,7},{7,6},{8,9},{9,8},{10,11... | collective-permute-start | bytes 393224 | tf_op jit(solution)/shard_map/ppermute | solution.py:23
  4.8 1.8 %collective-permute-start.1 = (f32[8,8,512]{2,1,0:T(8,128)S(1)}, f32[8,8,512]{2,1,0:T(8,128)S(1)}, u32[]{:S(2)}, u32[]{:S(2)}) collective-permute-start(f32[8,8,512]{2,1,0:T(8,128)S(1)} %get-tuple-element.16), channel_id=1, source_target_pairs={{0,3},{1,2},{2,1},{3,0},{4,7},{5,6},{6,5},{7,4},{8,11},{9,10},{10,... | collective-permute-start | bytes 393224 | tf_op jit(solution)/shard_map/ppermute | solution.py:23
  6.6 0.0 copy-done.1
  6.6 1.2 %x_edges_inner.1 = (f32[3,80,512]{2,1,0:T(8,128)S(1)}, f32[3,80,512]{2,1,0:T(8,128)S(1)}, s32[128,128]{1,0:T(8,128)}, s32[16,128]{1,0:T(8,128)S(1)}) custom-call(f32[16,64,512]{2,1,0:T(8,128)S(1)} %get-tuple-element.17.snapshot_ref, s32[16,4,64]{2,1,0:T(4,128)S(1)} %bitcast.9), custom_call_target="tpu_custom_call" | custom-call | tf_op jit(solution)/shard_map/x_edges_inner/pallas_call | solution.py:251
  7.8 0.0 collective-permute-done.y_inner_ref
  7.8 2.0 %collective-permute-done.1.y_outer_ref = f32[8,8,512]{2,1,0:T(8,128)S(1)} collective-permute-done((f32[8,8,512]{2,1,0:T(8,128)S(1)}, f32[8,8,512]{2,1,0:T(8,128)S(1)}, u32[]{:S(2)}, u32[]{:S(2)}) %collective-permute-start.1) | collective-permute-done | bytes 131104 | tf_op jit(solution)/shard_map/ppermute | solution.py:23
  9.8 0.2 x_edges_halo.1
  10.0 2.2 %collective-permute-start.2 = (f32[3,80,512]{2,1,0:T(8,128)S(1)}, f32[3,80,512]{2,1,0:T(8,128)}, u32[]{:S(2)}, u32[]{:S(2)}) collective-permute-start(f32[3,80,512]{2,1,0:T(8,128)S(1)} %get-tuple-element.20), channel_id=1, source_target_pairs={{0,4},{4,0},{8,12},{12,8},{16,20},{20,16},{24,28},{28,24},{32,36},... | collective-permute-start | bytes 1474568 | tf_op jit(solution)/shard_map/ppermute | solution.py:23
  12.1 1.3 %collective-permute-start.3 = (f32[3,80,512]{2,1,0:T(8,128)S(1)}, f32[3,80,512]{2,1,0:T(8,128)}, u32[]{:S(2)}, u32[]{:S(2)}) collective-permute-start(f32[3,80,512]{2,1,0:T(8,128)S(1)} %get-tuple-element.21), channel_id=1, source_target_pairs={{0,124},{4,8},{8,4},{12,16},{16,12},{20,24},{24,20},{28,32},{32,28... | collective-permute-start | bytes 1474568 | tf_op jit(solution)/shard_map/ppermute | solution.py:23
  13.4 8.9 %all-to-all-start = ((s32[128,1,128]{2,1,0:T(1,128)}), s32[128,1,128]{2,1,0:T(1,128)S(1)}, u32[]{:S(2)}, u32[]{:S(2)}) async-start(s32[128,1,128]{2,1,0:T(1,128)} %bitcast.2), calls=%async_computation | async-start | bytes 131072 | tf_op jit(solution)/shard_map/all_to_all | solution.py:592
  22.3 0.1 reshape.21.flags_ref
  22.4 0.0 copy-done.2
  22.4 0.0 collective-permute-done.2.x_inner_ref
  22.4 0.0 collective-permute-done.3.x_outer_ref
  22.4 0.0 copy-done
  22.4 4.1 %lift.1 = (f32[16,64,512]{2,1,0:T(8,128)}, f32[8,64,512]{2,1,0:T(8,128)S(1)}) custom-call(f32[4]{0:T(128)S(1)} %multiply_exponential_fusion.scales_ref, f32[16,64,512]{2,1,0:T(8,128)S(1)} %copy-done, f32[8,8,512]{2,1,0:T(8,128)S(1)} %collective-permute-done.y_inner_ref, f32[8,8,512]{2,1,0:T(8,128)S(1)} %collective-permute-done.1.y_outer_ref, ...), custom_call_target="tpu_custom_call" | custom-call | flops 2000000000 | bytes 16777216 | tf_op jit(solution)/shard_map/lift/pallas_call | solution.py:428
  26.6 5.4 %all-to-all-done = s32[128,1,128]{2,1,0:T(1,128)S(1)} async-done(((s32[128,1,128]{2,1,0:T(1,128)}), s32[128,1,128]{2,1,0:T(1,128)S(1)}, u32[]{:S(2)}, u32[]{:S(2)}) %all-to-all-start) | async-done | bytes 65568 | tf_op jit(solution)/shard_map/all_to_all | solution.py:592
  31.9 2.6 %pack.1 = (f32[4096,128]{1,0:T(8,128)S(1)}, s32[1,128]{1,0:T(1,128)S(1)}) custom-call(s32[128,128]{1,0:T(8,128)S(1)} %bitcast.8, s32[16,128]{1,0:T(8,128)S(1)} %get-tuple-element.24.starts_ref, f32[16,64,512]{2,1,0:T(8,128)} %get-tuple-element.30.coefficients_hbm_ref, f32[8,64,512]{2,1,0:T(8,128)S(1)} %get-tuple-element.25.front_ref, ...), custom_call_target="tpu_custom_call" | custom-call | tf_op jit(solution)/shard_map/pack/pallas_call | solution.py:528
  34.6 36.5 %all_to_all.15.arrived_ref = f32[128,32,128]{2,1,0:T(8,128)S(1)} all-to-all(f32[128,32,128]{2,1,0:T(8,128)S(1)} %bitcast.7), channel_id=1, replica_groups=mesh['gx'=32,'gy'=4] {'gx','gy'}, dimensions={0} | all-to-all | bytes 4194304 | tf_op jit(solution)/shard_map/all_to_all | solution.py:600
  71.0 1.4 %merge.1 = f32[128,32,128]{2,1,0:T(8,128)S(1)} custom-call(s32[1,128]{1,0:T(1,128)S(1)} %get-tuple-element.26.counts_ref, f32[128,32,128]{2,1,0:T(8,128)S(1)} %all_to_all.15.arrived_ref), custom_call_target="tpu_custom_call" | custom-call | tf_op jit(solution)/shard_map/merge/pallas_call | solution.py:573
  72.4 34.2 %all_to_all.16 = f32[128,32,128]{2,1,0:T(8,128)S(1)} all-to-all(f32[128,32,128]{2,1,0:T(8,128)S(1)} %merge.1), channel_id=1, replica_groups=mesh['gx'=32,'gy'=4] {'gx','gy'}, dimensions={0} | all-to-all | bytes 4194304 | tf_op jit(solution)/shard_map/all_to_all | solution.py:602
  106.6 1.3 %copy.11 = f32[4096,128]{1,0:T(8,128)} copy(f32[4096,128]{1,0:T(8,128)S(1)} %bitcast.11) | data formatting | bytes 4194304
  (1 shorter events, 0.0 us)
Async XLA Ops:
  0.6 5.9 %copy-start.1 = (s32[16,64,4]{1,2,0:T(4,128)S(1)}, s32[16,64,4]{1,2,0:T(4,128)}, u32[]{:S(2)}) copy-start(s32[16,64,4]{1,2,0:T(4,128)} %param.4) | copy-start | bytes 49156
  2.6 19.8 %copy-start.2 = (s32[4]{0:T(128)S(1)}, s32[4]{0:T(128)}, u32[]{:S(2)}) copy-start(s32[4]{0:T(128)} %param.5) | copy-start | bytes 52
  2.6 19.8 %copy-start = (f32[16,64,512]{2,1,0:T(8,128)S(1)}, f32[16,64,512]{2,1,0:T(8,128)}, u32[]{:S(2)}) copy-start(f32[16,64,512]{2,1,0:T(8,128)} %snapshot_ref.1) | copy-start | bytes 6291460
  2.6 5.1 %collective-permute-start = (f32[8,8,512]{2,1,0:T(8,128)S(1)}, f32[8,8,512]{2,1,0:T(8,128)S(1)}, u32[]{:S(2)}, u32[]{:S(2)}) collective-permute-start(f32[8,8,512]{2,1,0:T(8,128)S(1)} %get-tuple-element.15), channel_id=1, source_target_pairs={{0,1},{1,0},{2,3},{3,2},{4,5},{5,4},{6,7},{7,6},{8,9},{9,8},{10,11... | collective-permute-start | bytes 393224 | tf_op jit(solution)/shard_map/ppermute | solution.py:23
  4.8 5.0 %collective-permute-start.1 = (f32[8,8,512]{2,1,0:T(8,128)S(1)}, f32[8,8,512]{2,1,0:T(8,128)S(1)}, u32[]{:S(2)}, u32[]{:S(2)}) collective-permute-start(f32[8,8,512]{2,1,0:T(8,128)S(1)} %get-tuple-element.16), channel_id=1, source_target_pairs={{0,3},{1,2},{2,1},{3,0},{4,7},{5,6},{6,5},{7,4},{8,11},{9,10},{10,... | collective-permute-start | bytes 393224 | tf_op jit(solution)/shard_map/ppermute | solution.py:23
  10.0 12.5 %collective-permute-start.2 = (f32[3,80,512]{2,1,0:T(8,128)S(1)}, f32[3,80,512]{2,1,0:T(8,128)}, u32[]{:S(2)}, u32[]{:S(2)}) collective-permute-start(f32[3,80,512]{2,1,0:T(8,128)S(1)} %get-tuple-element.20), channel_id=1, source_target_pairs={{0,4},{4,0},{8,12},{12,8},{16,20},{20,16},{24,28},{28,24},{32,36},... | collective-permute-start | bytes 1474568 | tf_op jit(solution)/shard_map/ppermute | solution.py:23
  12.1 10.3 %collective-permute-start.3 = (f32[3,80,512]{2,1,0:T(8,128)S(1)}, f32[3,80,512]{2,1,0:T(8,128)}, u32[]{:S(2)}, u32[]{:S(2)}) collective-permute-start(f32[3,80,512]{2,1,0:T(8,128)S(1)} %get-tuple-element.21), channel_id=1, source_target_pairs={{0,124},{4,8},{8,4},{12,16},{16,12},{20,24},{24,20},{28,32},{32,28... | collective-permute-start | bytes 1474568 | tf_op jit(solution)/shard_map/ppermute | solution.py:23
  13.4 18.5 %all-to-all-start = ((s32[128,1,128]{2,1,0:T(1,128)}), s32[128,1,128]{2,1,0:T(1,128)S(1)}, u32[]{:S(2)}, u32[]{:S(2)}) async-start(s32[128,1,128]{2,1,0:T(1,128)} %bitcast.2), calls=%async_computation | async-start | bytes 131072 | tf_op jit(solution)/shard_map/all_to_all | solution.py:592
